TPU v7x, 32 devices: a whole 2x2x4 slice. The times are simulated.
32 devices in a mesh: dp: 4 (over y, core), seq: 8 (over z, x).
Axes of the slice: x: 2, y: 2, z: 4, core: 2. Of those that a mesh axis runs over, the one named last changes fastest.
Arguments:
- tokens: bfloat16 [2048, 16, 768], P('seq', 'dp'), may hold values from -6 to 6
- cotangent: bfloat16 [2048, 16, 768], P('seq', 'dp'), may hold values from -6 to 6
- picked_ids: int32 [16, 256], P('dp'), may hold values from 0 to 2047, as said below
- lengths: int32 [16], P('dp'), may hold values from 1024 to 2048, as said below
- qkv_w: float32 [2, 3, 768, 768], P(None, None, ('dp', 'seq')), may hold values from -0.21875 to 0.21875
- out_w: float32 [2, 768, 768], P(None, ('dp', 'seq')), may hold values from -3.5 to 3.5
- up_w: float32 [2, 768, 3072], P(None, ('dp', 'seq')), may hold values from -0.21875 to 0.21875
- down_w: float32 [2, 3072, 768], P(None, ('dp', 'seq')), may hold values from -0.109375 to 0.109375
- vectors: float32 [5, 768], P(None, ('dp', 'seq')), may hold values from -1 to 3, as said below
- qkv_mom: float32 [2, 3, 768, 768], P(None, None, ('dp', 'seq')), may hold values from -0.00390625 to 0.00390625
- out_mom: float32 [2, 768, 768], P(None, ('dp', 'seq')), may hold values from -0.00390625 to 0.00390625
- up_mom: float32 [2, 768, 3072], P(None, ('dp', 'seq')), may hold values from -0.00390625 to 0.00390625
- down_mom: float32 [2, 3072, 768], P(None, ('dp', 'seq')), may hold values from -0.00390625 to 0.00390625
- vec_mom: float32 [5, 768], P(None, ('dp', 'seq')), may hold values from -0.00390625 to 0.00390625
- qkv_avg: float32 [2, 3, 768, 768], P(None, None, ('dp', 'seq')), may hold values from -0.21875 to 0.21875
- out_avg: float32 [2, 768, 768], P(None, ('dp', 'seq')), may hold values from -3.5 to 3.5
- up_avg: float32 [2, 768, 3072], P(None, ('dp', 'seq')), may hold values from -0.21875 to 0.21875
- down_avg: float32 [2, 3072, 768], P(None, ('dp', 'seq')), may hold values from -0.109375 to 0.109375
- vec_avg: float32 [5, 768], P(None, ('dp', 'seq')), may hold values from 0.5 to 1.5
Outputs:
- activations: bfloat16 [2048, 16, 768], P('seq', 'dp')
- input_grad: float32 [2048, 16, 768], P('seq', 'dp')
- grad_norm: float32 [], replicated
- qkv_new: float32 [2, 3, 768, 768], P(None, None, ('dp', 'seq'))
- out_new: float32 [2, 768, 768], P(None, ('dp', 'seq'))
- up_new: float32 [2, 768, 3072], P(None, ('dp', 'seq'))
- down_new: float32 [2, 3072, 768], P(None, ('dp', 'seq'))
- vec_new: float32 [5, 768], P(None, ('dp', 'seq'))
- qkv_mom_new: float32 [2, 3, 768, 768], P(None, None, ('dp', 'seq'))
- out_mom_new: float32 [2, 768, 768], P(None, ('dp', 'seq'))
- up_mom_new: float32 [2, 768, 3072], P(None, ('dp', 'seq'))
- down_mom_new: float32 [2, 3072, 768], P(None, ('dp', 'seq'))
- vec_mom_new: float32 [5, 768], P(None, ('dp', 'seq'))
- qkv_avg_new: float32 [2, 3, 768, 768], P(None, None, ('dp', 'seq'))
- out_avg_new: float32 [2, 768, 768], P(None, ('dp', 'seq'))
- up_avg_new: float32 [2, 768, 3072], P(None, ('dp', 'seq'))
- down_avg_new: float32 [2, 3072, 768], P(None, ('dp', 'seq'))
- vec_avg_new: float32 [5, 768], P(None, ('dp', 'seq'))
Inputs may be any that keep to these rules, and one draw needn't show every extreme that they name: `lengths`: every length is 2048 or 1024, and both values occur. `picked_ids`: each sequence's 256 picks are distinct positions below its length, in rising order. `vectors`: rows 0, 1, 3, 4 are norm gains, row 2 the router's weight.
All inputs are finite; a program needn't handle non-finite values.
Results may differ from a plain program's by a relative error of at most 0.023.
Values may be sent and summed in bfloat16 or wider, within the bound.
No kernel may reach another device: no remote copies, remote signals or barrier semaphores. Data moves between devices by JAX's collectives and lax.ppermute only.
A program may use at most 256 MiB of HBM per device.

v0:
```python
import math

import jax
import jax.numpy as jnp
from jax import lax
from jax.sharding import PartitionSpec as P

D = 768
LEN = 2048
NPARAMS = 14159616


norm_eps = 1e-06


def from_partner(value, axis, bit):
    mask = 2**bit
    pairs = [(source, source ^ mask) for source in range(lax.axis_size(axis))]
    return lax.ppermute(value, axis, pairs)


def normed(value, gain):
    return value * lax.rsqrt(jnp.mean(value * value, axis=-1, keepdims=True) + norm_eps) * gain


def project(left, weight):
    return jnp.einsum("rsd,de->rse", left, weight, preferred_element_type=jnp.float32)


def project_back(grad_in, weight):
    return jnp.einsum("rse,de->rsd", grad_in, weight, preferred_element_type=jnp.float32)


def weight_grad(left, grad_in):
    return jnp.einsum("rsd,rse->de", left, grad_in, preferred_element_type=jnp.float32)


def score_block(query, all_keys, q_pos, k_pos, k_limit, step_id, head_pairs, span_rows):
    seq_count = query.shape[1]
    row_start = step_id // head_pairs * span_rows
    col_start = step_id % head_pairs * 128
    q_block = lax.dynamic_slice(
        query, (row_start, 0, col_start), (span_rows, seq_count, 128)
    ).reshape(span_rows, seq_count, 2, 64)
    k_block = lax.dynamic_slice_in_dim(all_keys, col_start, 128, 2).reshape(
        all_keys.shape[0], seq_count, 2, 64
    )
    q_places = lax.dynamic_slice_in_dim(q_pos, row_start, span_rows, 0).T
    k_places = k_pos.T
    allowed = (k_places[:, None, :] <= q_places[:, :, None]) & (k_places < k_limit[:, None])[
        :, None, :
    ]
    scores = (
        jnp.einsum("qsha,ksha->shqk", q_block, k_block, preferred_element_type=jnp.float32) * 0.125
    )
    scores = jnp.where(allowed[:, None], scores, -1e30)
    return (q_block, k_block, allowed, scores, row_start, col_start)


def attend(query, all_keys, all_values, q_pos, k_pos, k_limit):
    row_count, seq_count, feat_width = query.shape
    key_count = all_keys.shape[0]
    span_rows = min(512, row_count)
    head_pairs = feat_width // 128
    steps_all = row_count // span_rows * head_pairs

    def one_step(step_id, state_in):
        out_acc, lse_acc = state_in
        q_block, k_block, allowed, scores, row_start, col_start = score_block(
            query, all_keys, q_pos, k_pos, k_limit, step_id, head_pairs, span_rows
        )
        v_block = lax.dynamic_slice_in_dim(all_values, col_start, 128, 2).reshape(
            key_count, seq_count, 2, 64
        )
        top_score = jnp.max(scores, axis=-1, keepdims=True)
        exp_scores = jnp.exp(scores - top_score)
        weight_sum = jnp.sum(exp_scores, axis=-1, keepdims=True)
        probs_low = (exp_scores / weight_sum).astype(jnp.bfloat16)
        mixed_out = jnp.einsum(
            "shqk,ksha->qsha", probs_low, v_block, preferred_element_type=jnp.float32
        )
        out_acc = lax.dynamic_update_slice(
            out_acc,
            mixed_out.reshape(span_rows, seq_count, 128).astype(jnp.bfloat16),
            (row_start, 0, col_start),
        )
        lse_acc = lax.dynamic_update_slice(
            lse_acc,
            (top_score + jnp.log(weight_sum))[..., 0],
            (0, 2 * (step_id % head_pairs), row_start),
        )
        return (out_acc, lse_acc)

    start_state = (
        jnp.zeros((row_count, seq_count, feat_width), jnp.bfloat16),
        jnp.zeros((seq_count, feat_width // 64, row_count), jnp.float32),
    )
    return lax.fori_loop(0, steps_all, one_step, start_state)


def attend_back(query, all_keys, all_values, q_pos, k_pos, k_limit, lse_rows, out_grad):
    row_count, seq_count, feat_width = query.shape
    key_count = all_keys.shape[0]
    span_rows = min(512, row_count)
    head_pairs = feat_width // 128
    steps_all = row_count // span_rows * head_pairs

    def one_step(step_id, state_in):
        dq_acc, dk_acc, dv_acc = state_in
        q_block, k_block, allowed, scores, row_start, col_start = score_block(
            query, all_keys, q_pos, k_pos, k_limit, step_id, head_pairs, span_rows
        )
        v_block = lax.dynamic_slice_in_dim(all_values, col_start, 128, 2).reshape(
            key_count, seq_count, 2, 64
        )
        g_block = lax.dynamic_slice(
            out_grad, (row_start, 0, col_start), (span_rows, seq_count, 128)
        ).reshape(span_rows, seq_count, 2, 64)
        lse_block = lax.dynamic_slice(
            lse_rows, (0, 2 * (step_id % head_pairs), row_start), (seq_count, 2, span_rows)
        )
        probs_all = jnp.where(allowed[:, None], jnp.exp(scores - lse_block[..., None]), 0.0)
        d_probs = jnp.einsum(
            "qsha,ksha->shqk", g_block, v_block, preferred_element_type=jnp.float32
        )
        inner_sum = jnp.sum(probs_all * d_probs, axis=-1, keepdims=True)
        d_scores = (probs_all * (d_probs - inner_sum)).astype(jnp.bfloat16)
        dq_block = (
            jnp.einsum("shqk,ksha->qsha", d_scores, k_block, preferred_element_type=jnp.float32)
            * 0.125
        )
        dk_block = (
            jnp.einsum("shqk,qsha->ksha", d_scores, q_block, preferred_element_type=jnp.float32)
            * 0.125
        )
        dv_block = jnp.einsum(
            "shqk,qsha->ksha",
            probs_all.astype(jnp.bfloat16),
            g_block,
            preferred_element_type=jnp.float32,
        )
        dq_acc = lax.dynamic_update_slice(
            dq_acc, dq_block.reshape(span_rows, seq_count, 128), (row_start, 0, col_start)
        )
        dk_old = lax.dynamic_slice_in_dim(dk_acc, col_start, 128, 2)
        dk_acc = lax.dynamic_update_slice_in_dim(
            dk_acc, dk_old + dk_block.reshape(key_count, seq_count, 128), col_start, 2
        )
        dv_old = lax.dynamic_slice_in_dim(dv_acc, col_start, 128, 2)
        dv_acc = lax.dynamic_update_slice_in_dim(
            dv_acc, dv_old + dv_block.reshape(key_count, seq_count, 128), col_start, 2
        )
        return (dq_acc, dk_acc, dv_acc)

    start_state = (
        jnp.zeros((row_count, seq_count, feat_width), jnp.float32),
        jnp.zeros((key_count, seq_count, feat_width), jnp.float32),
        jnp.zeros((key_count, seq_count, feat_width), jnp.float32),
    )
    return lax.fori_loop(0, steps_all, one_step, start_state)


def block_forward(rows_in, weights, gain_first, gain_second, q_pos, far_pos, k_limit, share_keys):
    w_query, w_key, w_value, w_proj, w_up, w_down = weights
    first_n = normed(rows_in, gain_first).astype(jnp.bfloat16)
    query = project(first_n, w_query).astype(jnp.bfloat16)
    key_own = project(first_n, w_key).astype(jnp.bfloat16)
    value_own = project(first_n, w_value).astype(jnp.bfloat16)
    far_pair = share_keys(jnp.stack([key_own, value_own]))
    all_keys = jnp.concatenate([key_own, far_pair[0]], axis=0)
    all_values = jnp.concatenate([value_own, far_pair[1]], axis=0)
    k_pos = jnp.concatenate([q_pos, far_pos], axis=0)
    attended, lse_rows = attend(query, all_keys, all_values, q_pos, k_pos, k_limit)
    branch = project(attended, w_proj)
    middle = rows_in + branch
    second_n = normed(middle, gain_second).astype(jnp.bfloat16)
    pre_act = project(second_n, w_up)
    act_low = jax.nn.gelu(pre_act).astype(jnp.bfloat16)
    mlp_out = project(act_low, w_down)
    saved = (
        first_n,
        query,
        all_keys,
        all_values,
        k_pos,
        attended,
        lse_rows,
        middle,
        second_n,
        pre_act,
        act_low,
    )
    return (branch, middle, mlp_out, saved)


def block_backward(
    rows_in,
    weights,
    gain_first,
    gain_second,
    q_pos,
    k_limit,
    saved,
    d_mlp,
    d_top,
    d_extra,
    share_back,
):
    (
        first_n,
        query,
        all_keys,
        all_values,
        k_pos,
        attended,
        lse_rows,
        middle,
        second_n,
        pre_act,
        act_low,
    ) = saved
    w_query, w_key, w_value, w_proj, w_up, w_down = weights
    mlp_low = d_mlp.astype(jnp.bfloat16)
    g_down = weight_grad(act_low, mlp_low)
    d_act = project_back(mlp_low, w_down)
    gelu_back = jax.vjp(jax.nn.gelu, pre_act)[1]
    pre_low = gelu_back(d_act)[0].astype(jnp.bfloat16)
    g_up = weight_grad(second_n, pre_low)
    second_back = jax.vjp(normed, middle, gain_second)[1]
    d_middle, g_gain_second = second_back(project_back(pre_low, w_up))
    if d_top is not None:
        d_middle = d_middle + d_top
    d_branch = d_middle if d_extra is None else d_middle + d_extra
    branch_low = d_branch.astype(jnp.bfloat16)
    g_proj = weight_grad(attended, branch_low)
    out_low = project_back(branch_low, w_proj).astype(jnp.bfloat16)
    d_query, d_keys, d_values = attend_back(
        query, all_keys, all_values, q_pos, k_pos, k_limit, lse_rows, out_low
    )
    own_count = query.shape[0]
    returned = share_back(jnp.stack([d_keys[own_count:], d_values[own_count:]]))
    key_low = (d_keys[:own_count] + returned[0]).astype(jnp.bfloat16)
    value_low = (d_values[:own_count] + returned[1]).astype(jnp.bfloat16)
    query_low = d_query.astype(jnp.bfloat16)
    d_first = (
        project_back(query_low, w_query)
        + project_back(key_low, w_key)
        + project_back(value_low, w_value)
    )
    first_back = jax.vjp(normed, rows_in, gain_first)[1]
    d_rows, g_gain_first = first_back(d_first)
    grads_out = (
        weight_grad(first_n, query_low),
        weight_grad(first_n, key_low),
        weight_grad(first_n, value_low),
        g_proj,
        g_up,
        g_down,
    )
    return (d_rows + d_middle, grads_out, g_gain_first, g_gain_second)


def starts_of(which_half, quarter):
    return (which_half * quarter, 3 * quarter - which_half * quarter)


def rows_of(full_rows, first_start, second_start, quarter):
    return jnp.concatenate(
        [
            lax.dynamic_slice_in_dim(full_rows, first_start, quarter, 0),
            lax.dynamic_slice_in_dim(full_rows, second_start, quarter, 0),
        ],
        axis=0,
    )


def positions_of(first_start, second_start, quarter):
    steps_local = jnp.arange(quarter, dtype=jnp.int32)
    places = jnp.concatenate([first_start + steps_local, second_start + steps_local])
    return places[:, None]


def place_rows(rows_in, first_start, second_start, full_len):
    quarter = rows_in.shape[0] // 2
    canvas = jnp.zeros((full_len,) + rows_in.shape[1:], jnp.float32)
    canvas = lax.dynamic_update_slice_in_dim(canvas, rows_in[:quarter], first_start, 0)
    return lax.dynamic_update_slice_in_dim(canvas, rows_in[quarter:], second_start, 0)


def body(
    tokens,
    cotangent,
    picked_ids,
    lengths,
    qkv_w,
    out_w,
    up_w,
    down_w,
    vectors,
    qkv_mom,
    out_mom,
    up_mom,
    down_mom,
    vec_mom,
    qkv_avg,
    out_avg,
    up_avg,
    down_avg,
    vec_avg,
):
    w_qkv, w_out, w_up, w_down, w_vec = (
        lax.all_gather(qkv_w.astype(jnp.bfloat16), ("dp", "seq"), axis=2, tiled=True),
        lax.all_gather(out_w.astype(jnp.bfloat16), ("dp", "seq"), axis=1, tiled=True),
        lax.all_gather(up_w.astype(jnp.bfloat16), ("dp", "seq"), axis=1, tiled=True),
        lax.all_gather(down_w.astype(jnp.bfloat16), ("dp", "seq"), axis=1, tiled=True),
        lax.all_gather(vectors.astype(jnp.bfloat16), ("dp", "seq"), axis=1, tiled=True),
    )
    gains_all = w_vec.astype(jnp.float32)
    shard_pos, group_seqs, feat_width = tokens.shape
    seq_devices = lax.axis_size("seq")
    pair_count = seq_devices // 2
    per_pair = group_seqs // pair_count
    full_len = shard_pos * seq_devices
    quarter = full_len // 4
    my_index = lax.axis_index("seq")
    my_half = my_index % 2
    pair_id = my_index // 2

    def spread(source):
        widened = jnp.broadcast_to(
            source.reshape(shard_pos, pair_count, 1, per_pair, feat_width),
            (shard_pos, pair_count, 2, per_pair, feat_width),
        )
        return widened.reshape(shard_pos, seq_devices, per_pair, feat_width)

    full_x, full_cot = (
        lax.all_to_all(spread(tokens), "seq", split_axis=1, concat_axis=0, tiled=True),
        lax.all_to_all(spread(cotangent), "seq", split_axis=1, concat_axis=0, tiled=True),
    )
    full_x = full_x.reshape(full_len, per_pair, feat_width)
    full_cot = full_cot.reshape(full_len, per_pair, feat_width)
    my_picks = lax.dynamic_slice_in_dim(picked_ids, pair_id * per_pair, per_pair, 0).T
    my_lengths = lax.dynamic_slice_in_dim(lengths, pair_id * per_pair, per_pair, 0)
    cap_quarter = my_picks.shape[0] // 4
    pick_first, pick_second = starts_of(my_half, cap_quarter)
    far_pick_first, far_pick_second = starts_of(1 - my_half, cap_quarter)
    own_slots = rows_of(my_picks, pick_first, pick_second, cap_quarter)
    far_slots = rows_of(my_picks, far_pick_first, far_pick_second, cap_quarter)
    seq_cols = jnp.arange(per_pair)[None, :]

    def layer_weights(layer_id):
        return (
            w_qkv[layer_id, 0],
            w_qkv[layer_id, 1],
            w_qkv[layer_id, 2],
            w_out[layer_id],
            w_up[layer_id],
            w_down[layer_id],
        )

    def share_picks(stacked):
        return from_partner(stacked, "seq", 0)

    def share_dense(stacked):
        return from_partner(stacked, "seq", 0)

    def return_dense(stacked):
        return from_partner(stacked.astype(jnp.bfloat16), "seq", 0).astype(stacked.dtype)

    def return_picks(stacked):
        return from_partner(stacked.astype(jnp.bfloat16), "seq", 0).astype(stacked.dtype)

    chosen = full_x[own_slots, seq_cols]
    x_rows = chosen.astype(jnp.float32)
    routed_w = layer_weights(0)
    logits = jnp.einsum("rsd,d->rs", chosen, w_vec[2], preferred_element_type=jnp.float32)
    gate = jax.nn.sigmoid(logits)
    branch_r, middle_r, mlp_r, saved_r = block_forward(
        x_rows, routed_w, gains_all[0], gains_all[1], own_slots, far_slots, my_lengths, share_picks
    )
    combined_r = branch_r + mlp_r
    delta_own = (gate[..., None] * combined_r).astype(jnp.bfloat16)
    delta_far = from_partner(delta_own, "seq", 0)
    mixed_full = (
        full_x.astype(jnp.float32)
        .at[own_slots, seq_cols]
        .add(delta_own.astype(jnp.float32))
        .at[far_slots, seq_cols]
        .add(delta_far.astype(jnp.float32))
    )
    own_first, own_second = starts_of(my_half, quarter)
    far_first, far_second = starts_of(1 - my_half, quarter)
    own_pos = positions_of(own_first, own_second, quarter)
    far_pos = positions_of(far_first, far_second, quarter)
    dense_w = layer_weights(1)
    dense_in = rows_of(mixed_full, own_first, own_second, quarter)
    branch_d, middle_d, mlp_d, saved_d = block_forward(
        dense_in, dense_w, gains_all[3], gains_all[4], own_pos, far_pos, my_lengths, share_dense
    )
    live = (own_pos < my_lengths[None, :]).astype(jnp.float32)[..., None]
    out_rows = (live * (middle_d + mlp_d)).astype(jnp.bfloat16)
    d_top = live * rows_of(full_cot, own_first, own_second, quarter).astype(jnp.float32)
    d_dense_in, grads_dense, g_gain_three, g_gain_four = block_backward(
        dense_in,
        dense_w,
        gains_all[3],
        gains_all[4],
        own_pos,
        my_lengths,
        saved_d,
        d_top,
        d_top,
        None,
        return_dense,
    )
    dx_full = place_rows(d_dense_in, own_first, own_second, full_len)
    d_far = from_partner(dx_full[far_slots, seq_cols].astype(jnp.bfloat16), "seq", 0).astype(
        jnp.float32
    )
    d_delta = dx_full[own_slots, seq_cols] + d_far
    gated = gate[..., None] * d_delta
    d_gate = jnp.sum(d_delta * combined_r, axis=-1)
    d_logit = d_gate * gate * (1.0 - gate)
    d_rows_r, grads_routed, g_gain_zero, g_gain_one = block_backward(
        x_rows,
        routed_w,
        gains_all[0],
        gains_all[1],
        own_slots,
        my_lengths,
        saved_r,
        gated,
        None,
        gated,
        return_picks,
    )
    d_chosen = d_rows_r + d_logit[..., None] * gains_all[2]
    g_router = jnp.einsum("rs,rsd->d", d_logit, x_rows)
    dx_full = dx_full.at[own_slots, seq_cols].add(d_chosen)
    y_full = place_rows(out_rows.astype(jnp.float32), own_first, own_second, full_len)
    y_back, dx_back = (
        lax.all_to_all(
            y_full.astype(jnp.bfloat16), "seq", split_axis=0, concat_axis=1, tiled=True
        ).astype(y_full.dtype),
        lax.all_to_all(
            dx_full.astype(jnp.bfloat16), "seq", split_axis=0, concat_axis=1, tiled=True
        ).astype(dx_full.dtype),
    )
    activations = (
        y_back.reshape(shard_pos, pair_count, 2, per_pair, feat_width)
        .sum(axis=2)
        .reshape(shard_pos, group_seqs, feat_width)
        .astype(jnp.bfloat16)
    )
    input_grad = (
        dx_back.reshape(shard_pos, pair_count, 2, per_pair, feat_width)
        .sum(axis=2)
        .reshape(shard_pos, group_seqs, feat_width)
    )
    g_qkv = jnp.stack([jnp.stack(grads_routed[0:3]), jnp.stack(grads_dense[0:3])])
    g_out = jnp.stack([grads_routed[3], grads_dense[3]])
    g_up = jnp.stack([grads_routed[4], grads_dense[4]])
    g_down = jnp.stack([grads_routed[5], grads_dense[5]])
    g_vec = jnp.stack([g_gain_zero, g_gain_one, g_router, g_gain_three, g_gain_four])
    partial_sums = (
        lax.psum_scatter(g_qkv.astype(jnp.bfloat16), "dp", scatter_dimension=2, tiled=True).astype(
            jnp.float32
        ),
        lax.psum_scatter(g_out.astype(jnp.bfloat16), "dp", scatter_dimension=1, tiled=True).astype(
            jnp.float32
        ),
        lax.psum_scatter(g_up.astype(jnp.bfloat16), "dp", scatter_dimension=1, tiled=True).astype(
            jnp.float32
        ),
        lax.psum_scatter(g_down.astype(jnp.bfloat16), "dp", scatter_dimension=1, tiled=True).astype(
            jnp.float32
        ),
        lax.psum_scatter(g_vec.astype(jnp.bfloat16), "dp", scatter_dimension=1, tiled=True).astype(
            jnp.float32
        ),
    )
    shards = (
        lax.psum_scatter(
            partial_sums[0].astype(jnp.bfloat16), "seq", scatter_dimension=2, tiled=True
        ).astype(jnp.float32),
        lax.psum_scatter(
            partial_sums[1].astype(jnp.bfloat16), "seq", scatter_dimension=1, tiled=True
        ).astype(jnp.float32),
        lax.psum_scatter(
            partial_sums[2].astype(jnp.bfloat16), "seq", scatter_dimension=1, tiled=True
        ).astype(jnp.float32),
        lax.psum_scatter(
            partial_sums[3].astype(jnp.bfloat16), "seq", scatter_dimension=1, tiled=True
        ).astype(jnp.float32),
        lax.psum_scatter(
            partial_sums[4].astype(jnp.bfloat16), "seq", scatter_dimension=1, tiled=True
        ).astype(jnp.float32),
    )
    squares = sum((jnp.sum(piece * piece) for piece in shards))
    grad_norm = jnp.sqrt(lax.psum(squares, ("dp", "seq")))
    factor = 1.0 / jnp.maximum(grad_norm, 1.0)
    base_rate = math.sqrt(NPARAMS / D)
    rates = (base_rate, math.sqrt(NPARAMS * LEN / (8 * D)), base_rate, base_rate, base_rate)
    masters = (qkv_w, out_w, up_w, down_w, vectors)
    moms = (qkv_mom, out_mom, up_mom, down_mom, vec_mom)
    avgs = (qkv_avg, out_avg, up_avg, down_avg, vec_avg)
    new_weights = []
    new_moms = []
    new_avgs = []
    for weight, gradient, momentum, average, rate in zip(masters, shards, moms, avgs, rates):
        clipped = gradient * factor
        momentum_new = 0.5 * momentum + clipped
        weight_new = weight - rate * (clipped + 0.5 * momentum_new)
        new_weights.append(weight_new)
        new_moms.append(momentum_new)
        new_avgs.append(0.5 * average + 0.5 * weight_new)
    return (
        activations,
        input_grad,
        grad_norm,
        new_weights[0],
        new_weights[1],
        new_weights[2],
        new_weights[3],
        new_weights[4],
        new_moms[0],
        new_moms[1],
        new_moms[2],
        new_moms[3],
        new_moms[4],
        new_avgs[0],
        new_avgs[1],
        new_avgs[2],
        new_avgs[3],
        new_avgs[4],
    )


def solution(mesh):
    placed = (
        P("seq", "dp", None),
        P("seq", "dp", None),
        P("dp", None),
        P("dp"),
        P(None, None, ("dp", "seq"), None),
        P(None, ("dp", "seq"), None),
        P(None, ("dp", "seq"), None),
        P(None, ("dp", "seq"), None),
        P(None, ("dp", "seq")),
        P(None, None, ("dp", "seq"), None),
        P(None, ("dp", "seq"), None),
        P(None, ("dp", "seq"), None),
        P(None, ("dp", "seq"), None),
        P(None, ("dp", "seq")),
        P(None, None, ("dp", "seq"), None),
        P(None, ("dp", "seq"), None),
        P(None, ("dp", "seq"), None),
        P(None, ("dp", "seq"), None),
        P(None, ("dp", "seq")),
    )
    return jax.shard_map(
        body,
        mesh=mesh,
        in_specs=placed,
        out_specs=(
            P("seq", "dp", None),
            P("seq", "dp", None),
            P(),
            P(None, None, ("dp", "seq"), None),
            P(None, ("dp", "seq"), None),
            P(None, ("dp", "seq"), None),
            P(None, ("dp", "seq"), None),
            P(None, ("dp", "seq")),
            P(None, None, ("dp", "seq"), None),
            P(None, ("dp", "seq"), None),
            P(None, ("dp", "seq"), None),
            P(None, ("dp", "seq"), None),
            P(None, ("dp", "seq")),
            P(None, None, ("dp", "seq"), None),
            P(None, ("dp", "seq"), None),
            P(None, ("dp", "seq"), None),
            P(None, ("dp", "seq"), None),
            P(None, ("dp", "seq")),
        ),
        check_vma=False,
    )
```

profile of v0, /device:TPU:0, one launch (start us, length us, event | category | flops | bytes accessed | tf_op | source)
XLA Modules:
  0.0 1840.4 jit_solution(11473546357094572272)
XLA Ops:
  16.6 7.4 all-to-all-start
  24.6 150.8 %all-gather = bf16[32,24,5]{1,2,0:T(8,128)(2,1)S(1)} all-gather(bf16[1,24,5]{1,2,0:T(8,128)(2,1)S(1)} %convert_bitcast_fusion.4), channel_id=1, replica_groups=mesh['dp'=4,'seq'=8] {'dp','seq'}, dimensions={0}, use_global_device_ids=true | all-gather | bytes 7920 | tf_op jit(solution)/shard_map/all_gather | solution.py:316
  203.4 21.7 %collective-permute-done = bf16[2,128,1,768]{3,1,2,0:T(8,128)(2,1)} collective-permute-done((bf16[2,128,1,768]{3,1,2,0:T(8,128)(2,1)}, bf16[2,128,1,768]{3,1,2,0:T(8,128)(2,1)}, u32[]{:S(2)}, u32[]{:S(2)}) %collective-permute-start) | collective-permute-done | bytes 393248 | tf_op jit(solution)/shard_map/ppermute | solution.py:19
  234.7 22.4 %while.72 = (s32[]{:T(128)}, bf16[128,1,768]{0,2,1:T(8,128)(2,1)S(1)}, f32[1,12,128]{2,1,0:T(8,128)}, bf16[256,1,768]{0,2,1:T(8,128)(2,1)}, s32[256,1]{0,1:T(1,1...) while((s32[]{:T(128)}, ...), condition=%wide.region_4.5_spmd, body=%wide.region_1.4_spmd.sunk | while | flops 17383436 | bytes 1453375 | solution.py:98
  260.2 43.8 %all-gather.10.cloned.1.call-done = bf16[2,768,3072]{2,1,0:T(8,128)(2,1)} async-done(((bf16[2,24,3072]{2,1,0:T(8,128)(2,1)}), bf16[2,768,3072]{2,1,0:T(8,128)(2,1)}) %all-gather.10.cloned.1.call-update) | async-done | bytes 9437200 | tf_op jit(solution)/shard_map/all_gather | solution.py:314
  308.4 79.2 %all-gather.12.cloned.1.call-done = bf16[2,3072,768]{2,1,0:T(8,128)(2,1)} async-done(((bf16[2,96,768]{2,1,0:T(8,128)(2,1)}), bf16[2,3072,768]{2,1,0:T(8,128)(2,1)}) %all-gather.12.cloned.1.call-update) | async-done | bytes 9437200 | tf_op jit(solution)/shard_map/all_gather | solution.py:315
  397.1 7.0 scatter_custom_fusion
  404.1 7.3 scatter_custom_fusion.1
  447.9 50.2 %collective-permute-done.2 = bf16[2,1024,1,768]{3,1,2,0:T(8,128)(2,1)} collective-permute-done((bf16[2,1024,1,768]{3,1,2,0:T(8,128)(2,1)}, bf16[2,1024,1,768]{3,1,2,0:T(8,128)(2,1)}, u32[]{:S(2)}, u32[]{:S(2)}) %collective-permute-start.2) | collective-permute-done | bytes 3145760 | tf_op jit(solution)/shard_map/ppermute | solution.py:19
  517.8 136.5 %while.73 = (s32[]{:T(128)}, bf16[1024,1,768]{0,2,1:T(8,128)(2,1)}, f32[1,12,1024]{2,1,0:T(8,128)S(1)}, bf16[2048,1,768]{0,2,1:T(8,128)(2,1)}, s32[2048,1]{0,1:T...) while((s32[]{:T(128)}, bf16[1024,1,768]{0,2,1:T(8,128)(2,1)}, ...), condition=%wide.region_12.13_spmd, body=%wide.region_9.12_spmd.sunk | while | flops 564200448 | bytes 33352148 | solution.py:98
  657.7 12.4 fusion.33
  670.2 16.8 fusion.23
  687.1 8.5 multiply_reduce_fusion.2
  707.1 347.5 %while.74 = (s32[]{:T(128)}, bf16[1024,1,768]{0,2,1:T(8,128)(2,1)}, f32[2048,1,768]{0,2,1:T(8,128)}, f32[2048,1,768]{0,2,1:T(8,128)}, bf16[2048,1,768]{0,2,1:T(8...) while((s32[]{:T(128)}, bf16[1024,1,768]{0,2,1:T(8,128)(2,1)}, ...), condition=%wide.region_18.19_spmd, body=%wide.region_16.18_spmd.sunk | while | flops 1366164480 | bytes 124959312 | solution.py:160
  719.0 6.6 multiply_convert_fusion.21
  747.9 6.6 multiply_convert_fusion.21
  776.9 6.6 multiply_convert_fusion.21
  805.8 6.6 multiply_convert_fusion.21
  834.8 6.6 multiply_convert_fusion.21
  863.7 6.6 multiply_convert_fusion.21
  892.6 6.6 multiply_convert_fusion.21
  921.6 6.6 multiply_convert_fusion.21
  950.5 6.6 multiply_convert_fusion.21
  979.4 6.6 multiply_convert_fusion.21
  1002.5 5.9 multiply_reduce_fusion.12
  1008.4 6.6 multiply_convert_fusion.21
  1037.3 6.6 multiply_convert_fusion.21
  1070.9 59.4 %collective-permute-done.3 = bf16[2,1024,1,768]{1,3,2,0:T(8,128)(2,1)} collective-permute-done((bf16[2,1024,1,768]{1,3,2,0:T(8,128)(2,1)}, bf16[2,1024,1,768]{1,3,2,0:T(8,128)(2,1)}, u32[]{:S(2)}, u32[]{:S(2)}) %collective-permute-start.3) | collective-permute-done | bytes 3145760 | tf_op jit(solution)/shard_map/ppermute | solution.py:19
  1185.7 36.4 %while.75 = (s32[]{:T(128)}, bf16[128,1,768]{0,2,1:T(8,128)(2,1)S(1)}, f32[256,1,768]{0,2,1:T(8,128)S(1)}, f32[256,1,768]{0,2,1:T(8,128)S(1)}, bf16[256,1,768]{0...) while((s32[]{:T(128)}, ...), condition=%wide.region_23.24_spmd, body=%wide.region_21.23_spmd.sunk | while | flops 42795024 | bytes 3973475 | solution.py:160
  1236.3 9.7 fusion.26
  1249.7 8.9 pad_maximum_fusion
  1260.0 13.2 fusion.27
  1277.0 8.4 pad_maximum_fusion.1
  1297.2 11.3 fusion.46
  1335.0 6.8 convert_element_type.614
  1342.4 33.4 %reduce.83 = bf16[2048,768]{1,0:T(8,128)(2,1)} reduce(bf16[2048,1,768]{2,1,0:T(2,128)(2,1)} %convert_element_type.614, bf16[]{:T(256)} %broadcast.1133), dimensions={1}, to_apply=%convert_element_type.614.reduce_sub_computation | reduce | bytes 6291458 | tf_op jit(solution)/shard_map/convert_element_type | solution.py:443
  1375.8 6.4 reshape.2469
  1393.2 7.3 copy.228
  1400.6 7.4 scatter_custom_fusion.2
  1421.4 33.0 %all-to-all-done.1 = bf16[8,2,98304]{2,1,0:T(2,128)(2,1)} async-done(((bf16[8,2,98304]{2,1,0:T(2,128)(2,1)}), bf16[8,2,98304]{2,1,0:T(2,128)(2,1)}, u32[]{:S(2)}, u32[]{:S(2)}) %all-to-all-start.1) | async-done | bytes 3145760 | tf_op jit(solution)/shard_map/all_to_all | solution.py:442
  1461.5 21.5 %reduce-scatter.35.cloned.1.call-done = bf16[192,5]{1,0:T(8,128)(2,1)} async-done(((bf16[768,5]{1,0:T(8,128)(2,1)}), bf16[192,5]{1,0:T(8,128)(2,1)}) %reduce-scatter.35.cloned.1.call-update) | async-done | bytes 1936
  1483.8 42.5 %all-reduce.2 = bf16[5,192]{1,0:T(8,128)(2,1)S(1)} all-reduce(bf16[5,192]{1,0:T(8,128)(2,1)S(1)} %copy.180), channel_id=11, replica_groups=mesh['dp'=4,'seq'=8] {'seq'}, use_global_device_ids=true, to_apply=%region_45.46.clone | all-reduce | flops 960 | bytes 3840
  1527.0 8.0 reshape.2470
  1553.1 7.8 convert_bitcast_fusion
  1571.0 63.8 %reduce-scatter.29.cloned.1.call-done = bf16[24,4608]{1,0:T(8,128)(2,1)} async-done(((bf16[192,4608]{1,0:T(8,128)(2,1)}), bf16[24,4608]{1,0:T(8,128)(2,1)}) %reduce-scatter.29.cloned.1.call-update) | async-done | bytes 221200
  1637.9 68.1 %reduce-scatter.33.cloned.1.call-done = bf16[24,6144]{1,0:T(8,128)(2,1)} async-done(((bf16[192,6144]{1,0:T(8,128)(2,1)}), bf16[24,6144]{1,0:T(8,128)(2,1)}) %reduce-scatter.33.cloned.1.call-update) | async-done | bytes 294928
  1710.2 67.3 %reduce-scatter.27.cloned.1.call-done = bf16[2,96,768]{2,1,0:T(8,128)(2,1)} async-done(((bf16[2,768,768]{2,1,0:T(8,128)(2,1)}), bf16[2,96,768]{2,1,0:T(8,128)(2,1)}) %reduce-scatter.27.cloned.1.call-update) | async-done | bytes 294928 | tf_op jit(solution)/shard_map/reduce_scatter | solution.py:492
  1784.2 39.5 %psum.7 = f32[]{:T(128)} all-reduce(f32[]{:T(128)S(6)} %add.753), channel_id=1, replica_groups=mesh['dp'=4,'seq'=8] {'dp','seq'}, use_global_device_ids=true, to_apply=%region_47.48 | all-reduce | flops 1 | bytes 8 | tf_op jit(solution)/shard_map/psum | solution.py:500
  (1002 shorter events, 802.8 us)
Async XLA Ops:
  7.2 184.2 %all-gather.6.cloned.1.call-start = ((), (), s32[]{:S(2)}) async-start(), calls=%async_computation.13 | async-start | bytes 7299072 | tf_op jit(solution)/shard_map/all_gather | solution.py:312
  9.1 248.0 %all-gather.8.cloned.1.call-start = ((), (), s32[]{:S(2)}) async-start(), calls=%async_computation.14 | async-start | bytes 2433024 | tf_op jit(solution)/shard_map/all_gather | solution.py:313
  10.7 293.2 %all-gather.10.cloned.1.call-start = ((), (), s32[]{:S(2)}) async-start(), calls=%async_computation.15 | async-start | bytes 9732096 | tf_op jit(solution)/shard_map/all_gather | solution.py:314
  12.6 375.0 %all-gather.12.cloned.1.call-start = ((), (), s32[]{:S(2)}) async-start(), calls=%async_computation.16 | async-start | bytes 9732096 | tf_op jit(solution)/shard_map/all_gather | solution.py:315
  16.6 165.4 %all-to-all-start = ((bf16[256,8,1,768]{3,0,2,1:T(8,128)(2,1)}), bf16[256,8,1,768]{3,0,2,1:T(8,128)(2,1)S(1)}, u32[]{:S(2)}, u32[]{:S(2)}) async-start(bf16[256,8,1,768]{3,0,2,1:T(8,128)(2,1)} %bitcast.662), calls=%async_computation | async-start | bytes 6291456 | tf_op jit(solution)/shard_map/all_to_all | solution.py:337
  24.0 155.3 %copy-start.104 = (s32[4,256]{1,0:T(4,128)S(1)}, s32[4,256]{1,0:T(4,128)}, u32[]{:S(2)}) copy-start(s32[4,256]{1,0:T(4,128)} %param.29) | copy-start | bytes 12292
  180.8 123.1 %copy-start.62 = (f32[768]{0:T(1024)}, f32[768]{0:T(1024)S(1)}, u32[]{:S(2)}) copy-start(f32[768]{0:T(1024)S(1)} %get-tuple-element.1269) | copy-start | bytes 9220
  185.3 243.7 %all-to-all-start.2 = ((bf16[256,8,1,768]{0,3,2,1:T(8,128)(2,1)}), bf16[256,8,1,768]{0,3,2,1:T(8,128)(2,1)}, u32[]{:S(2)}, u32[]{:S(2)}) async-start(bf16[256,8,1,768]{0,3,2,1:T(8,128)(2,1)} %bitcast.661), calls=%async_computation.2 | async-start | bytes 6291456 | tf_op jit(solution)/shard_map/all_to_all | solution.py:338
  189.8 1104.7 %reduce-scatter.21.cloned.1.call-start = ((), (), s32[]{:S(2)}) async-start(), calls=%async_computation.18 | async-start | bytes 2949120 | tf_op jit(solution)/shard_map/reduce_scatter | solution.py:469
  191.2 65.9 %copy-start.7 = (bf16[128,768]{1,0:T(8,128)(2,1)}, bf16[128,768]{1,0:T(8,128)(2,1)S(1)}, u32[]{:S(2)}) copy-start(bf16[128,768]{1,0:T(8,128)(2,1)S(1)} %gather_fusion) | copy-start | bytes 589828
  196.0 29.1 %collective-permute-start = (bf16[2,128,1,768]{3,1,2,0:T(8,128)(2,1)}, bf16[2,128,1,768]{3,1,2,0:T(8,128)(2,1)}, u32[]{:S(2)}, u32[]{:S(2)}) collective-permute-start(bf16[2,128,1,768]{3,1,2,0:T(8,128)(2,1)} %pad_maximum_fusion.11), channel_id=1, source_target_pairs={{0,1},{1,0},{2,3},{3,2},{4,5},{5,4},{6,7},{7,6},{8,9},{9,8},{10,11... | collective-permute-start | bytes 1179656 | tf_op jit(solution)/shard_map/ppermute | solution.py:19
  199.3 35.4 %copy-start.73 = (s32[128,1]{0,1:T(1,128)S(1)}, s32[128,1]{0,1:T(1,128)}, u32[]{:S(2)}) copy-start(s32[128,1]{0,1:T(1,128)} %pad_add_fusion.4) | copy-start | bytes 1540
  257.0 51.4 %copy-start.33 = (bf16[128,1,768]{0,2,1:T(8,128)(2,1)}, bf16[128,1,768]{0,2,1:T(8,128)(2,1)S(1)}, u32[]{:S(2)}) copy-start(bf16[128,1,768]{0,2,1:T(8,128)(2,1)S(1)} %get-tuple-element.1044) | copy-start | bytes 589828
  257.0 51.4 %copy-start.57 = (s32[256,1]{0,1:T(1,128)}, s32[256,1]{0,1:T(1,128)S(1)}, u32[]{:S(2)}) copy-start(s32[256,1]{0,1:T(1,128)S(1)} %get-tuple-element.2008) | copy-start | bytes 3076
  260.2 48.2 %copy-start.86 = (f32[128]{0:T(128)}, f32[128]{0:T(128)S(1)}, u32[]{:S(2)}) copy-start(f32[128]{0:T(128)S(1)} %fusion.182) | copy-start | bytes 1540
  392.3 11.7 collective-permute-start.1
  415.1 239.2 %copy-start.1 = (f32[512,768]{0,1:T(8,128)}, f32[512,768]{0,1:T(8,128)S(1)}, u32[]{:S(2)}) copy-start(f32[512,768]{0,1:T(8,128)S(1)} %copy.188) | copy-start | bytes 4718596
  417.6 236.7 %copy-start.3 = (f32[512,768]{0,1:T(8,128)}, f32[512,768]{0,1:T(8,128)S(1)}, u32[]{:S(2)}) copy-start(f32[512,768]{0,1:T(8,128)S(1)} %copy.189) | copy-start | bytes 4718596
  427.8 70.3 %collective-permute-start.2 = (bf16[2,1024,1,768]{3,1,2,0:T(8,128)(2,1)}, bf16[2,1024,1,768]{3,1,2,0:T(8,128)(2,1)}, u32[]{:S(2)}, u32[]{:S(2)}) collective-permute-start(bf16[2,1024,1,768]{3,1,2,0:T(8,128)(2,1)} %pad_maximum_fusion.4), channel_id=1, source_target_pairs={{0,1},{1,0},{2,3},{3,2},{4,5},{5,4},{6,7},{7,6},{8,9},{9,8},{10,11... | collective-permute-start | bytes 9437192 | tf_op jit(solution)/shard_map/ppermute | solution.py:19
  429.0 266.6 %copy-start.80 = (f32[1024]{0:T(1024)}, f32[1024]{0:T(1024)S(1)}, u32[]{:S(2)}) copy-start(f32[1024]{0:T(1024)S(1)} %compare_convert_fusion) | copy-start | bytes 12292
  447.9 53.4 %copy-start.17 = (bf16[1024,768]{1,0:T(8,128)(2,1)S(1)}, bf16[1024,768]{1,0:T(8,128)(2,1)}, u32[]{:S(2)}) copy-start(bf16[1024,768]{1,0:T(8,128)(2,1)} %copy-done.16) | copy-start | bytes 4718596
  657.6 38.0 %copy-start.24 = (f32[1024,768]{0,1:T(8,128)}, f32[1024,768]{0,1:T(8,128)S(1)}, u32[]{:S(2)}) copy-start(f32[1024,768]{0,1:T(8,128)S(1)} %get-tuple-element.1420) | copy-start | bytes 9437188
  657.7 37.9 %copy-start.82 = (f32[1024]{0:T(1024)}, f32[1024]{0:T(1024)S(1)}, u32[]{:S(2)}) copy-start(f32[1024]{0:T(1024)S(1)} %fusion.177) | copy-start | bytes 12292
  1060.9 69.4 %collective-permute-start.3 = (bf16[2,1024,1,768]{1,3,2,0:T(8,128)(2,1)}, bf16[2,1024,1,768]{1,3,2,0:T(8,128)(2,1)}, u32[]{:S(2)}, u32[]{:S(2)}) collective-permute-start(bf16[2,1024,1,768]{1,3,2,0:T(8,128)(2,1)} %pad_maximum_fusion.7), channel_id=1, source_target_pairs={{0,1},{1,0},{2,3},{3,2},{4,5},{5,4},{6,7},{7,6},{8,9},{9,8},{10,11... | collective-permute-start | bytes 9437192 | tf_op jit(solution)/shard_map/ppermute | solution.py:19
  1065.9 67.0 %slice-start.2 = ((s8[6291456]{0:T(1024)(128)(4,1)}), s8[4194304]{0:T(1024)(128)(4,1)S(1)}, s32[]{:S(2)}) async-start(s8[6291456]{0:T(1024)(128)(4,1)} %bitcast.644), calls=%async_computation.28 | async-start | bytes 8388608
  1068.4 64.6 %slice-start = ((s8[6291456]{0:T(1024)(128)(4,1)}), s8[4194304]{0:T(1024)(128)(4,1)S(1)}, s32[]{:S(2)}) async-start(s8[6291456]{0:T(1024)(128)(4,1)} %bitcast.642), calls=%async_computation.26 | async-start | bytes 8388608
  1068.4 64.6 %slice-start.3 = ((s8[6291456]{0:T(1024)(128)(4,1)}), s8[2097152]{0:T(1024)(128)(4,1)S(1)}, s32[]{:S(2)}) async-start(s8[6291456]{0:T(1024)(128)(4,1)} %bitcast.644), calls=%async_computation.29 | async-start | bytes 4194304
  1070.9 62.1 %slice-start.1 = ((s8[6291456]{0:T(1024)(128)(4,1)}), s8[2097152]{0:T(1024)(128)(4,1)S(1)}, s32[]{:S(2)}) async-start(s8[6291456]{0:T(1024)(128)(4,1)} %bitcast.642), calls=%async_computation.27 | async-start | bytes 4194304
  1167.1 5.9 collective-permute-start.4
  1183.4 140.9 %reduce-scatter.19.cloned.1.call-start = ((), (), s32[]{:S(2)}) async-start(), calls=%async_computation.17 | async-start | bytes 8847360 | tf_op jit(solution)/shard_map/reduce_scatter | solution.py:466
  1222.3 8.1 collective-permute-start.5
  1235.7 151.0 %reduce-scatter.23.cloned.1.call-start = ((), (), s32[]{:S(2)}) async-start(), calls=%async_computation.19 | async-start | bytes 11796480 | tf_op jit(solution)/shard_map/reduce_scatter | solution.py:472
  1258.7 201.6 %reduce-scatter.25.cloned.1.call-start = ((), (), s32[]{:S(2)}) async-start(), calls=%async_computation.20 | async-start | bytes 11796480 | tf_op jit(solution)/shard_map/reduce_scatter | solution.py:475
  1285.5 197.5 %reduce-scatter.35.cloned.1.call-start = ((), (), s32[]{:S(2)}) async-start(), calls=%async_computation.25 | async-start | bytes 245760
  1294.5 271.4 %reduce-scatter.31.cloned.1.call-start = ((), (), s32[]{:S(2)}) async-start(), calls=%async_computation.23 | async-start | bytes 663552
  1297.1 337.7 %reduce-scatter.29.cloned.1.call-start = ((), (), s32[]{:S(2)}) async-start(), calls=%async_computation.22 | async-start | bytes 1990656
  1382.2 72.2 %all-to-all-start.1 = ((bf16[8,2,98304]{2,1,0:T(2,128)(2,1)}), bf16[8,2,98304]{2,1,0:T(2,128)(2,1)}, u32[]{:S(2)}, u32[]{:S(2)}) async-start(bf16[8,2,98304]{2,1,0:T(2,128)(2,1)} %reshape.2469), calls=%async_computation.1 | async-start | bytes 6291456 | tf_op jit(solution)/shard_map/all_to_all | solution.py:442
  1386.6 319.3 %reduce-scatter.33.cloned.1.call-start = ((), (), s32[]{:S(2)}) async-start(), calls=%async_computation.24 | async-start | bytes 2654208
  1421.4 38.9 %copy-start.111 = (u32[32]{0:T(128)S(1)}, u32[32]{0:T(128)}, u32[]{:S(2)}) copy-start(u32[32]{0:T(128)} %constant.749) | copy-start | bytes 388
  1454.4 93.4 %all-to-all-start.3 = ((bf16[8,2,98304]{2,1,0:T(2,128)(2,1)}), bf16[8,2,98304]{2,1,0:T(2,128)(2,1)S(1)}, u32[]{:S(2)}, u32[]{:S(2)}) async-start(bf16[8,2,98304]{2,1,0:T(2,128)(2,1)} %reshape.2471), calls=%async_computation.3 | async-start | bytes 6291456 | tf_op jit(solution)/shard_map/all_to_all | solution.py:445
  1458.0 319.4 %reduce-scatter.27.cloned.1.call-start = ((), (), s32[]{:S(2)}) async-start(), calls=%async_computation.21 | async-start | bytes 2654208 | tf_op jit(solution)/shard_map/reduce_scatter | solution.py:492
  1780.5 44.0 %copy-start.85 = (f32[5,24]{1,0:T(8,128)S(1)}, f32[5,24]{1,0:T(8,128)}, u32[]{:S(2)}) copy-start(f32[5,24]{1,0:T(8,128)} %param.35) | copy-start | bytes 1444
  1780.5 44.0 %copy-start.96 = (f32[5,24]{1,0:T(8,128)S(1)}, f32[5,24]{1,0:T(8,128)}, u32[]{:S(2)}) copy-start(f32[5,24]{1,0:T(8,128)} %param.45) | copy-start | bytes 1444
  1780.5 44.0 %copy-start.97 = (f32[5,24]{1,0:T(8,128)S(1)}, f32[5,24]{1,0:T(8,128)}, u32[]{:S(2)}) copy-start(f32[5,24]{1,0:T(8,128)} %param.40) | copy-start | bytes 1444
  1784.2 45.5 %copy-start.30 = (bf16[24,2,3072]{2,1,0:T(2,128)(2,1)S(1)}, bf16[24,2,3072]{2,1,0:T(2,128)(2,1)}, u32[]{:S(2)}) copy-start(bf16[24,2,3072]{2,1,0:T(2,128)(2,1)} %reshape.2451) | copy-start | bytes 884740
  1784.2 45.5 %copy-start.31 = (f32[2,24,3072]{2,1,0:T(8,128)S(1)}, f32[2,24,3072]{2,1,0:T(8,128)}, u32[]{:S(2)}) copy-start(f32[2,24,3072]{2,1,0:T(8,128)} %param.33) | copy-start | bytes 1769476
  1784.2 45.5 %copy-start.53 = (f32[2,24,3072]{2,1,0:T(8,128)S(1)}, f32[2,24,3072]{2,1,0:T(8,128)}, u32[]{:S(2)}) copy-start(f32[2,24,3072]{2,1,0:T(8,128)} %param.43) | copy-start | bytes 1769476
  1784.2 45.5 %copy-start.54 = (f32[2,24,3072]{2,1,0:T(8,128)S(1)}, f32[2,24,3072]{2,1,0:T(8,128)}, u32[]{:S(2)}) copy-start(f32[2,24,3072]{2,1,0:T(8,128)} %param.38) | copy-start | bytes 1769476
  (131 other events, 665.7 us)
Sparse Core Ops, SparseCore 0:
  11.7 118.0 all-gather.5
  133.4 56.2 all-gather.7
  193.4 110.5 all-gather.9
  307.4 80.0 all-gather.11
  1183.5 31.6 reduce-scatter.20
  1235.8 62.2 reduce-scatter.18
  1300.7 78.4 reduce-scatter.22
  1381.8 78.4 reduce-scatter.24
  1463.2 19.6 reduce-scatter.34
  1486.7 79.1 reduce-scatter.30
  1569.7 65.0 reduce-scatter.28
  1638.1 67.7 reduce-scatter.32
  1709.4 68.0 reduce-scatter.26
where the time goes:
time: 1860 us; the launch traced here: 1840 us
  waiting for transfers between devices  517 us (28%)
  matrix products  382 us (21%)
  other arithmetic  355 us (19%)
  local copies, waits for them, and re-layouts  304 us (16%)
  blocking collectives  233 us (13%)
  starting transfers between devices  26.2 us (1%)
  between operations  21.5 us (1%)
    unnamed x17, waiting for transfers between devices  155 us
    all_gather x1, blocking collectives, body(): lax.all_gather(vectors.astype(jnp.bfloat16), ('dp', 'seq'), axis=1, tiled...  151 us
    ppermute x6, waiting for transfers between devices, from_partner(): return lax.ppermute(value, axis, pairs)  137 us
    dot_general x36, matrix products, score_block(): jnp.einsum('qsha,ksha->shqk', q_block, k_block, preferred_element_type=jn...  98.2 us
    unnamed x266, local copies, waits for them, and re-layouts  84.6 us
    convert_element_type x18, other arithmetic, one_step(): d_scores = (probs_all * (d_probs - inner_sum)).astype(jnp.bfloat16)  79.3 us
    all_gather x1, waiting for transfers between devices, body(): lax.all_gather(down_w.astype(jnp.bfloat16), ('dp', 'seq'), axis=1, tiled=...  79.2 us
    reduce_scatter x1, waiting for transfers between devices, body(): lax.psum_scatter(partial_sums[3].astype(jnp.bfloat16), 'seq', scatter_dim...  67.3 us
  transfers between devices with their start and end apart: 23, of which 14 were waited for; matrix products, arithmetic and copies ran while one was open for 22% of the time, Pallas kernels for 0%

commit v1 on v0

v1 whole, which is shorter than its diff:
```python
import functools
import math

import jax
import jax.numpy as jnp
from jax import lax
from jax.experimental import pallas as pl
from jax.experimental.pallas import tpu as pltpu
from jax.sharding import Mesh
from jax.sharding import PartitionSpec as P

D = 768
FF = 3072
LEN = 2048
NPARAMS = 14159616
EPS = 1e-06
PAIRS = 6
TQ = 256
NN = (((1,), (0,)), ((), ()))
NT = (((1,), (1,)), ((), ()))
TN = (((0,), (0,)), ((), ()))
BF = jnp.bfloat16
F32 = jnp.float32


def dotf(left, right, dims):
    return lax.dot_general(left, right, dims, preferred_element_type=F32)


def far_mask(core, tile, lb, q_axis):
    shift = lb.bit_length() - 1
    iq = lax.broadcasted_iota(jnp.int32, (TQ, TQ), q_axis) >> shift
    ik = lax.broadcasted_iota(jnp.int32, (TQ, TQ), 1 - q_axis) >> shift
    odd = (core + tile * (TQ >> shift) + iq) & 1
    return (iq > ik) | ((iq == ik) & (odd == 1))


def attend_kernel(lb, core_ref, *refs):
    if lb:
        q_ref, ko, vo, kf, vf, o_ref, lse_ref = refs
    else:
        q_ref, ko, vo, o_ref, lse_ref = refs
    rows = q_ref.shape[0]
    lane = lax.broadcasted_iota(jnp.int32, (TQ, 128), 1)
    tri = lax.broadcasted_iota(jnp.int32, (TQ, TQ), 0) >= lax.broadcasted_iota(
        jnp.int32, (TQ, TQ), 1
    )
    for t in range(rows // TQ):
        n = t * TQ
        q = q_ref[pl.ds(n, TQ), :] * BF(0.125)
        outs = []
        cols = []
        if lb:
            fm = far_mask(core_ref[0], t, lb, 0)
        for h in range(2):
            qm = jnp.where((lane >= 64) if h else (lane < 64), q, BF(0))
            segs = []
            if t:
                segs.append((dotf(qm, ko[pl.ds(0, n), :], NT), vo[pl.ds(0, n), :]))
            segs.append(
                (jnp.where(tri, dotf(qm, ko[pl.ds(n, TQ), :], NT), -1e30), vo[pl.ds(n, TQ), :])
            )
            if lb:
                if t:
                    segs.append((dotf(qm, kf[pl.ds(0, n), :], NT), vf[pl.ds(0, n), :]))
                segs.append(
                    (jnp.where(fm, dotf(qm, kf[pl.ds(n, TQ), :], NT), -1e30), vf[pl.ds(n, TQ), :])
                )
            top = functools.reduce(
                jnp.maximum, [jnp.max(s, axis=1, keepdims=True) for s, _ in segs]
            )
            total = 0.0
            acc = 0.0
            for s, v in segs:
                e = jnp.exp(s - top)
                total = total + jnp.sum(e, axis=1, keepdims=True)
                acc = acc + dotf(e.astype(BF), v, NN)
            outs.append(acc * (1.0 / total))
            cols.append(jnp.broadcast_to(top + jnp.log(total), (TQ, 128)))
        o_ref[pl.ds(n, TQ), :] = jnp.where(lane < 64, outs[0], outs[1]).astype(BF)
        for h in range(2):
            lse_ref[0, pl.ds(h, 1), pl.ds(n, TQ)] = cols[h].T[0:1, :]


def attend(q, k_own, v_own, far, core, lb):
    rows = q[0].shape[0]
    ops = [q, k_own, v_own] + list(far)

    def spec(off):
        return pl.BlockSpec((rows, 128), lambda i, off=off: (0, off + i))

    size = 12 * rows * rows * (1 if far else 0.5)
    return pl.pallas_call(
        functools.partial(attend_kernel, lb if far else 0),
        grid=(PAIRS,),
        in_specs=[pl.BlockSpec(memory_space=pltpu.SMEM)] + [spec(o) for _, o in ops],
        out_specs=[spec(0), pl.BlockSpec((1, 2, rows), lambda i: (i, 0, 0))],
        out_shape=[
            jax.ShapeDtypeStruct((rows, D), BF),
            jax.ShapeDtypeStruct((PAIRS, 2, rows), F32),
        ],
        compiler_params=pltpu.CompilerParams(vmem_limit_bytes=40 * 2**20),
        cost_estimate=pl.CostEstimate(
            flops=int(4 * 64 * 6 * size), bytes_accessed=rows * D * 12, transcendentals=int(size)
        ),
        name="attend_far" if far else "attend_own",
    )(core, *[a for a, _ in ops])


def attend_back_kernel(lb, kc, core_ref, *refs):
    if lb:
        q_ref, do_ref, o_ref, lse_ref, ko, vo, kf, vf = refs[:8]
        dq_ref, dko, dvo, dkf, dvf, k_t, aok, aov, afk, afv = refs[8:]
        parts = [(ko, vo, aok, aov, 0), (kf, vf, afk, afv, 1)]
    else:
        q_ref, do_ref, o_ref, lse_ref, ko, vo, dq_ref, dko, dvo, k_t, aok, aov = refs
        parts = [(ko, vo, aok, aov, 0)]
    rows = q_ref.shape[0]
    lane = lax.broadcasted_iota(jnp.int32, (TQ, 128), 1)
    tri = lax.broadcasted_iota(jnp.int32, (TQ, TQ), 1) >= lax.broadcasted_iota(
        jnp.int32, (TQ, TQ), 0
    )
    for k, _, ak, av, s in parts:
        k_t[s] = k[...].astype(F32).T.astype(BF)
        ak[...] = jnp.zeros_like(ak)
        av[...] = jnp.zeros_like(av)
    for t in range(rows // TQ):
        n = t * TQ
        q = q_ref[pl.ds(n, TQ), :] * BF(0.125)
        do = do_ref[pl.ds(n, TQ), :]
        prod = (do.astype(F32) * o_ref[pl.ds(n, TQ), :].astype(F32)).T
        dqs = []
        if lb:
            fm = far_mask(core_ref[0], t, lb, 1)
        for h in range(2):
            half = (lane >= 64) if h else (lane < 64)
            qm = jnp.where(half, q, BF(0))
            dom = jnp.where(half, do, BF(0))
            inner = jnp.sum(prod[64 * h : 64 * h + 64], axis=0, keepdims=True)
            lse = lse_ref[0, pl.ds(h, 1), pl.ds(n, TQ)]
            dq_t = 0.0
            for k, v, ak, av, s in parts:
                spans = []
                a = 0
                while a < n:
                    w = min(kc, n - a)
                    spans.append((a, w, None))
                    a += w
                spans.append((n, TQ, fm if s else tri))
                for a, w, mask in spans:
                    p = jnp.exp(dotf(k[pl.ds(a, w), :], qm, NT) - lse)
                    if mask is not None:
                        p = jnp.where(mask, p, 0.0)
                    dp = dotf(v[pl.ds(a, w), :], dom, NT)
                    ds = (p * (dp - inner)).astype(BF)
                    av[pl.ds(a, w), :] += dotf(p.astype(BF), dom, NN)
                    ak[pl.ds(a, w), :] += dotf(ds, qm, NN)
                    dq_t = dq_t + dotf(k_t[s, 64 * h : 64 * h + 64, a : a + w], ds, NN)
            dqs.append(dq_t)
        dq_ref[pl.ds(n, TQ), :] = (jnp.concatenate(dqs, axis=0) * 0.125).T.astype(BF)
    dko[...] = aok[...].astype(dko.dtype)
    dvo[...] = aov[...].astype(dvo.dtype)
    if lb:
        dkf[...] = afk[...].astype(dkf.dtype)
        dvf[...] = afv[...].astype(dvf.dtype)


def attend_back(q, do, o, lse, k_own, v_own, far, core, lb, own_type, kc=512):
    rows = do[0].shape[0]

    def spec(off):
        return pl.BlockSpec((rows, 128), lambda i, off=off: (0, off + i))

    lse_spec = pl.BlockSpec((1, 2, rows), lambda i: (i, 0, 0))
    ops = [q, do, o, None, k_own, v_own] + list(far)
    types = [BF, own_type, own_type] + ([BF] * 2 if far else [])
    size = 12 * rows * rows * (1 if far else 0.5)
    return pl.pallas_call(
        functools.partial(attend_back_kernel, lb if far else 0, kc),
        grid=(PAIRS,),
        in_specs=[pl.BlockSpec(memory_space=pltpu.SMEM)]
        + [lse_spec if e is None else spec(e[1]) for e in ops],
        out_specs=[spec(0)] * len(types),
        out_shape=[jax.ShapeDtypeStruct((rows, D), t) for t in types],
        scratch_shapes=[pltpu.VMEM((2 if far else 1, 128, rows), BF)]
        + [pltpu.VMEM((rows, 128), F32)] * (len(types) - 1),
        compiler_params=pltpu.CompilerParams(vmem_limit_bytes=40 * 2**20),
        cost_estimate=pl.CostEstimate(
            flops=int(10 * 64 * 5 * size), bytes_accessed=rows * D * 24, transcendentals=int(size)
        ),
        name="attend_back_far" if far else "attend_back_own",
    )(core, *[lse if e is None else e[0] for e in ops])


def norm_parts(rows):
    scale = lax.rsqrt(jnp.mean(rows * rows, axis=-1, keepdims=True) + EPS)
    return rows * scale, scale


def norm_back(d_out, unit, scale, gain):
    d_gain = jnp.sum(d_out * unit, axis=0)
    d_unit = d_out * gain
    d_rows = scale * (d_unit - unit * jnp.mean(d_unit * unit, axis=-1, keepdims=True))
    return d_rows, d_gain


def gelu_parts(pre):
    c = math.sqrt(2.0 / math.pi)
    sq = pre * pre
    t = jnp.tanh(c * pre * (1.0 + 0.044715 * sq))
    act = 0.5 * pre * (1.0 + t)
    slope = 0.5 * (1.0 + t) + 0.5 * pre * (1.0 - t * t) * (c * (1.0 + 3 * 0.044715 * sq))
    return act.astype(BF), slope.astype(BF)


def block_forward(rows, weights, gain_a, gain_b, far_of, core, lb):
    w_qkv, w_out, w_up, w_down = weights
    unit_a, scale_a = norm_parts(rows)
    n1 = (unit_a * gain_a).astype(BF)
    qkv = dotf(n1, w_qkv, NN).astype(BF)
    far = far_of(qkv)
    own = ((qkv, 0), (qkv, 6), (qkv, 12))
    o, lse = attend(*own, far, core, lb)
    branch = dotf(o, w_out, NN)
    mid = rows + branch
    unit_b, scale_b = norm_parts(mid)
    n2 = (unit_b * gain_b).astype(BF)
    act, slope = gelu_parts(dotf(n2, w_up, NN))
    mlp = dotf(act, w_down, NN)
    return branch, mid, mlp, (n1, own, far, o, lse, n2, act, slope)


def block_backward(
    rows, mid, weights, gain_a, gain_b, saved, d_mlp, d_top, d_extra, home, pick, core, lb
):
    w_qkv, w_out, w_up, w_down = weights
    n1, own, far, o, lse, n2, act, slope = saved
    mlp_low = d_mlp.astype(BF)
    g_down = dotf(pick(act), mlp_low, TN).astype(BF)
    d_pre = (slope.astype(F32) * dotf(mlp_low, w_down, NT)).astype(BF)
    g_up = dotf(pick(n2), d_pre, TN).astype(BF)
    unit_b, scale_b = norm_parts(mid)
    d_mid, g_b = norm_back(dotf(d_pre, w_up, NT), unit_b, scale_b, gain_b)
    if d_top is not None:
        d_mid = d_mid + d_top
    d_branch = (d_mid if d_extra is None else d_mid + d_extra).astype(BF)
    g_out = dotf(pick(o), d_branch, TN).astype(BF)
    do = dotf(d_branch, w_out, NT).astype(BF)
    back = attend_back(own[0], (do, 0), (o, 0), lse, own[1], own[2], far, core, lb, F32 if far else BF)
    d_qkv = jnp.concatenate([back[0]] + home(back[1:]), axis=1)
    g_qkv = dotf(pick(n1), d_qkv, TN).astype(BF)
    unit_a, scale_a = norm_parts(rows)
    d_rows, g_a = norm_back(dotf(d_qkv, w_qkv, NT), unit_a, scale_a, gain_a)
    return d_rows + d_mid, (g_qkv, g_out, g_up, g_down), g_a, g_b


def shifted(value, axes, sizes, steps):
    pairs = []
    total = math.prod(sizes)
    for source in range(total):
        rest = source
        place = []
        for size in reversed(sizes):
            place.append(rest % size)
            rest //= size
        target = 0
        for size, at, step in zip(sizes, reversed(place), steps):
            target = target * size + (at + step) % size
        pairs.append((source, target))
    return lax.ppermute(value, axes, pairs)


def solution(mesh):
    dp, seq = mesh.shape["dp"], mesh.shape["seq"]
    y_n = dp // 2
    x_n = y_n if seq % y_n == 0 else 1
    z_n = seq // x_n
    half = seq // 2
    ways = dp * seq
    inner = Mesh(mesh.devices.reshape(y_n, 2, z_n, x_n), ("y", "core", "z", "x"))
    every = ("y", "core", "z", "x")
    home_axes = ("core", "z", "x")
    lb = LEN // seq

    def route(t):
        pairs = []
        for c in range(2):
            for s in range(seq):
                block = s // 2
                core = (s ^ block) & 1
                pairs.append((c * seq + s, core * seq + 2 * ((block + t) % half) + c))
        return pairs

    routes = [route(t) for t in range(half)]

    def swap_core(value):
        return lax.ppermute(value, "core", [(0, 1), (1, 0)])

    def all_sum(value):
        for axis, size in (("core", 2), ("x", x_n), ("y", y_n), ("z", z_n)):
            value = sum(
                (shifted(value, (axis,), (size,), (s,)) for s in range(1, size)), start=value
            )
        return value

    def body(
        tokens, cotangent, picked_ids, lengths,
        qkv_w, out_w, up_w, down_w, vectors,
        qkv_mom, out_mom, up_mom, down_mom, vec_mom,
        qkv_avg, out_avg, up_avg, down_avg, vec_avg,
    ):
        y, core, z, x = (lax.axis_index(a) for a in every)
        chip = z * x_n + x
        seq_id = chip // 2
        group = chip % 2
        core_arr = jnp.full((1,), core, jnp.int32)
        piece = D // ways

        def grown(value, axis, size, place, dim):
            if size == 1:
                return jnp.expand_dims(value, dim)
            behind = [shifted(value, (axis,), (size,), (s,)) for s in range(1, size)]
            if size == 2:
                first = place == 0
                return jnp.stack(
                    [jnp.where(first, value, behind[0]), jnp.where(first, behind[0], value)], dim
                )
            twice = jnp.stack(([value] + behind[::-1]) * 2, dim)
            return lax.dynamic_slice_in_dim(twice, size - place, size, dim)

        def spread(shard, x_first):
            value = grown(shard, "z", z_n, z, 0)
            if x_first:
                value = grown(value, "x", x_n, x, 1)
                value = grown(value, "y", y_n, y, 0)
            else:
                value = grown(value, "y", y_n, y, 0)
                value = grown(value, "x", x_n, x, 2)
            value = grown(value, "core", 2, core, 1)
            return value.reshape(ways * shard.shape[0], shard.shape[1])

        shard_a = jnp.concatenate(
            [qkv_w[0].transpose(1, 0, 2).reshape(piece, 3 * D), out_w[0]], axis=1
        ).astype(BF)
        gains_row = jnp.pad(vectors.T, ((0, 0), (0, 128 - 5))).astype(BF)
        full_a = spread(jnp.concatenate([shard_a, gains_row], axis=1), True)
        gains = full_a[:, 4 * D : 4 * D + 5].T.astype(F32)
        weights0 = (
            full_a[:, : 3 * D],
            full_a[:, 3 * D : 4 * D],
            spread(up_w[0].astype(BF), False),
            spread(down_w[0].astype(BF), True),
        )

        packed = jnp.concatenate(
            [
                qkv_w[1].reshape(3 * piece, D),
                out_w[1],
                up_w[1].reshape(piece, 4, D).transpose(1, 0, 2).reshape(4 * piece, D),
                down_w[1],
            ]
        ).astype(BF)
        full = lax.all_gather(packed, every, axis=0, tiled=False)
        w_qkv = full[:, : 3 * piece].reshape(ways, 3, piece, D).transpose(0, 2, 1, 3)
        w_out = full[:, 3 * piece : 4 * piece]
        w_up = full[:, 4 * piece : 8 * piece].reshape(ways, 4, piece, D).transpose(0, 2, 1, 3)
        w_down = full[:, 8 * piece :]
        weights1 = (
            w_qkv.reshape(D, 3 * D),
            w_out.reshape(D, D),
            w_up.reshape(D, FF),
            w_down.reshape(FF, D),
        )

        def rolled(parts, start):
            count = len(parts)
            twice = jnp.stack(parts + parts)
            return lax.dynamic_slice_in_dim(twice, (count - start) % count, count, 0)

        def come(source):
            by_seq = source.transpose(1, 0, 2)
            got = []
            for t in range(half):
                sent = lax.dynamic_index_in_dim(by_seq, (chip // 2 + t) % half, 0, keepdims=False)
                got.append(lax.ppermute(sent, home_axes, routes[t]))
            return rolled(got[:1] + got[:0:-1], seq_id).reshape(half * lb, D)

        def leave(rows):
            got = []
            for t in range(half):
                sent = lax.dynamic_slice(rows, (((seq_id - t) % half) * lb, 0), (lb, D))
                got.append(lax.ppermute(sent, home_axes, [(b, a) for a, b in routes[t]]))
            return rolled(got, chip // 2).transpose(1, 0, 2)

        own_x = come(tokens)
        own_cot = come(cotangent)
        meta = jnp.concatenate([picked_ids, lengths[:, None]], axis=1)
        meta = lax.dynamic_index_in_dim(
            jnp.where(group == core, meta, swap_core(meta)), seq_id, 0, keepdims=False
        )
        picks, length = meta[:-1], meta[-1]
        row_ids = jnp.arange(half * lb, dtype=jnp.int32)
        block = row_ids // lb
        places = (2 * block + ((core + block) & 1)) * lb + row_ids % lb
        chosen = (picks[:, None] == places[None, :]).astype(BF)
        live = (places < length).astype(F32)[:, None]

        def at_picks(rows):
            part = dotf(chosen, rows, NN).astype(BF)
            return part + swap_core(part)

        def to_rows(values):
            return dotf(chosen, values, TN)

        x_low = at_picks(own_x)
        x_rows = x_low.astype(F32)
        gate = jax.nn.sigmoid(jnp.sum(x_rows * gains[2], axis=-1, keepdims=True))
        branch0, mid0, mlp0, saved0 = block_forward(
            x_rows, weights0, gains[0], gains[1], lambda qkv: (), core_arr, lb
        )
        both0 = branch0 + mlp0
        delta = (gate * both0).astype(BF)
        mixed = own_x.astype(F32) + to_rows(delta)

        def far_of(qkv):
            far = swap_core(qkv[:, D:])
            return ((far, 0), (far, 6))

        def home1(parts):
            dk, dv, dk_far, dv_far = parts
            back = swap_core(jnp.concatenate([dk_far, dv_far], axis=1)).astype(F32)
            return [(dk + back[:, :D]).astype(BF), (dv + back[:, D:]).astype(BF)]

        branch1, mid1, mlp1, saved1 = block_forward(
            mixed, weights1, gains[3], gains[4], far_of, core_arr, lb
        )
        activations = leave((live * (mid1 + mlp1)).astype(BF))
        d_top = live * own_cot.astype(F32)
        d_mixed, grads1, g_a1, g_b1 = block_backward(
            mixed, mid1, weights1, gains[3], gains[4], saved1, d_top, d_top, None,
            home1, lambda a: a, core_arr, lb,
        )

        def mine(rows):
            width = rows.shape[1]
            split = rows.reshape(rows.shape[0], y_n, 2, width // dp)
            return lax.dynamic_index_in_dim(split, core, 2, keepdims=False).reshape(
                rows.shape[0], width // 2
            )

        d_delta = at_picks(d_mixed.astype(BF)).astype(F32)
        gated = gate * d_delta
        d_logit = gate * (1.0 - gate) * jnp.sum(d_delta * both0, axis=-1, keepdims=True)
        d_rows0, grads0, g_a0, g_b0 = block_backward(
            x_rows, mid0, weights0, gains[0], gains[1], saved0, gated, None, gated,
            lambda parts: list(parts), mine, core_arr, lb,
        )
        g_r = jnp.sum(d_logit * x_rows, axis=0)
        d_chosen = (d_rows0 + d_logit * gains[2]).astype(BF)
        input_grad = leave((d_mixed + to_rows(d_chosen)).astype(BF)).astype(F32)

        def packed_rows(grad, which):
            cores = 1 if which is None else 2
            block = grad.shape[0] * grad.shape[1] // (y_n * cores * z_n * x_n * D)
            wide = grad.shape[1] // D
            split = grad.reshape(y_n, cores, z_n, x_n, block // wide, wide, D)
            if which is None:
                split = split[:, 0]
            else:
                split = lax.dynamic_index_in_dim(split, which, 1, keepdims=False)
            return jnp.swapaxes(split, 3, 4).reshape(y_n, z_n, x_n, block, D)

        def pack(grads, which):
            return jnp.concatenate([packed_rows(g, which) for g in grads], axis=3)

        def over_core(grads):
            got = swap_core(pack(grads, 1 - core))
            return (pack(grads, core).astype(F32) + got.astype(F32)).astype(BF)

        def over(value, axis, size, place, dim, kind=BF):
            total = lax.dynamic_index_in_dim(value, place, dim, keepdims=False).astype(F32)
            for s in range(1, size):
                sent = lax.dynamic_index_in_dim(value, (place + s) % size, dim, keepdims=False)
                total = total + shifted(sent, (axis,), (size,), (s,)).astype(F32)
            return total.astype(kind)

        def over_chips(value):
            cut = value.shape[3] // 16 * 8
            one = over(over(value[..., :cut, :], "y", y_n, y, 0), "x", x_n, x, 1)
            two = over(over(value[..., cut:, :], "x", x_n, x, 2), "y", y_n, y, 0)
            return over(jnp.concatenate([one, two], axis=1), "z", z_n, z, 0, F32)

        tail1 = lax.psum_scatter(
            over_core(grads1[1:]).reshape(ways // 2, 9 * piece, D),
            ("y", "z", "x"), scatter_dimension=0,
        ).astype(F32)
        head1 = over_chips(over_core(grads1[:1]))
        tail0 = over_chips(pack(grads0[1:], None))
        head0 = over_chips(pack(grads0[:1], None))
        g_vec = all_sum(jnp.stack([0.5 * g_a0, 0.5 * g_b0, 0.5 * g_r, g_a1, g_b1]))
        shard_id = ((y * 2 + core) * z_n + z) * x_n + x
        both = ((head0, tail0), (head1, tail1))
        shards = [
            jnp.stack([h.reshape(3, piece, D) for h, _ in both]),
            jnp.stack([t[:piece] for _, t in both]),
            jnp.stack(
                [
                    t[piece : 5 * piece].reshape(4, piece, D).transpose(1, 0, 2).reshape(piece, FF)
                    for _, t in both
                ]
            ),
            jnp.stack([t[5 * piece :] for _, t in both]),
        ]
        squares = sum(jnp.sum(s * s) for s in shards)
        norm_sq = all_sum(squares.reshape(1, 1))[0, 0] + jnp.sum(g_vec * g_vec)
        grad_norm = jnp.sqrt(norm_sq)
        shards.append(lax.dynamic_slice(g_vec, (0, shard_id * piece), (5, piece)))
        factor = 1.0 / jnp.maximum(grad_norm, 1.0)
        base_rate = math.sqrt(NPARAMS / D)
        rates = (base_rate, math.sqrt(NPARAMS * LEN / (8 * D)), base_rate, base_rate, base_rate)
        masters = (qkv_w, out_w, up_w, down_w, vectors)
        moms = (qkv_mom, out_mom, up_mom, down_mom, vec_mom)
        avgs = (qkv_avg, out_avg, up_avg, down_avg, vec_avg)
        new_w, new_m, new_z = [], [], []
        for weight, grad, mom, avg, rate in zip(masters, shards, moms, avgs, rates):
            clipped = grad * factor
            m = 0.5 * mom + clipped
            w = weight - rate * (clipped + 0.5 * m)
            new_w.append(w)
            new_m.append(m)
            new_z.append(0.5 * avg + 0.5 * w)
        return (activations, input_grad, grad_norm, *new_w, *new_m, *new_z)

    group_spec = ("y", "core")
    pos_spec = ("z", "x")
    rows_spec = P(pos_spec, group_spec, None)
    param_specs = (
        P(None, None, every, None),
        P(None, every, None),
        P(None, every, None),
        P(None, every, None),
        P(None, every),
    )
    return jax.shard_map(
        body,
        mesh=inner,
        in_specs=(rows_spec, rows_spec, P(group_spec, None), P(group_spec)) + param_specs * 3,
        out_specs=(rows_spec, rows_spec, P()) + param_specs * 3,
        check_vma=False,
    )
```

time: 1860 us -> 948 us (0.51)
  other arithmetic: 355 us -> 83.5 us
  matrix products: 382 us -> 113 us
  blocking collectives: 233 us -> 0 us
  waiting for transfers between devices: 517 us -> 312 us
  local copies, waits for them, and re-layouts: 304 us -> 188 us
  Pallas kernels: 0 us -> 94.7 us
  starting transfers between devices: 26.2 us -> 114 us
    dot_general x164 -> x28, matrix products: 382 us -> 113 us  [dotf(): return lax.dot_general(left, right, dims, preferred_element_type=F32)]
    ppermute x6 -> x74, waiting for transfers between devices: 137 us -> 312 us  [the longest x51 252 us: shifted(): return lax.ppermute(value, axes, pairs)]
    unnamed x17 -> x2, waiting for transfers between devices: 155 us -> 0.03 us
    all_gather x1 -> x0, blocking collectives: 151 us -> none  [body(): lax.all_gather(vectors.astype(jnp.bfloat16), ('dp', 'seq'), axis=1, tiled...]
    all_gather x4 -> x1, waiting for transfers between devices: 123 us -> 0.01 us  [body(): full = lax.all_gather(packed, every, axis=0, tiled=False)]
    convert_element_type x34 -> x25, other arithmetic: 152 us -> 31.3 us  [the longest x2 9.79 us: over_core(): return (pack(grads, core).astype(F32) + got.astype(F32)).astype(BF)]
    ppermute x6 -> x74, starting transfers between devices: 5.72 us -> 114 us  [the longest x51 73.2 us: shifted(): return lax.ppermute(value, axes, pairs)]
    pallas_call x0 -> x4, Pallas kernels: none -> 94.7 us  [the longest x2 58.1 us: attend_back(): pl.pallas_call(functools.partial(attend_back_kernel, lb if far else 0, kc...]
  transfers between devices with their start and end apart: 23 -> 76, of which waited for: 14 -> 29; matrix products, arithmetic and copies ran while one was open for 22% -> 29% of each run, Pallas kernels for 0% -> 7%
where the time goes in v1:
time: 948 us; the launch traced here: 931 us
  waiting for transfers between devices  312 us (33%)
  local copies, waits for them, and re-layouts  188 us (20%)
  starting transfers between devices  114 us (12%)
  matrix products  113 us (12%)
  Pallas kernels  94.7 us (10%)
  other arithmetic  83.5 us (9%)
  between operations  24.8 us (3%)
    ppermute x51, waiting for transfers between devices, shifted(): return lax.ppermute(value, axes, pairs)  252 us
    dot_general x28, matrix products, dotf(): return lax.dot_general(left, right, dims, preferred_element_type=F32)  113 us
    ppermute x51, starting transfers between devices, shifted(): return lax.ppermute(value, axes, pairs)  73.2 us
    unnamed x357, local copies, waits for them, and re-layouts  64.9 us
    pallas_call x2, Pallas kernels, attend_back(): pl.pallas_call(functools.partial(attend_back_kernel, lb if far else 0, kc...  58.1 us
    ppermute x8, waiting for transfers between devices, leave(): got.append(lax.ppermute(sent, home_axes, [(b, a) for a, b in routes[t]]))  49.2 us
    pallas_call x2, Pallas kernels, attend(): pl.pallas_call(functools.partial(attend_kernel, lb if far else 0), grid=(...  36.6 us
    ppermute x8, starting transfers between devices, leave(): got.append(lax.ppermute(sent, home_axes, [(b, a) for a, b in routes[t]]))  20.7 us
  transfers between devices with their start and end apart: 76, of which 29 were waited for; matrix products, arithmetic and copies ran while one was open for 29% of the time, Pallas kernels for 7%

profile of v1, /device:TPU:0, one launch (start us, length us, event | category | flops | bytes accessed | tf_op | source)
XLA Modules:
  0.0 930.8 jit_solution(13877715841360057989)
XLA Ops:
  26.1 6.8 collective-permute-done.12
  37.0 5.4 collective-permute-done.13
  55.4 7.5 collective-permute-done.19
  69.3 7.7 constant_dynamic-slice_fusion.16
  113.2 11.7 %collective-permute-start.30 = (bf16[256,768]{1,0:T(8,128)(2,1)}, bf16[256,768]{1,0:T(8,128)(2,1)}, u32[]{:S(2)}, u32[]{:S(2)}) collective-permute-start(bf16[256,768]{1,0:T(8,128)(2,1)} %bitcast.381), channel_id=1, source_target_pairs={{0,6},{1,14},{2,8},{3,0},{4,2},{5,10},{6,12},{7,4},{8,7},{9,15},{1... | collective-permute-start | bytes 1179656 | tf_op jit(solution)/shard_map/ppermute | solution.py:385
  124.9 10.5 %collective-permute-done.2 = bf16[256,768]{1,0:T(8,128)(2,1)S(1)} collective-permute-done((bf16[256,768]{1,0:T(8,128)(2,1)}, bf16[256,768]{1,0:T(8,128)(2,1)S(1)}, u32[]{:S(2)}, u32[]{:S(2)}) %collective-permute-start.2) | collective-permute-done | bytes 393248 | tf_op jit(solution)/shard_map/ppermute | solution.py:385
  141.7 9.8 %collective-permute-done.15 = bf16[4,24,3072]{2,1,0:T(8,128)(2,1)} collective-permute-done((bf16[4,24,3072]{2,1,0:T(8,128)(2,1)}, bf16[4,24,3072]{2,1,0:T(8,128)(2,1)}, u32[]{:S(2)}, u32[]{:S(2)}) %collective-permute-start.15) | collective-permute-done | bytes 589856 | tf_op jit(solution)/shard_map/ppermute | solution.py:270
  153.4 4.1 collective-permute-done.21
  158.8 20.7 %collective-permute-done.9 = bf16[4,24,3200]{2,1,0:T(8,128)(2,1)S(1)} collective-permute-done((bf16[4,24,3200]{2,1,0:T(8,128)(2,1)}, bf16[4,24,3200]{2,1,0:T(8,128)(2,1)S(1)}, u32[]{:S(2)}, u32[]{:S(2)}) %collective-permute-start.9) | collective-permute-done | bytes 614432 | tf_op jit(solution)/shard_map/ppermute | solution.py:270
  181.7 38.8 %collective-permute-done.22 = bf16[4,2,96,768]{3,2,1,0:T(8,128)(2,1)S(1)} collective-permute-done((bf16[4,2,96,768]{3,2,1,0:T(8,128)(2,1)S(1)}, bf16[4,2,96,768]{3,2,1,0:T(8,128)(2,1)S(1)}, u32[]{:S(2)}, u32[]{:S(2)}) %collective-permute-start.22) | collective-permute-done | bytes 1179680 | tf_op jit(solution)/shard_map/ppermute | solution.py:270
  224.8 24.0 %collective-permute-done.10 = bf16[4,2,24,3200]{3,2,0,1:T(8,128)(2,1)S(1)} collective-permute-done((bf16[4,2,24,3200]{3,2,0,1:T(8,128)(2,1)S(1)}, bf16[4,2,24,3200]{3,2,0,1:T(8,128)(2,1)S(1)}, u32[]{:S(2)}, u32[]{:S(2)}) %collective-permute-start.10) | collective-permute-done | bytes 1228832 | tf_op jit(solution)/shard_map/ppermute | solution.py:270
  263.6 5.5 attend_own.1
  282.9 4.5 convolution_convert_fusion.refs_0_.refs_1_.refs_2_.refs_4_.refs_5_
  311.8 5.2 reshape.449
  317.0 4.2 constant_dynamic-slice_fusion.5
  321.1 4.6 copy.207
  329.7 7.9 fusion.149
  337.6 4.8 copy.159
  344.9 31.1 %attend_far.1 = (bf16[1024,768]{1,0:T(8,128)(2,1)S(1)}, f32[6,2,1024]{2,1,0:T(2,128)S(1)}) custom-call(s32[1]{0:T(128)} %bitcast.28.core_ref, bf16[1024,2304]{1,0:T(8,128)(2,1)S(1)} %bitcast.388, bf16[1024,2304]{1,0:T(8,128)(2,1)S(1)} %bitcast.388, bf16[1024,2304]{1,0:T(8,128)(2,1)S(1)} %bitcast.388, ...), custom_call_target="tpu_custom_call" | custom-call | flops 19327352832 | bytes 9437184 | tf_op jit(solution)/shard_map/attend_far/pallas_call | solution.py:93
  377.7 8.5 fusion.148
  386.2 14.5 %multiply_convert_fusion = bf16[1024,3072]{1,0:T(8,128)(2,1)} fusion(bf16[1024,768]{1,0:T(8,128)(2,1)S(1)} %bitcast.450, bf16[3072,768]{1,0:T(8,128)(2,1)S(1)} %bitcast.437, f32[1024,3072]{1,0:T(8,128)} %fusion.148), kind=kOutput, calls=%fused_computation | convolution fusion | flops 4894752768 | bytes 25165824 | tf_op jit(solution)/shard_map/dot_general | solution.py:27
  400.7 10.0 %multiply_reduce_fusion = (f32[768]{0:T(1024)}, f32[1024]{0:T(1024)S(1)}, f32[1024,768]{0,1:T(8,128)}) fusion(f32[1024,768]{0,1:T(8,128)S(1)} %get-tuple-element.230, f32[1024]{0:T(1024)S(1)} %add_rsqrt_fusion, f32[768]{0:T(1024)S(1)} %get-tuple-element.123, bf16[1024,3072]{1,0:T(8,128)(2,1)} %multiply_convert_fusion, bf16[768,3072]{1,0:T(8,128)(2,1)S(1)} %bitcast.399), kind=kOutput, calls=%fused_computation.31 | convolution fusion | flops 4836554752 | bytes 17315840 | tf_op jit(solution)/shard_map/dot_general | solution.py:27
  410.7 6.9 convolution_convert_fusion.2
  417.6 9.3 multiply_convert_fusion.3
  426.9 12.5 %convolution_convert_fusion.1 = bf16[3072,768]{1,0:T(8,128)(2,1)} fusion(f32[1024,768]{0,1:T(8,128)} %copy.194, f32[1024]{0:T(1024)S(1)} %copy-done.104, f32[1024,3072]{1,0:T(8,128)S(1)} %bitcast.407), kind=kOutput, calls=%fused_computation.7 | convolution fusion | flops 4864081920 | bytes 20451328 | tf_op jit(solution)/shard_map/dot_general | solution.py:27
  439.3 9.7 %reshape.452 = bf16[2,2,4,2,24,4,768]{6,5,4,3,2,1,0:T(4,128)(2,1)} reshape(bf16[768,3072]{1,0:T(8,128)(2,1)} %convolution_convert_fusion.2) | data formatting | bytes 9437184 | tf_op jit(solution)/shard_map/reshape | solution.py:466
  456.5 10.9 %collective-permute-start.26 = (bf16[256,768]{0,1:T(8,128)(2,1)S(1)}, bf16[256,768]{0,1:T(8,128)(2,1)S(1)}, u32[]{:S(2)}, u32[]{:S(2)}) collective-permute-start(bf16[256,768]{0,1:T(8,128)(2,1)S(1)} %get-tuple-element.182), channel_id=1, source_target_pairs={{2,0},{10,1},{12,2},{4,3},{6,4},{14,5},{8,6},{0,7},{3,8},{11,9},{1... | collective-permute-start | bytes 1179656 | tf_op jit(solution)/shard_map/ppermute | solution.py:392
  469.1 53.0 %attend_back_far.1 = (bf16[1024,768]{1,0:T(8,128)(2,1)S(1)}, f32[1024,768]{1,0:T(8,128)S(1)}, f32[1024,768]{1,0:T(8,128)S(1)}, bf16[1024,768]{1,0:T(8,128)(2,1)S(1)}, bf16[1024,768]{1,0:T(8,128)(2,1)S(1)}) custom-call(s32[1]{0:T(128)} %bitcast.28.core_ref, bf16[1024,2304]{1,0:T(8,128)(2,1)} %copy-done.4, ...), custom_call_target="tpu_custom_call" | custom-call | flops 40265318400 | bytes 18874368 | tf_op jit(solution)/shard_map/attend_back_far/pallas_call | solution.py:178
  541.9 26.3 %collective-permute-done.27 = bf16[256,768]{0,1:T(8,128)(2,1)S(1)} collective-permute-done((bf16[256,768]{0,1:T(8,128)(2,1)S(1)}, bf16[256,768]{0,1:T(8,128)(2,1)S(1)}, u32[]{:S(2)}, u32[]{:S(2)}) %collective-permute-start.27) | collective-permute-done | bytes 393248 | tf_op jit(solution)/shard_map/ppermute | solution.py:392
  581.2 6.0 multiply_reduce_fusion.1
  591.8 5.2 convolution_convert_fusion.3
  597.6 5.4 reshape.442
  603.0 4.1 constant_dynamic-slice_fusion.10
  630.1 5.1 attend_back_own.1
  635.4 5.0 fusion.57
  644.1 7.6 add_convert_fusion.1
  668.2 5.0 squeeze_reshape.6
  689.8 9.0 collective-permute-done.39
  699.1 20.2 %collective-permute-done.36 = bf16[256,768]{0,1:T(8,128)(2,1)S(1)} collective-permute-done((bf16[256,768]{0,1:T(8,128)(2,1)S(1)}, bf16[256,768]{0,1:T(8,128)(2,1)S(1)}, u32[]{:S(2)}, u32[]{:S(2)}) %collective-permute-start.36) | collective-permute-done | bytes 393248 | tf_op jit(solution)/shard_map/ppermute | solution.py:392
  725.8 46.1 %collective-permute-done.41 = bf16[2,4,40,768]{3,2,1,0:T(8,128)(2,1)S(1)} collective-permute-done((bf16[2,4,40,768]{3,2,1,0:T(8,128)(2,1)S(1)}, bf16[2,4,40,768]{3,2,1,0:T(8,128)(2,1)S(1)}, u32[]{:S(2)}, u32[]{:S(2)}) %collective-permute-start.41) | collective-permute-done | bytes 491552 | tf_op jit(solution)/shard_map/ppermute | solution.py:270
  776.2 4.9 copy.188
  783.2 15.0 %collective-permute-start.43 = (bf16[72,768]{1,0:T(8,128)(2,1)S(1)}, bf16[72,768]{1,0:T(8,128)(2,1)S(1)}, u32[]{:S(2)}, u32[]{:S(2)}) collective-permute-start(bf16[72,768]{1,0:T(8,128)(2,1)S(1)} %get-tuple-element.211), channel_id=1, source_target_pairs={{0,2},{2,4},{4,6},{6,0},{1,3},{3,5},{5,7},{7,1},{8,10},{10,12},{12... | collective-permute-start | bytes 331784 | tf_op jit(solution)/shard_map/ppermute | solution.py:270
  814.0 8.7 collective-permute-done.49
  822.8 10.9 %collective-permute-done.55 = bf16[4,104,768]{2,1,0:T(8,128)(2,1)S(1)} collective-permute-done((bf16[4,104,768]{2,1,0:T(8,128)(2,1)S(1)}, bf16[4,104,768]{2,1,0:T(8,128)(2,1)S(1)}, u32[]{:S(2)}, u32[]{:S(2)}) %collective-permute-start.55) | collective-permute-done | bytes 639008 | tf_op jit(solution)/shard_map/ppermute | solution.py:270
  834.2 5.2 collective-permute-done.48
  839.6 6.0 collective-permute-done.50
  854.7 25.6 %collective-permute-done.52 = bf16[72,768]{1,0:T(8,128)(2,1)S(1)} collective-permute-done((bf16[72,768]{1,0:T(8,128)(2,1)S(1)}, bf16[72,768]{1,0:T(8,128)(2,1)S(1)}, u32[]{:S(2)}, u32[]{:S(2)}) %collective-permute-start.52) | collective-permute-done | bytes 110624 | tf_op jit(solution)/shard_map/ppermute | solution.py:270
  907.3 4.1 collective-permute-done.65
  (684 shorter events, 330.8 us)
Async XLA Ops:
  7.2 270.0 %all-gather.2.cloned.1.call-start = ((), (), s32[]{:S(2)}) async-start(), calls=%async_computation.1 | async-start | bytes 14598144 | tf_op jit(solution)/shard_map/all_gather | solution.py:363
  11.4 94.6 %collective-permute-start.7 = (bf16[24,3200]{1,0:T(8,128)(2,1)}, bf16[24,3200]{1,0:T(8,128)(2,1)S(1)}, u32[]{:S(2)}, u32[]{:S(2)}) collective-permute-start(bf16[24,3200]{1,0:T(8,128)(2,1)} %fusion.103), channel_id=1, source_target_pairs={{0,4},{2,6},{4,0},{6,2},{1,5},{3,7},{5,1},{7,3},{8,12},{10,14},{12... | collective-permute-start | bytes 460808 | tf_op jit(solution)/shard_map/ppermute | solution.py:270
  15.4 88.1 %collective-permute-start.6 = (bf16[24,3200]{1,0:T(8,128)(2,1)}, bf16[24,3200]{1,0:T(8,128)(2,1)}, u32[]{:S(2)}, u32[]{:S(2)}) collective-permute-start(bf16[24,3200]{1,0:T(8,128)(2,1)} %fusion.103), channel_id=1, source_target_pairs={{0,6},{2,0},{4,2},{6,4},{1,7},{3,1},{5,3},{7,5},{8,14},{10,8},{12,... | collective-permute-start | bytes 460808 | tf_op jit(solution)/shard_map/ppermute | solution.py:270
  16.8 90.9 %collective-permute-start.8 = (bf16[24,3200]{1,0:T(8,128)(2,1)}, bf16[24,3200]{1,0:T(8,128)(2,1)}, u32[]{:S(2)}, u32[]{:S(2)}) collective-permute-start(bf16[24,3200]{1,0:T(8,128)(2,1)} %fusion.103), channel_id=1, source_target_pairs={{0,2},{2,4},{4,6},{6,0},{1,3},{3,5},{5,7},{7,1},{8,10},{10,12},{12... | collective-permute-start | bytes 460808 | tf_op jit(solution)/shard_map/ppermute | solution.py:270
  19.2 24.6 %collective-permute-start.14 = (bf16[24,3072]{1,0:T(8,128)(2,1)}, bf16[24,3072]{1,0:T(8,128)(2,1)}, u32[]{:S(2)}, u32[]{:S(2)}) collective-permute-start(bf16[24,3072]{1,0:T(8,128)(2,1)} %get-tuple-element.209), channel_id=1, source_target_pairs={{0,2},{2,4},{4,6},{6,0},{1,3},{3,5},{5,7},{7,1},{8,10},{10,12},{12... | collective-permute-start | bytes 442376 | tf_op jit(solution)/shard_map/ppermute | solution.py:270
  42.5 21.7 %collective-permute-start.20 = (bf16[96,768]{1,0:T(8,128)(2,1)}, bf16[96,768]{1,0:T(8,128)(2,1)}, u32[]{:S(2)}, u32[]{:S(2)}) collective-permute-start(bf16[96,768]{1,0:T(8,128)(2,1)} %get-tuple-element.207), channel_id=1, source_target_pairs={{0,2},{2,4},{4,6},{6,0},{1,3},{3,5},{5,7},{7,1},{8,10},{10,12},{12... | collective-permute-start | bytes 442376 | tf_op jit(solution)/shard_map/ppermute | solution.py:270
  62.9 23.5 %collective-permute-start = (s32[4,257]{1,0:T(4,128)S(1)}, s32[4,257]{1,0:T(4,128)S(1)}, u32[]{:S(2)}, u32[]{:S(2)}) collective-permute-start(s32[4,257]{1,0:T(4,128)S(1)} %pad_add_fusion), channel_id=1, source_target_pairs={{0,8},{8,0},{1,9},{9,1},{2,10},{10,2},{3,11},{11,3},{4,12},{12,4},... | collective-permute-start | bytes 12344 | tf_op jit(solution)/shard_map/ppermute | solution.py:297
  69.2 812.5 %reduce-scatter.2.cloned.1.call-start = ((), (), s32[]{:S(2)}) async-start(), calls=%async_computation.2 | async-start | bytes 5640192 | tf_op jit(solution)/shard_map/reduce_scatter | solution.py:493
  77.8 59.4 %collective-permute-start.4 = (bf16[256,768]{1,0:T(8,128)(2,1)}, bf16[256,768]{1,0:T(8,128)(2,1)}, u32[]{:S(2)}, u32[]{:S(2)}) collective-permute-start(bf16[256,768]{1,0:T(8,128)(2,1)} %bitcast.383), channel_id=1, source_target_pairs={{0,2},{1,10},{2,12},{3,4},{4,6},{5,14},{6,8},{7,0},{8,3},{9,11},{1... | collective-permute-start | bytes 1179656 | tf_op jit(solution)/shard_map/ppermute | solution.py:385
  86.4 49.1 %collective-permute-start.3 = (bf16[256,768]{1,0:T(8,128)(2,1)}, bf16[256,768]{1,0:T(8,128)(2,1)S(1)}, u32[]{:S(2)}, u32[]{:S(2)}) collective-permute-start(bf16[256,768]{1,0:T(8,128)(2,1)} %bitcast.384), channel_id=1, source_target_pairs={{0,4},{1,12},{2,14},{3,6},{4,0},{5,8},{6,10},{7,2},{8,5},{9,13},{1... | collective-permute-start | bytes 1179656 | tf_op jit(solution)/shard_map/ppermute | solution.py:385
  103.6 31.8 %collective-permute-start.2 = (bf16[256,768]{1,0:T(8,128)(2,1)}, bf16[256,768]{1,0:T(8,128)(2,1)S(1)}, u32[]{:S(2)}, u32[]{:S(2)}) collective-permute-start(bf16[256,768]{1,0:T(8,128)(2,1)} %bitcast.385), channel_id=1, source_target_pairs={{0,6},{1,14},{2,8},{3,0},{4,2},{5,10},{6,12},{7,4},{8,7},{9,15},{1... | collective-permute-start | bytes 1179656 | tf_op jit(solution)/shard_map/ppermute | solution.py:385
  107.7 143.1 %collective-permute-start.29 = (bf16[256,768]{1,0:T(8,128)(2,1)}, bf16[256,768]{1,0:T(8,128)(2,1)S(1)}, u32[]{:S(2)}, u32[]{:S(2)}) collective-permute-start(bf16[256,768]{1,0:T(8,128)(2,1)} %bitcast.463), channel_id=1, source_target_pairs={{0,0},{1,8},{2,10},{3,2},{4,4},{5,12},{6,14},{7,6},{8,1},{9,9},{10... | collective-permute-start | bytes 1179656 | tf_op jit(solution)/shard_map/ppermute | solution.py:385
  113.2 178.1 %collective-permute-start.30 = (bf16[256,768]{1,0:T(8,128)(2,1)}, bf16[256,768]{1,0:T(8,128)(2,1)}, u32[]{:S(2)}, u32[]{:S(2)}) collective-permute-start(bf16[256,768]{1,0:T(8,128)(2,1)} %bitcast.381), channel_id=1, source_target_pairs={{0,6},{1,14},{2,8},{3,0},{4,2},{5,10},{6,12},{7,4},{8,7},{9,15},{1... | collective-permute-start | bytes 1179656 | tf_op jit(solution)/shard_map/ppermute | solution.py:385
  135.4 157.2 %collective-permute-start.31 = (bf16[256,768]{1,0:T(8,128)(2,1)}, bf16[256,768]{1,0:T(8,128)(2,1)}, u32[]{:S(2)}, u32[]{:S(2)}) collective-permute-start(bf16[256,768]{1,0:T(8,128)(2,1)} %bitcast.380), channel_id=1, source_target_pairs={{0,4},{1,12},{2,14},{3,6},{4,0},{5,8},{6,10},{7,2},{8,5},{9,13},{1... | collective-permute-start | bytes 1179656 | tf_op jit(solution)/shard_map/ppermute | solution.py:385
  137.1 20.4 %collective-permute-start.21 = (bf16[4,96,768]{2,1,0:T(8,128)(2,1)}, bf16[4,96,768]{2,1,0:T(8,128)(2,1)}, u32[]{:S(2)}, u32[]{:S(2)}) collective-permute-start(bf16[4,96,768]{2,1,0:T(8,128)(2,1)} %constant_dynamic-slice_fusion.24), channel_id=1, source_target_pairs={{0,1},{1,0},{2,3},{3,2},{4,5},{5,4},{6,7},{7,6},{8,9},{9,8},{10,11... | collective-permute-start | bytes 1769480 | tf_op jit(solution)/shard_map/ppermute | solution.py:270
  151.5 28.0 %collective-permute-start.9 = (bf16[4,24,3200]{2,1,0:T(8,128)(2,1)}, bf16[4,24,3200]{2,1,0:T(8,128)(2,1)S(1)}, u32[]{:S(2)}, u32[]{:S(2)}) collective-permute-start(bf16[4,24,3200]{2,1,0:T(8,128)(2,1)} %constant_dynamic-slice_fusion.26), channel_id=1, source_target_pairs={{0,1},{1,0},{2,3},{3,2},{4,5},{5,4},{6,7},{7,6},{8,9},{9,8},{10,11... | collective-permute-start | bytes 1843208 | tf_op jit(solution)/shard_map/ppermute | solution.py:270
  157.5 66.9 %collective-permute-start.16 = (bf16[2,4,24,3072]{3,2,1,0:T(8,128)(2,1)S(1)}, bf16[2,4,24,3072]{3,2,1,0:T(8,128)(2,1)S(1)}, u32[]{:S(2)}, u32[]{:S(2)}) collective-permute-start(bf16[2,4,24,3072]{3,2,1,0:T(8,128)(2,1)S(1)} %pad_maximum_fusion.12), channel_id=1, source_target_pairs={{0,1},{1,0},{2,3},{3,2},{4,5},{5,4},{6,7},{7,6},{8,9},{9,8},{10,11... | collective-permute-start | bytes 3538952 | tf_op jit(solution)/shard_map/ppermute | solution.py:270
  179.5 41.0 %collective-permute-start.22 = (bf16[4,2,96,768]{3,2,1,0:T(8,128)(2,1)S(1)}, bf16[4,2,96,768]{3,2,1,0:T(8,128)(2,1)S(1)}, u32[]{:S(2)}, u32[]{:S(2)}) collective-permute-start(bf16[4,2,96,768]{3,2,1,0:T(8,128)(2,1)S(1)} %pad_maximum_fusion.13), channel_id=1, source_target_pairs={{0,16},{16,0},{1,17},{17,1},{2,18},{18,2},{3,19},{19,3},{4,20},{20... | collective-permute-start | bytes 3538952 | tf_op jit(solution)/shard_map/ppermute | solution.py:270
  220.5 28.3 %collective-permute-start.10 = (bf16[4,2,24,3200]{3,2,0,1:T(8,128)(2,1)S(1)}, bf16[4,2,24,3200]{3,2,0,1:T(8,128)(2,1)S(1)}, u32[]{:S(2)}, u32[]{:S(2)}) collective-permute-start(bf16[4,2,24,3200]{3,2,0,1:T(8,128)(2,1)S(1)} %pad_maximum_fusion.11), channel_id=1, source_target_pairs={{0,16},{16,0},{1,17},{17,1},{2,18},{18,2},{3,19},{19,3},{4,20},{20... | collective-permute-start | bytes 3686408 | tf_op jit(solution)/shard_map/ppermute | solution.py:270
  224.5 28.3 %collective-permute-start.23 = (bf16[2,4,2,96,768]{4,3,2,1,0:T(8,128)(2,1)S(1)}, bf16[2,4,2,96,768]{4,3,2,1,0:T(8,128)(2,1)S(1)}, u32[]{:S(2)}, u32[]{:S(2)}) collective-permute-start(bf16[2,4,2,96,768]{4,3,2,1,0:T(8,128)(2,1)S(1)} %pad_maximum_fusion.8), channel_id=1, source_target_pairs={{0,8},{8,0},{1,9},{9,1},{2,10},{10,2},{3,11},{11,3},{4,12},{12,4},... | collective-permute-start | bytes 7077896 | tf_op jit(solution)/shard_map/ppermute | solution.py:270
  252.7 40.9 %collective-permute-start.32 = (bf16[256,768]{1,0:T(8,128)(2,1)}, bf16[256,768]{1,0:T(8,128)(2,1)}, u32[]{:S(2)}, u32[]{:S(2)}) collective-permute-start(bf16[256,768]{1,0:T(8,128)(2,1)} %bitcast.379), channel_id=1, source_target_pairs={{0,2},{1,10},{2,12},{3,4},{4,6},{5,14},{6,8},{7,0},{8,3},{9,11},{1... | collective-permute-start | bytes 1179656 | tf_op jit(solution)/shard_map/ppermute | solution.py:385
  291.2 53.6 %collective-permute-start.24 = (bf16[1024,1536]{1,0:T(8,128)(2,1)}, bf16[1024,1536]{1,0:T(8,128)(2,1)S(1)}, u32[]{:S(2)}, u32[]{:S(2)}) collective-permute-start(bf16[1024,1536]{1,0:T(8,128)(2,1)} %slice.182), channel_id=1, source_target_pairs={{0,8},{8,0},{1,9},{9,1},{2,10},{10,2},{3,11},{11,3},{4,12},{12,4},... | collective-permute-start | bytes 9437192 | tf_op jit(solution)/shard_map/ppermute | solution.py:297
  456.5 85.4 %collective-permute-start.26 = (bf16[256,768]{0,1:T(8,128)(2,1)S(1)}, bf16[256,768]{0,1:T(8,128)(2,1)S(1)}, u32[]{:S(2)}, u32[]{:S(2)}) collective-permute-start(bf16[256,768]{0,1:T(8,128)(2,1)S(1)} %get-tuple-element.182), channel_id=1, source_target_pairs={{2,0},{10,1},{12,2},{4,3},{6,4},{14,5},{8,6},{0,7},{3,8},{11,9},{1... | collective-permute-start | bytes 1179656 | tf_op jit(solution)/shard_map/ppermute | solution.py:392
  467.5 74.3 %collective-permute-start.25 = (bf16[256,768]{0,1:T(8,128)(2,1)}, bf16[256,768]{0,1:T(8,128)(2,1)S(1)}, u32[]{:S(2)}, u32[]{:S(2)}) collective-permute-start(bf16[256,768]{0,1:T(8,128)(2,1)} %get-tuple-element.183), channel_id=1, source_target_pairs={{0,0},{8,1},{10,2},{2,3},{4,4},{12,5},{14,6},{6,7},{1,8},{9,9},{11... | collective-permute-start | bytes 1179656 | tf_op jit(solution)/shard_map/ppermute | solution.py:392
  525.2 48.6 %collective-permute-start.33 = (bf16[1024,1536]{1,0:T(8,128)(2,1)}, bf16[1024,1536]{1,0:T(8,128)(2,1)}, u32[]{:S(2)}, u32[]{:S(2)}) collective-permute-start(bf16[1024,1536]{1,0:T(8,128)(2,1)} %pad_maximum_fusion.5), channel_id=1, source_target_pairs={{0,8},{8,0},{1,9},{9,1},{2,10},{10,2},{3,11},{11,3},{4,12},{12,4},... | collective-permute-start | bytes 9437192 | tf_op jit(solution)/shard_map/ppermute | solution.py:297
  538.8 29.4 %collective-permute-start.28 = (bf16[256,768]{0,1:T(8,128)(2,1)S(1)}, bf16[256,768]{0,1:T(8,128)(2,1)S(1)}, u32[]{:S(2)}, u32[]{:S(2)}) collective-permute-start(bf16[256,768]{0,1:T(8,128)(2,1)S(1)} %get-tuple-element.180), channel_id=1, source_target_pairs={{6,0},{14,1},{8,2},{0,3},{2,4},{10,5},{12,6},{4,7},{7,8},{15,9},{9... | collective-permute-start | bytes 1179656 | tf_op jit(solution)/shard_map/ppermute | solution.py:392
  538.8 29.4 %collective-permute-start.27 = (bf16[256,768]{0,1:T(8,128)(2,1)S(1)}, bf16[256,768]{0,1:T(8,128)(2,1)S(1)}, u32[]{:S(2)}, u32[]{:S(2)}) collective-permute-start(bf16[256,768]{0,1:T(8,128)(2,1)S(1)} %get-tuple-element.181), channel_id=1, source_target_pairs={{4,0},{12,1},{14,2},{6,3},{0,4},{8,5},{10,6},{2,7},{5,8},{13,9},{1... | collective-permute-start | bytes 1179656 | tf_op jit(solution)/shard_map/ppermute | solution.py:392
  541.7 102.3 %collective-permute-start.61 = (bf16[2,4,2,216,768]{4,3,2,1,0:T(8,128)(2,1)}, bf16[2,4,2,216,768]{4,3,2,1,0:T(8,128)(2,1)}, u32[]{:S(2)}, u32[]{:S(2)}) collective-permute-start(bf16[2,4,2,216,768]{4,3,2,1,0:T(8,128)(2,1)} %pad_maximum_fusion), channel_id=1, source_target_pairs={{0,8},{8,0},{1,9},{9,1},{2,10},{10,2},{3,11},{11,3},{4,12},{12,4},... | collective-permute-start | bytes 15925256 | tf_op jit(solution)/shard_map/ppermute | solution.py:297
  591.2 19.8 %collective-permute-start.34 = (bf16[256,768]{1,0:T(8,128)(2,1)}, bf16[256,768]{1,0:T(8,128)(2,1)}, u32[]{:S(2)}, u32[]{:S(2)}) collective-permute-start(bf16[256,768]{1,0:T(8,128)(2,1)} %fusion.32), channel_id=1, source_target_pairs={{0,8},{8,0},{1,9},{9,1},{2,10},{10,2},{3,11},{11,3},{4,12},{12,4},... | collective-permute-start | bytes 1179656 | tf_op jit(solution)/shard_map/ppermute | solution.py:297
  608.6 193.7 %collective-permute-start.46 = (bf16[2,4,2,72,768]{4,3,2,1,0:T(8,128)(2,1)}, bf16[2,4,2,72,768]{4,3,2,1,0:T(8,128)(2,1)}, u32[]{:S(2)}, u32[]{:S(2)}) collective-permute-start(bf16[2,4,2,72,768]{4,3,2,1,0:T(8,128)(2,1)} %bitcast.107), channel_id=1, source_target_pairs={{0,8},{8,0},{1,9},{9,1},{2,10},{10,2},{3,11},{11,3},{4,12},{12,4},... | collective-permute-start | bytes 5308424 | tf_op jit(solution)/shard_map/ppermute | solution.py:297
  642.3 21.9 %collective-permute-start.68 = (f32[5,768]{1,0:T(8,128)}, f32[5,768]{1,0:T(8,128)}, u32[]{:S(2)}, u32[]{:S(2)}) collective-permute-start(f32[5,768]{1,0:T(8,128)} %stack.310), channel_id=1, source_target_pairs={{0,8},{8,0},{1,9},{9,1},{2,10},{10,2},{3,11},{11,3},{4,12},{12,4},... | collective-permute-start | bytes 46088 | tf_op jit(solution)/shard_map/ppermute | solution.py:270
  657.2 31.8 %collective-permute-start.35 = (bf16[256,768]{0,1:T(8,128)(2,1)}, bf16[256,768]{0,1:T(8,128)(2,1)S(1)}, u32[]{:S(2)}, u32[]{:S(2)}) collective-permute-start(bf16[256,768]{0,1:T(8,128)(2,1)} %get-tuple-element.175), channel_id=1, source_target_pairs={{0,0},{8,1},{10,2},{2,3},{4,4},{12,5},{14,6},{6,7},{1,8},{9,9},{11... | collective-permute-start | bytes 1179656 | tf_op jit(solution)/shard_map/ppermute | solution.py:392
  683.8 41.3 %collective-permute-start.38 = (bf16[256,768]{0,1:T(8,128)(2,1)S(1)}, bf16[256,768]{0,1:T(8,128)(2,1)S(1)}, u32[]{:S(2)}, u32[]{:S(2)}) collective-permute-start(bf16[256,768]{0,1:T(8,128)(2,1)S(1)} %copy-done.83), channel_id=1, source_target_pairs={{6,0},{14,1},{8,2},{0,3},{2,4},{10,5},{12,6},{4,7},{7,8},{15,9},{9... | collective-permute-start | bytes 1179656 | tf_op jit(solution)/shard_map/ppermute | solution.py:392
  685.1 38.3 %collective-permute-start.37 = (bf16[256,768]{0,1:T(8,128)(2,1)S(1)}, bf16[256,768]{0,1:T(8,128)(2,1)S(1)}, u32[]{:S(2)}, u32[]{:S(2)}) collective-permute-start(bf16[256,768]{0,1:T(8,128)(2,1)S(1)} %copy-done.84), channel_id=1, source_target_pairs={{4,0},{12,1},{14,2},{6,3},{0,4},{8,5},{10,6},{2,7},{5,8},{13,9},{1... | collective-permute-start | bytes 1179656 | tf_op jit(solution)/shard_map/ppermute | solution.py:392
  689.1 30.3 %collective-permute-start.36 = (bf16[256,768]{0,1:T(8,128)(2,1)S(1)}, bf16[256,768]{0,1:T(8,128)(2,1)S(1)}, u32[]{:S(2)}, u32[]{:S(2)}) collective-permute-start(bf16[256,768]{0,1:T(8,128)(2,1)S(1)} %copy-done.85), channel_id=1, source_target_pairs={{2,0},{10,1},{12,2},{4,3},{6,4},{14,5},{8,6},{0,7},{3,8},{11,9},{1... | collective-permute-start | bytes 1179656 | tf_op jit(solution)/shard_map/ppermute | solution.py:392
  698.7 99.4 %collective-permute-start.54 = (bf16[4,2,104,768]{3,2,0,1:T(8,128)(2,1)}, bf16[4,2,104,768]{3,2,0,1:T(8,128)(2,1)}, u32[]{:S(2)}, u32[]{:S(2)}) collective-permute-start(bf16[4,2,104,768]{3,2,0,1:T(8,128)(2,1)} %fusion.25), channel_id=1, source_target_pairs={{0,16},{16,0},{1,17},{17,1},{2,18},{18,2},{3,19},{19,3},{4,20},{20... | collective-permute-start | bytes 3833864 | tf_op jit(solution)/shard_map/ppermute | solution.py:270
  719.4 86.9 %collective-permute-start.56 = (bf16[2,4,112,768]{3,2,1,0:T(8,128)(2,1)}, bf16[2,4,112,768]{3,2,1,0:T(8,128)(2,1)}, u32[]{:S(2)}, u32[]{:S(2)}) collective-permute-start(bf16[2,4,112,768]{3,2,1,0:T(8,128)(2,1)} %fusion.20), channel_id=1, source_target_pairs={{0,1},{1,0},{2,3},{3,2},{4,5},{5,4},{6,7},{7,6},{8,9},{9,8},{10,11... | collective-permute-start | bytes 4128776 | tf_op jit(solution)/shard_map/ppermute | solution.py:270
  723.4 48.4 %collective-permute-start.41 = (bf16[2,4,40,768]{3,2,1,0:T(8,128)(2,1)S(1)}, bf16[2,4,40,768]{3,2,1,0:T(8,128)(2,1)S(1)}, u32[]{:S(2)}, u32[]{:S(2)}) collective-permute-start(bf16[2,4,40,768]{3,2,1,0:T(8,128)(2,1)S(1)} %dynamic-slice_bitcast_fusion.8), channel_id=1, source_target_pairs={{0,1},{1,0},{2,3},{3,2},{4,5},{5,4},{6,7},{7,6},{8,9},{9,8},{10,11... | collective-permute-start | bytes 1474568 | tf_op jit(solution)/shard_map/ppermute | solution.py:270
  725.1 55.9 %collective-permute-start.40 = (bf16[4,32,768]{2,1,0:T(8,128)(2,1)}, bf16[4,32,768]{2,1,0:T(8,128)(2,1)}, u32[]{:S(2)}, u32[]{:S(2)}) collective-permute-start(bf16[4,32,768]{2,1,0:T(8,128)(2,1)} %dynamic-slice_bitcast_fusion.13), channel_id=1, source_target_pairs={{0,1},{1,0},{2,3},{3,2},{4,5},{5,4},{6,7},{7,6},{8,9},{9,8},{10,11... | collective-permute-start | bytes 589832 | tf_op jit(solution)/shard_map/ppermute | solution.py:270
  783.2 64.2 %collective-permute-start.43 = (bf16[72,768]{1,0:T(8,128)(2,1)S(1)}, bf16[72,768]{1,0:T(8,128)(2,1)S(1)}, u32[]{:S(2)}, u32[]{:S(2)}) collective-permute-start(bf16[72,768]{1,0:T(8,128)(2,1)S(1)} %get-tuple-element.211), channel_id=1, source_target_pairs={{0,2},{2,4},{4,6},{6,0},{1,3},{3,5},{5,7},{7,1},{8,10},{10,12},{12... | collective-permute-start | bytes 331784 | tf_op jit(solution)/shard_map/ppermute | solution.py:270
  798.1 52.1 %collective-permute-start.44 = (bf16[72,768]{1,0:T(8,128)(2,1)S(1)}, bf16[72,768]{1,0:T(8,128)(2,1)S(1)}, u32[]{:S(2)}, u32[]{:S(2)}) collective-permute-start(bf16[72,768]{1,0:T(8,128)(2,1)S(1)} %get-tuple-element.212), channel_id=1, source_target_pairs={{0,4},{2,6},{4,0},{6,2},{1,5},{3,7},{5,1},{7,3},{8,12},{10,14},{12... | collective-permute-start | bytes 331784 | tf_op jit(solution)/shard_map/ppermute | solution.py:270
  798.1 52.9 %collective-permute-start.45 = (bf16[72,768]{1,0:T(8,128)(2,1)S(1)}, bf16[72,768]{1,0:T(8,128)(2,1)S(1)}, u32[]{:S(2)}, u32[]{:S(2)}) collective-permute-start(bf16[72,768]{1,0:T(8,128)(2,1)S(1)} %get-tuple-element.213), channel_id=1, source_target_pairs={{0,6},{2,0},{4,2},{6,4},{1,7},{3,1},{5,3},{7,5},{8,14},{10,8},{12,... | collective-permute-start | bytes 331784 | tf_op jit(solution)/shard_map/ppermute | solution.py:270
  813.3 20.4 %collective-permute-start.55 = (bf16[4,104,768]{2,1,0:T(8,128)(2,1)S(1)}, bf16[4,104,768]{2,1,0:T(8,128)(2,1)S(1)}, u32[]{:S(2)}, u32[]{:S(2)}) collective-permute-start(bf16[4,104,768]{2,1,0:T(8,128)(2,1)S(1)} %dynamic-slice_bitcast_fusion.4), channel_id=1, source_target_pairs={{0,1},{1,0},{2,3},{3,2},{4,5},{5,4},{6,7},{7,6},{8,9},{9,8},{10,11... | collective-permute-start | bytes 1916936 | tf_op jit(solution)/shard_map/ppermute | solution.py:270
  845.8 35.2 %collective-permute-start.58 = (bf16[216,768]{1,0:T(8,128)(2,1)S(1)}, bf16[216,768]{1,0:T(8,128)(2,1)S(1)}, u32[]{:S(2)}, u32[]{:S(2)}) collective-permute-start(bf16[216,768]{1,0:T(8,128)(2,1)S(1)} %get-tuple-element.188), channel_id=1, source_target_pairs={{0,2},{2,4},{4,6},{6,0},{1,3},{3,5},{5,7},{7,1},{8,10},{10,12},{12... | collective-permute-start | bytes 995336 | tf_op jit(solution)/shard_map/ppermute | solution.py:270
  847.3 33.8 %collective-permute-start.59 = (bf16[216,768]{1,0:T(8,128)(2,1)S(1)}, bf16[216,768]{1,0:T(8,128)(2,1)S(1)}, u32[]{:S(2)}, u32[]{:S(2)}) collective-permute-start(bf16[216,768]{1,0:T(8,128)(2,1)S(1)} %get-tuple-element.189), channel_id=1, source_target_pairs={{0,4},{2,6},{4,0},{6,2},{1,5},{3,7},{5,1},{7,3},{8,12},{10,14},{12... | collective-permute-start | bytes 995336 | tf_op jit(solution)/shard_map/ppermute | solution.py:270
  850.3 30.8 %collective-permute-start.60 = (bf16[216,768]{1,0:T(8,128)(2,1)S(1)}, bf16[216,768]{1,0:T(8,128)(2,1)S(1)}, u32[]{:S(2)}, u32[]{:S(2)}) collective-permute-start(bf16[216,768]{1,0:T(8,128)(2,1)S(1)} %get-tuple-element.190), channel_id=1, source_target_pairs={{0,6},{2,0},{4,2},{6,4},{1,7},{3,1},{5,3},{7,5},{8,14},{10,8},{12,... | collective-permute-start | bytes 995336 | tf_op jit(solution)/shard_map/ppermute | solution.py:270
  851.0 29.3 %collective-permute-start.52 = (bf16[72,768]{1,0:T(8,128)(2,1)S(1)}, bf16[72,768]{1,0:T(8,128)(2,1)S(1)}, u32[]{:S(2)}, u32[]{:S(2)}) collective-permute-start(bf16[72,768]{1,0:T(8,128)(2,1)S(1)} %get-tuple-element.215), channel_id=1, source_target_pairs={{0,4},{2,6},{4,0},{6,2},{1,5},{3,7},{5,1},{7,3},{8,12},{10,14},{12... | collective-permute-start | bytes 331784 | tf_op jit(solution)/shard_map/ppermute | solution.py:270
  853.6 26.7 %collective-permute-start.53 = (bf16[72,768]{1,0:T(8,128)(2,1)S(1)}, bf16[72,768]{1,0:T(8,128)(2,1)S(1)}, u32[]{:S(2)}, u32[]{:S(2)}) collective-permute-start(bf16[72,768]{1,0:T(8,128)(2,1)S(1)} %get-tuple-element.216), channel_id=1, source_target_pairs={{0,6},{2,0},{4,2},{6,4},{1,7},{3,1},{5,3},{7,5},{8,14},{10,8},{12,... | collective-permute-start | bytes 331784 | tf_op jit(solution)/shard_map/ppermute | solution.py:270
  (176 other events, 1922.1 us)
Sparse Core Ops, SparseCore 0:
  69.3 169.3 all-gather.1
  651.8 180.7 reduce-scatter.1

commit v2 on v1

v2 whole, which is shorter than its diff:
```python
import functools
import math

import jax
import jax.numpy as jnp
from jax import lax
from jax.experimental import pallas as pl
from jax.experimental.pallas import tpu as pltpu
from jax.sharding import Mesh
from jax.sharding import PartitionSpec as P

D = 768
FF = 3072
LEN = 2048
NPARAMS = 14159616
EPS = 1e-06
PAIRS = 6
TQ = 256
NN = (((1,), (0,)), ((), ()))
NT = (((1,), (1,)), ((), ()))
TN = (((0,), (0,)), ((), ()))
BF = jnp.bfloat16
F32 = jnp.float32


def dotf(left, right, dims):
    return lax.dot_general(left, right, dims, preferred_element_type=F32)


def far_mask(core, tile, lb, q_axis):
    shift = lb.bit_length() - 1
    iq = lax.broadcasted_iota(jnp.int32, (TQ, TQ), q_axis) >> shift
    ik = lax.broadcasted_iota(jnp.int32, (TQ, TQ), 1 - q_axis) >> shift
    odd = (core + tile * (TQ >> shift) + iq) & 1
    return (iq > ik) | ((iq == ik) & (odd == 1))


def attend_kernel(lb, core_ref, *refs):
    if lb:
        q_ref, ko, vo, kf, vf, o_ref, lse_ref = refs
    else:
        q_ref, ko, vo, o_ref, lse_ref = refs
    rows = q_ref.shape[0]
    lane = lax.broadcasted_iota(jnp.int32, (TQ, 128), 1)
    tri = lax.broadcasted_iota(jnp.int32, (TQ, TQ), 0) >= lax.broadcasted_iota(
        jnp.int32, (TQ, TQ), 1
    )
    for t in range(rows // TQ):
        n = t * TQ
        q = q_ref[pl.ds(n, TQ), :] * BF(0.125)
        outs = []
        cols = []
        if lb:
            fm = far_mask(core_ref[0], t, lb, 0)
        for h in range(2):
            qm = jnp.where((lane >= 64) if h else (lane < 64), q, BF(0))
            segs = []
            if t:
                segs.append((dotf(qm, ko[pl.ds(0, n), :], NT), vo[pl.ds(0, n), :]))
            segs.append(
                (jnp.where(tri, dotf(qm, ko[pl.ds(n, TQ), :], NT), -1e30), vo[pl.ds(n, TQ), :])
            )
            if lb:
                if t:
                    segs.append((dotf(qm, kf[pl.ds(0, n), :], NT), vf[pl.ds(0, n), :]))
                segs.append(
                    (jnp.where(fm, dotf(qm, kf[pl.ds(n, TQ), :], NT), -1e30), vf[pl.ds(n, TQ), :])
                )
            top = functools.reduce(
                jnp.maximum, [jnp.max(s, axis=1, keepdims=True) for s, _ in segs]
            )
            total = 0.0
            acc = 0.0
            for s, v in segs:
                e = jnp.exp(s - top)
                total = total + jnp.sum(e, axis=1, keepdims=True)
                acc = acc + dotf(e.astype(BF), v, NN)
            outs.append(acc * (1.0 / total))
            cols.append(jnp.broadcast_to(top + jnp.log(total), (TQ, 128)))
        o_ref[pl.ds(n, TQ), :] = jnp.where(lane < 64, outs[0], outs[1]).astype(BF)
        for h in range(2):
            lse_ref[0, pl.ds(h, 1), pl.ds(n, TQ)] = cols[h].T[0:1, :]


def attend(q, k_own, v_own, far, core, lb):
    rows = q[0].shape[0]
    ops = [q, k_own, v_own] + list(far)

    def spec(off):
        return pl.BlockSpec((rows, 128), lambda i, off=off: (0, off + i))

    size = 12 * rows * rows * (1 if far else 0.5)
    return pl.pallas_call(
        functools.partial(attend_kernel, lb if far else 0),
        grid=(PAIRS,),
        in_specs=[pl.BlockSpec(memory_space=pltpu.SMEM)] + [spec(o) for _, o in ops],
        out_specs=[spec(0), pl.BlockSpec((1, 2, rows), lambda i: (i, 0, 0))],
        out_shape=[
            jax.ShapeDtypeStruct((rows, D), BF),
            jax.ShapeDtypeStruct((PAIRS, 2, rows), F32),
        ],
        compiler_params=pltpu.CompilerParams(vmem_limit_bytes=40 * 2**20),
        cost_estimate=pl.CostEstimate(
            flops=int(4 * 64 * 6 * size), bytes_accessed=rows * D * 12, transcendentals=int(size)
        ),
        name="attend_far" if far else "attend_own",
    )(core, *[a for a, _ in ops])


def attend_back_kernel(lb, kc, core_ref, *refs):
    if lb:
        q_ref, do_ref, o_ref, lse_ref, ko, vo, kf, vf = refs[:8]
        dq_ref, d_own, d_far, k_t, aok, aov, afk, afv = refs[8:]
        parts = [(ko, vo, aok, aov, 0), (kf, vf, afk, afv, 1)]
    else:
        q_ref, do_ref, o_ref, lse_ref, ko, vo, dq_ref, d_own, k_t, aok, aov = refs
        parts = [(ko, vo, aok, aov, 0)]
    rows = q_ref.shape[0]
    lane = lax.broadcasted_iota(jnp.int32, (TQ, 128), 1)
    tri = lax.broadcasted_iota(jnp.int32, (TQ, TQ), 1) >= lax.broadcasted_iota(
        jnp.int32, (TQ, TQ), 0
    )
    for k, _, ak, av, s in parts:
        k_t[s] = k[...].astype(F32).T.astype(BF)
        ak[...] = jnp.zeros_like(ak)
        av[...] = jnp.zeros_like(av)
    for t in range(rows // TQ):
        n = t * TQ
        q = q_ref[pl.ds(n, TQ), :] * BF(0.125)
        do = do_ref[pl.ds(n, TQ), :]
        prod = (do.astype(F32) * o_ref[pl.ds(n, TQ), :].astype(F32)).T
        dqs = []
        if lb:
            fm = far_mask(core_ref[0], t, lb, 1)
        for h in range(2):
            half = (lane >= 64) if h else (lane < 64)
            qm = jnp.where(half, q, BF(0))
            dom = jnp.where(half, do, BF(0))
            inner = jnp.sum(prod[64 * h : 64 * h + 64], axis=0, keepdims=True)
            lse = lse_ref[0, pl.ds(h, 1), pl.ds(n, TQ)]
            dq_t = 0.0
            for k, v, ak, av, s in parts:
                spans = []
                a = 0
                while a < n:
                    w = min(kc, n - a)
                    spans.append((a, w, None))
                    a += w
                spans.append((n, TQ, fm if s else tri))
                for a, w, mask in spans:
                    p = jnp.exp(dotf(k[pl.ds(a, w), :], qm, NT) - lse)
                    if mask is not None:
                        p = jnp.where(mask, p, 0.0)
                    dp = dotf(v[pl.ds(a, w), :], dom, NT)
                    ds = (p * (dp - inner)).astype(BF)
                    av[pl.ds(a, w), :] += dotf(p.astype(BF), dom, NN)
                    ak[pl.ds(a, w), :] += dotf(ds, qm, NN)
                    dq_t = dq_t + dotf(k_t[s, 64 * h : 64 * h + 64, a : a + w], ds, NN)
            dqs.append(dq_t)
        dq_ref[pl.ds(n, TQ), :] = (jnp.concatenate(dqs, axis=0) * 0.125).T.astype(BF)
    d_own[0] = aok[...].astype(d_own.dtype)
    d_own[1] = aov[...].astype(d_own.dtype)
    if lb:
        d_far[0] = afk[...].astype(BF)
        d_far[1] = afv[...].astype(BF)


def attend_back(q, do, o, lse, k_own, v_own, far, core, lb, first, count, kc=512):
    rows = do[0].shape[0]

    def spec(off):
        return pl.BlockSpec((rows, 128), lambda i, off=off: (0, off + i))

    two = pl.BlockSpec((2, rows, 128), lambda i: (0, 0, i))
    lse_spec = pl.BlockSpec((1, 2, rows), lambda i: (i + first, 0, 0))
    ops = [q, do, o, None, k_own, v_own] + list(far)
    wide = count * 128
    outs = [
        jax.ShapeDtypeStruct((rows, wide), BF),
        jax.ShapeDtypeStruct((2, rows, wide), F32 if far else BF),
    ]
    if far:
        outs.append(jax.ShapeDtypeStruct((2, rows, wide), BF))
    size = 2 * count * rows * rows * (1 if far else 0.5)
    return pl.pallas_call(
        functools.partial(attend_back_kernel, lb if far else 0, kc),
        grid=(count,),
        in_specs=[pl.BlockSpec(memory_space=pltpu.SMEM)]
        + [lse_spec if e is None else spec(e[1] + first) for e in ops],
        out_specs=[spec(0)] + [two] * (len(outs) - 1),
        out_shape=outs,
        scratch_shapes=[pltpu.VMEM((2 if far else 1, 128, rows), BF)]
        + [pltpu.VMEM((rows, 128), F32)] * (4 if far else 2),
        compiler_params=pltpu.CompilerParams(vmem_limit_bytes=40 * 2**20),
        cost_estimate=pl.CostEstimate(
            flops=int(10 * 64 * 5 * size), bytes_accessed=rows * D * 24, transcendentals=int(size)
        ),
        name="attend_back_far" if far else "attend_back_own",
    )(core, *[lse if e is None else e[0] for e in ops])


def place_kernel(count, start_ref, *refs):
    out = refs[count]
    for s in range(count):
        at = start_ref[0] + s
        out[0, jnp.where(at >= count, at - count, at)] = refs[s][0]


def placed(parts, start, dim):
    count = len(parts)
    shape = parts[0].shape
    r, c = shape[-2:]
    g = math.prod(shape[:dim])
    h = math.prod(shape[dim:-2])
    cut = h
    while cut % 2 == 0 and cut * r * c * count > 2**20:
        cut //= 2
    got = pl.pallas_call(
        functools.partial(place_kernel, count),
        grid=(g, h // cut),
        in_specs=[pl.BlockSpec(memory_space=pltpu.SMEM)]
        + [pl.BlockSpec((1, cut, r, c), lambda i, j: (i, j, 0, 0))] * count,
        out_specs=pl.BlockSpec((1, count, cut, r, c), lambda i, j: (i, 0, j, 0, 0)),
        out_shape=jax.ShapeDtypeStruct((g, count, h, r, c), parts[0].dtype),
        compiler_params=pltpu.CompilerParams(vmem_limit_bytes=32 * 2**20),
        cost_estimate=pl.CostEstimate(
            flops=0, bytes_accessed=4 * count * math.prod(shape), transcendentals=0
        ),
        name="place",
    )(start.reshape(1).astype(jnp.int32), *[p.reshape(g, h, r, c) for p in parts])
    return got.reshape(shape[:dim] + (count,) + shape[dim:])


def mlp_kernel(n2_ref, up_ref, down_ref, act_ref, slope_ref, mlp_ref):
    rows = n2_ref.shape[0]

    @pl.when(pl.program_id(0) == 0)
    def _():
        mlp_ref[...] = jnp.zeros_like(mlp_ref)

    for t in range(rows // TQ):
        part = pl.ds(t * TQ, TQ)
        act, slope = gelu_parts(dotf(n2_ref[part, :], up_ref[...], NN))
        act_ref[part, :] = act
        slope_ref[part, :] = slope
        mlp_ref[part, :] += dotf(act, down_ref[...], NN)


def up_spec(wide):
    return pl.BlockSpec((D, wide), lambda i: (0, i))


def down_spec(wide, first=0):
    cuts = D // wide
    return pl.BlockSpec((wide, D), lambda i: (i % cuts, first + i // cuts))


def mlp_forward(n2, w_mlp, wide=768):
    rows = n2.shape[0]
    whole = pl.BlockSpec((rows, D), lambda i: (0, 0))
    across = pl.BlockSpec((rows, wide), lambda i: (0, i))
    return pl.pallas_call(
        mlp_kernel,
        grid=(FF // wide,),
        in_specs=[whole, up_spec(wide), down_spec(wide, FF // D)],
        out_specs=[across, across, whole],
        out_shape=[
            jax.ShapeDtypeStruct((rows, FF), BF),
            jax.ShapeDtypeStruct((rows, FF), BF),
            jax.ShapeDtypeStruct((rows, D), F32),
        ],
        compiler_params=pltpu.CompilerParams(vmem_limit_bytes=40 * 2**20),
        cost_estimate=pl.CostEstimate(
            flops=4 * rows * D * FF,
            bytes_accessed=4 * rows * FF + 4 * D * FF + 6 * rows * D,
            transcendentals=rows * FF,
        ),
        name="mlp_forward",
    )(n2, w_mlp, w_mlp)


def mlp_back_kernel(
    dm_ref, n2_ref, act_ref, slope_ref, up_ref, down_ref, gu_ref, gd_ref, dn_ref, dm_t, n2_t, pre
):
    rows = dm_ref.shape[0]

    @pl.when(pl.program_id(0) == 0)
    def _():
        dm_t[...] = dm_ref[...].astype(F32).T.astype(BF)
        n2_t[...] = n2_ref[...].astype(F32).T.astype(BF)
        dn_ref[...] = jnp.zeros_like(dn_ref)

    for t in range(rows // TQ):
        part = pl.ds(t * TQ, TQ)
        d_act = dotf(dm_ref[part, :], down_ref[...], NT)
        d_pre = (slope_ref[part, :].astype(F32) * d_act).astype(BF)
        pre[part, :] = d_pre
        dn_ref[part, :] += dotf(d_pre, up_ref[...], NT)
    gu_ref[...] = dotf(n2_t[...], pre[...], NN).astype(BF)
    gd_ref[...] = dotf(dm_t[...], act_ref[...], NN).T.astype(BF)


def mlp_backward(d_mlp, n2, act, slope, w_mlp, wide=768):
    rows = n2.shape[0]
    whole = pl.BlockSpec((rows, D), lambda i: (0, 0))
    across = pl.BlockSpec((rows, wide), lambda i: (0, i))
    return pl.pallas_call(
        mlp_back_kernel,
        grid=(FF // wide,),
        in_specs=[whole, whole, across, across, up_spec(wide), down_spec(wide, FF // D)],
        out_specs=[up_spec(wide), down_spec(wide), whole],
        out_shape=[
            jax.ShapeDtypeStruct((D, FF), BF),
            jax.ShapeDtypeStruct((D, FF), BF),
            jax.ShapeDtypeStruct((rows, D), F32),
        ],
        scratch_shapes=[
            pltpu.VMEM((D, rows), BF),
            pltpu.VMEM((D, rows), BF),
            pltpu.VMEM((rows, wide), BF),
        ],
        compiler_params=pltpu.CompilerParams(vmem_limit_bytes=48 * 2**20),
        cost_estimate=pl.CostEstimate(
            flops=8 * rows * D * FF,
            bytes_accessed=4 * rows * FF + 8 * D * FF + 8 * rows * D,
            transcendentals=0,
        ),
        name="mlp_backward",
    )(d_mlp, n2, act, slope, w_mlp, w_mlp)


def norm_parts(rows):
    scale = lax.rsqrt(jnp.mean(rows * rows, axis=-1, keepdims=True) + EPS)
    return rows * scale, scale


def norm_back(d_out, unit, scale, gain):
    d_gain = jnp.sum(d_out * unit, axis=0)
    d_unit = d_out * gain
    d_rows = scale * (d_unit - unit * jnp.mean(d_unit * unit, axis=-1, keepdims=True))
    return d_rows, d_gain


def gelu_parts(pre):
    c = math.sqrt(2.0 / math.pi)
    sq = pre * pre
    t = jnp.tanh(c * pre * (1.0 + 0.044715 * sq))
    act = 0.5 * pre * (1.0 + t)
    slope = 0.5 * (1.0 + t) + 0.5 * pre * (1.0 - t * t) * (c * (1.0 + 3 * 0.044715 * sq))
    return act.astype(BF), slope.astype(BF)


def after(value, *others):
    return lax.optimization_barrier((value, *others))[0]


def forward_first(rows, gain_a, w_a):
    unit_a, _ = norm_parts(rows)
    n1 = (unit_a * gain_a).astype(BF)
    return n1, dotf(n1, w_a[:, D : 3 * D], NN).astype(BF)


def forward_second(rows, gain_b, w_a, o):
    branch = dotf(o, w_a[:, 3 * D : 4 * D], NN)
    mid = rows + branch
    unit_b, _ = norm_parts(mid)
    return branch, mid, (unit_b * gain_b).astype(BF)


def back_mlp(mid, weights, gain_b, saved, mlp_low, d_top, d_extra):
    o, n2, act, slope = saved
    w_a, w_mlp = weights
    g_up, g_down, d_n2 = mlp_backward(mlp_low, n2, act, slope, w_mlp)
    unit_b, scale_b = norm_parts(mid)
    d_mid, g_b = norm_back(d_n2, unit_b, scale_b, gain_b)
    if d_top is not None:
        d_mid = d_mid + d_top
    d_branch = (d_mid if d_extra is None else d_mid + d_extra).astype(BF)
    do = dotf(d_branch, w_a[:, 3 * D : 4 * D], NT).astype(BF)
    g_out = dotf(o, d_branch, TN).astype(BF)
    return d_mid, do, g_out, g_up, g_down, g_b


def back_qkv(rows, w_a, gain_a, n1, d_q, d_kv, d_mid):
    g_q = dotf(n1, d_q, TN).astype(BF)
    g_kv = dotf(n1, d_kv, TN).astype(BF)
    unit_a, scale_a = norm_parts(rows)
    d_n1 = dotf(d_q, w_a[:, :D], NT) + dotf(d_kv, w_a[:, D : 3 * D], NT)
    d_rows, g_a = norm_back(d_n1, unit_a, scale_a, gain_a)
    return d_rows + d_mid, g_q, g_kv, g_a


def ahead(value, axis, size, step):
    return lax.ppermute(value, axis, [(i, (i - step) % size) for i in range(size)])


def solution(mesh):
    dp, seq = mesh.shape["dp"], mesh.shape["seq"]
    y_n = dp // 2
    x_n = y_n if seq % y_n == 0 else 1
    z_n = seq // x_n
    half = seq // 2
    ways = dp * seq
    inner = Mesh(mesh.devices.reshape(y_n, 2, z_n, x_n), ("y", "core", "z", "x"))
    every = ("y", "core", "z", "x")
    home_axes = ("core", "z", "x")
    lb = LEN // seq

    def route(t):
        pairs = []
        for c in range(2):
            for s in range(seq):
                block = s // 2
                core = (s ^ block) & 1
                pairs.append((c * seq + s, core * seq + 2 * ((block + t) % half) + c))
        return pairs

    routes = [route(t) for t in range(half)]

    def swap_core(value):
        return lax.ppermute(value, "core", [(0, 1), (1, 0)])

    def all_sum(value):
        for axis, size in (("core", 2), ("x", x_n), ("y", y_n), ("z", z_n)):
            value = sum(
                (ahead(value, axis, size, s) for s in range(1, size)), start=value
            )
        return value

    def body(
        tokens, cotangent, picked_ids, lengths,
        qkv_w, out_w, up_w, down_w, vectors,
        qkv_mom, out_mom, up_mom, down_mom, vec_mom,
        qkv_avg, out_avg, up_avg, down_avg, vec_avg,
    ):
        y, core, z, x = (lax.axis_index(a) for a in every)
        chip = z * x_n + x
        seq_id = chip // 2
        group = chip % 2
        core_arr = jnp.full((1,), core, jnp.int32)
        piece = D // ways

        def grown(value, axis, size, place, dim):
            if size == 1:
                return jnp.expand_dims(value, dim)
            return placed(
                [value] + [ahead(value, axis, size, s) for s in range(1, size)], place, dim
            )

        def spread_z(shard):
            return grown(shard, "z", z_n, z, 0)

        def spread_x(value, x_first):
            return grown(value, "x", x_n, x, 1 if x_first else 2)

        def spread_y(value):
            return grown(value, "y", y_n, y, 0)

        def spread_core(value):
            value = grown(value, "core", 2, core, 1)
            return value.reshape(ways * value.shape[-2], value.shape[-1])

        def shard_a(layer):
            return jnp.concatenate(
                [qkv_w[layer].transpose(1, 0, 2).reshape(piece, 3 * D), out_w[layer]], axis=1
            ).astype(BF)

        def shard_mlp(layer):
            up = up_w[layer].astype(BF).reshape(piece, ways, 4, piece).swapaxes(1, 2)
            down = down_w[layer].astype(BF).reshape(4, piece, D).swapaxes(0, 1)
            return jnp.concatenate([up.reshape(piece, FF), down.reshape(piece, FF)], axis=1)

        def gather_mlp(shard):
            return lax.all_gather(shard, every, axis=0, tiled=True)

        def come(source):
            by_seq = source.transpose(1, 0, 2)
            got = []
            for t in range(half):
                sent = lax.dynamic_index_in_dim(by_seq, (chip // 2 + t) % half, 0, keepdims=False)
                got.append(lax.ppermute(sent, home_axes, routes[t]))
            return got

        def own_rows(got):
            return placed(got[:1] + got[:0:-1], seq_id, 0).reshape(half * lb, D)

        def leave(rows):
            got = []
            for t in range(half):
                sent = lax.dynamic_slice(rows, (((seq_id - t) % half) * lb, 0), (lb, D))
                got.append(lax.ppermute(sent, home_axes, [(b, a) for a, b in routes[t]]))
            return got

        def arrived(got):
            return placed(got, chip // 2, 0).transpose(1, 0, 2)

        gains_row = jnp.pad(vectors.T, ((0, 0), (0, 128 - 5))).astype(BF)
        mlp0 = gather_mlp(shard_mlp(0))
        chips_a = spread_z(jnp.concatenate([shard_a(0), gains_row], axis=1))
        chips_a = spread_x(chips_a, True)
        own_x = own_rows(come(tokens))
        next_a = after(shard_a(1), own_x)
        chips_b = spread_z(next_a)
        chips_a = after(spread_y(chips_a), own_x, chips_b)
        full_a = spread_core(chips_a)
        gains = full_a[:, 4 * D : 4 * D + 5].T.astype(F32)
        meta = jnp.concatenate([picked_ids, lengths[:, None]], axis=1)
        meta = lax.dynamic_index_in_dim(
            jnp.where(group == core, meta, swap_core(meta)), seq_id, 0, keepdims=False
        )
        picks, length = meta[:-1], meta[-1]
        row_ids = jnp.arange(half * lb, dtype=jnp.int32)
        block = row_ids // lb
        places = (2 * block + ((core + block) & 1)) * lb + row_ids % lb
        chosen = (picks[:, None] == places[None, :]).astype(BF)
        live = (places < length).astype(F32)[:, None]

        def at_picks(rows):
            part = dotf(chosen, rows, NN).astype(BF)
            return part + swap_core(part)

        def to_rows(values):
            return dotf(chosen, values, TN)

        mlp1 = gather_mlp(after(shard_mlp(1), full_a))
        x_low = at_picks(own_x)
        x_rows = x_low.astype(F32)
        gate = jax.nn.sigmoid(jnp.sum(x_rows * gains[2], axis=-1, keepdims=True))
        n1_0, kv0 = forward_first(x_rows, gains[0], full_a)
        q0 = dotf(n1_0, full_a[:, :D], NN).astype(BF)
        chips_b = spread_y(after(chips_b, x_low))
        own0 = ((q0, 0), (kv0, 0), (kv0, 6))
        o0, lse0 = attend(*own0, (), core_arr, lb)
        branch0, mid0, n2_0 = forward_second(x_rows, gains[1], full_a, o0)
        chips_b = spread_x(after(chips_b, q0), False)
        act0, slope0, out0 = mlp_forward(n2_0, mlp0)
        both0 = branch0 + out0
        delta = (gate * both0).astype(BF)
        mixed = own_x.astype(F32) + to_rows(delta)

        full_b = spread_core(after(chips_b, n2_0))
        cot_sent = come(after(cotangent, full_b))
        n1_1, kv1 = forward_first(mixed, gains[3], full_b)
        far = swap_core(kv1)
        far1 = ((far, 0), (far, 6))
        q1 = dotf(n1_1, full_b[:, :D], NN).astype(BF)
        own1 = ((q1, 0), (kv1, 0), (kv1, 6))
        o1, lse1 = attend(*own1, far1, core_arr, lb)
        branch1, mid1, n2_1 = forward_second(mixed, gains[4], full_b, o1)
        act1, slope1, out1 = mlp_forward(n2_1, mlp1)
        act_sent = leave((live * (mid1 + out1)).astype(BF))
        d_top = live * own_rows([after(c, o1) for c in cot_sent]).astype(F32)

        def by_shard(grad):
            return grad.reshape(y_n, 2, z_n, x_n, grad.shape[0] // ways, grad.shape[1])

        def at(grads, which, dim):
            return jnp.concatenate(
                [lax.dynamic_index_in_dim(g, which, dim, keepdims=False) for g in grads], axis=-1
            )

        def over_core(*grads):
            grads = [by_shard(g) for g in grads]
            got = swap_core(at(grads, 1 - core, 1))
            return (at(grads, core, 1).astype(F32) + got.astype(F32)).astype(BF)

        def of_core(*grads):
            return at([by_shard(g) for g in grads], core, 1)

        def over(value, axis, size, place, dim, kind=BF, late=()):
            total = at([value], place, dim).astype(F32)
            for s in range(1, size):
                sent = at([value], (place + size - s) % size, dim)
                total = total + after(ahead(sent, axis, size, s), *late).astype(F32)
            return total.astype(kind)

        def first_way(value, x_first):
            return over(value, "x", x_n, x, 2) if x_first else over(value, "y", y_n, y, 0)

        def second_way(value, x_first):
            return over(value, "y", y_n, y, 0) if x_first else over(value, "x", x_n, x, 1)

        def last_way(value, *late):
            return over(value, "z", z_n, z, 0, F32, late)

        def along(value, x_first):
            return last_way(second_way(first_way(value, x_first), x_first))

        def columns(*vectors):
            return jnp.pad(jnp.stack(vectors, 1), ((0, 0), (0, 128 - len(vectors)))).astype(BF)

        d_mid1, do1, g_out1, g_up1, g_down1, g_b1 = back_mlp(
            mid1, (full_b, mlp1), gains[4], (o1, n2_1, act1, slope1), d_top.astype(BF), d_top, None
        )
        up1, down1 = over_core(g_up1), over_core(g_down1)
        do1 = after(do1, up1, down1)
        up1, down1 = first_way(up1, False), first_way(down1, True)
        parts = []
        for first, count in ((0, 4), (4, 2)):
            dq, d_own, d_far = attend_back(
                own1[0], (do1, 0), (o1, 0), lse1, own1[1], own1[2], far1, core_arr, lb, first, count
            )
            parts.append((dq, d_own, swap_core(d_far)))
            up1, down1 = after(up1, dq), after(down1, dq)
            if first == 0:
                act_sent = [after(a, dq) for a in act_sent]
                do1 = after(do1, up1, down1, dq, *act_sent)
                up1, down1 = second_way(up1, False), second_way(down1, True)
        d_q1 = jnp.concatenate([parts[0][0], dq], axis=1)
        sums = [(d_own + back.astype(F32)).astype(BF) for _, d_own, back in parts]
        d_kv1 = jnp.concatenate([s[0] for s in sums] + [s[1] for s in sums], axis=1)
        d_mixed, g_q1, g_kv1, g_a1 = back_qkv(mixed, full_b, gains[3], n1_1, d_q1, d_kv1, d_mid1)
        head1 = over_core(g_q1, g_kv1, g_out1, columns(g_a1, g_b1))

        d_delta = at_picks(d_mixed.astype(BF)).astype(F32)
        gated = gate * d_delta
        d_logit = gate * (1.0 - gate) * jnp.sum(d_delta * both0, axis=-1, keepdims=True)
        activations = arrived([after(a, d_mixed) for a in act_sent])
        pair1 = jnp.concatenate([up1, down1], axis=-1)
        head1a = first_way(head1[..., : 2 * D], False)
        head1b = first_way(head1[..., 2 * D :], True)
        d_mid0, do0, g_out0, g_up0, g_down0, g_b0 = back_mlp(
            mid0, (full_a, mlp0), gains[1], (o0, n2_0, act0, slope0), gated.astype(BF), None, gated
        )
        up0, down0 = first_way(of_core(g_up0), False), first_way(of_core(g_down0), True)
        dq, d_kv = attend_back(
            own0[0], (do0, 0), (o0, 0), lse0, own0[1], own0[2], (), core_arr, lb, 0, PAIRS
        )
        head1a, head1b = second_way(after(head1a, dq), False), second_way(after(head1b, dq), True)
        d_kv0 = jnp.concatenate([d_kv[0], d_kv[1]], axis=1)
        d_rows0, g_q0, g_kv0, g_a0 = back_qkv(x_rows, full_a, gains[0], n1_0, dq, d_kv0, d_mid0)
        g_r = jnp.sum(d_logit * x_rows, axis=0)
        d_chosen = (d_rows0 + d_logit * gains[2]).astype(BF)
        grad_rows = (d_mixed + to_rows(d_chosen)).astype(BF)
        pair1 = last_way(pair1, grad_rows)
        grad_sent = leave(grad_rows)
        up0, down0 = second_way(up0, False), second_way(down0, True)
        head0a = after(of_core(g_q0, g_kv0[:, :D]), grad_rows, up0, down0)
        head0b = of_core(g_kv0[:, D:], g_out0, columns(g_a0, g_b0, g_r))
        head0b = after(head0b, grad_rows, up0, down0)
        early = jnp.concatenate([up0, down0, head1a, head1b], axis=-1)
        head0a, head0b = first_way(head0a, False), first_way(head0b, True)
        early = last_way(after(early, *grad_sent), head0a, head0b)
        head0a, head0b = second_way(head0a, False), second_way(head0b, True)
        head0 = last_way(after(jnp.concatenate([head0a, head0b], axis=-1), early))
        squares = sum(jnp.sum(v * v) for v in (early, head0, pair1))
        up0, down0, head1 = early[:, :FF], early[:, FF : 2 * FF], early[:, 2 * FF :]
        up1, down1 = pair1[:, :FF], pair1[:, FF:]
        input_grad = arrived(grad_sent).astype(F32)

        def unmixed(up):
            return up.reshape(piece, 4, ways, piece).swapaxes(1, 2).reshape(piece, FF)

        def unpacked(down):
            return down.reshape(piece, 4, D).swapaxes(0, 1).reshape(4 * piece, D)

        shards = [
            jnp.stack([h[:, : 3 * D].reshape(piece, 3, D).transpose(1, 0, 2) for h in (head0, head1)]),
            jnp.stack([head0[:, 3 * D : 4 * D], head1[:, 3 * D : 4 * D]]),
            jnp.stack([unmixed(up0), unmixed(up1)]),
            jnp.stack([unpacked(down0), unpacked(down1)]),
            jnp.concatenate([head0[:, 4 * D : 4 * D + 3].T, head1[:, 4 * D : 4 * D + 2].T]),
        ]
        grad_norm = jnp.sqrt(all_sum(squares.reshape(1, 1))[0, 0])
        factor = 1.0 / jnp.maximum(grad_norm, 1.0)
        base_rate = math.sqrt(NPARAMS / D)
        rates = (base_rate, math.sqrt(NPARAMS * LEN / (8 * D)), base_rate, base_rate, base_rate)
        masters = (qkv_w, out_w, up_w, down_w, vectors)
        moms = (qkv_mom, out_mom, up_mom, down_mom, vec_mom)
        avgs = (qkv_avg, out_avg, up_avg, down_avg, vec_avg)
        new_w, new_m, new_z = [], [], []
        for weight, grad, mom, avg, rate in zip(masters, shards, moms, avgs, rates):
            clipped = grad * factor
            m = 0.5 * mom + clipped
            w = weight - rate * (clipped + 0.5 * m)
            new_w.append(w)
            new_m.append(m)
            new_z.append(0.5 * avg + 0.5 * w)
        return (activations, input_grad, grad_norm, *new_w, *new_m, *new_z)

    group_spec = ("y", "core")
    pos_spec = ("z", "x")
    rows_spec = P(pos_spec, group_spec, None)
    param_specs = (
        P(None, None, every, None),
        P(None, every, None),
        P(None, every, None),
        P(None, every, None),
        P(None, every),
    )
    return jax.shard_map(
        body,
        mesh=inner,
        in_specs=(rows_spec, rows_spec, P(group_spec, None), P(group_spec)) + param_specs * 3,
        out_specs=(rows_spec, rows_spec, P()) + param_specs * 3,
        check_vma=False,
    )
```

time: 948 us -> 751 us (0.79); the launches traced: 931 us -> 745 us
  local copies, waits for them, and re-layouts: 188 us -> 103 us
  matrix products: 113 us -> 36 us
  Pallas kernels: 94.7 us -> 163 us
  waiting for transfers between devices: 312 us -> 263 us
  other arithmetic: 83.5 us -> 47.6 us
    dot_general x28 -> x22, matrix products: 113 us -> 36 us  [dotf(): return lax.dot_general(left, right, dims, preferred_element_type=F32)]
    pallas_call x0 -> x16, Pallas kernels: none -> 65.9 us  [the longest x2 37.1 us: mlp_backward(): pl.pallas_call(mlp_back_kernel, grid=(FF // wide,), in_specs=[whole, whol...]
    ppermute x51 -> x43, waiting for transfers between devices: 252 us -> 203 us  [ahead(): lax.ppermute(value, axis, [(i, (i - step) % size) for i in range(size)])]
    ppermute x8, waiting for transfers between devices: 49.2 us -> 13.3 us  [leave(): got.append(lax.ppermute(sent, home_axes, [(b, a) for a, b in routes[t]]))]
    ppermute x8, waiting for transfers between devices: 10.5 us -> 45.2 us  [come(): got.append(lax.ppermute(sent, home_axes, routes[t]))]
    unnamed x357 -> x260, local copies, waits for them, and re-layouts: 64.9 us -> 39.4 us
    reshape x8 -> x10, local copies, waits for them, and re-layouts: 29.4 us -> 8.58 us  [the longest x2 3.41 us: shard_mlp(): up.reshape(piece, FF)]
    squeeze x9 -> x33, local copies, waits for them, and re-layouts: 1.66 us -> 19.7 us  [the longest x28 19.3 us: at(): lax.dynamic_index_in_dim(g, which, dim, keepdims=False)]
  transfers between devices with their start and end apart: 76 -> 70, of which waited for: 29 -> 31; matrix products, arithmetic and copies ran while one was open for 29% -> 18% of each run, Pallas kernels for 7% -> 16%
where the time goes in v2:
time: 751 us; the launch traced here: 745 us
  waiting for transfers between devices  263 us (35%)
  Pallas kernels  163 us (22%)
  starting transfers between devices  107 us (14%)
  local copies, waits for them, and re-layouts  103 us (14%)
  other arithmetic  47.6 us (6%)
  matrix products  36 us (5%)
  between operations  24 us (3%)
    ppermute x43, waiting for transfers between devices, ahead(): lax.ppermute(value, axis, [(i, (i - step) % size) for i in range(size)])  203 us
    ppermute x43, starting transfers between devices, ahead(): lax.ppermute(value, axis, [(i, (i - step) % size) for i in range(size)])  73.8 us
    pallas_call x3, Pallas kernels, attend_back(): pl.pallas_call(functools.partial(attend_back_kernel, lb if far else 0, kc...  60 us
    ppermute x8, waiting for transfers between devices, come(): got.append(lax.ppermute(sent, home_axes, routes[t]))  45.2 us
    unnamed x260, local copies, waits for them, and re-layouts  39.4 us
    pallas_call x2, Pallas kernels, mlp_backward(): pl.pallas_call(mlp_back_kernel, grid=(FF // wide,), in_specs=[whole, whol...  37.1 us
    pallas_call x2, Pallas kernels, attend(): pl.pallas_call(functools.partial(attend_kernel, lb if far else 0), grid=(...  37 us
    dot_general x22, matrix products, dotf(): return lax.dot_general(left, right, dims, preferred_element_type=F32)  36 us
  transfers between devices with their start and end apart: 70, of which 31 were waited for; matrix products, arithmetic and copies ran while one was open for 18% of the time, Pallas kernels for 16%

profile of v2, /device:TPU:0, one launch (start us, length us, event | category | flops | bytes accessed | tf_op | source)
XLA Modules:
  0.0 744.6 jit_solution(3354290694277732776)
XLA Ops:
  13.7 5.1 collective-permute-start.6
  19.8 3.4 collective-permute-done.6
  23.2 13.3 %collective-permute-done.7 = bf16[24,3200]{1,0:T(8,128)(2,1)S(1)} collective-permute-done((bf16[24,3200]{1,0:T(8,128)(2,1)S(1)}, bf16[24,3200]{1,0:T(8,128)(2,1)S(1)}, u32[]{:S(2)}, u32[]{:S(2)}) %collective-permute-start.7) | collective-permute-done | bytes 153632 | tf_op jit(solution)/shard_map/ppermute | solution.py:394
  38.2 18.4 %collective-permute-done.9 = bf16[4,24,3200]{2,1,0:T(8,128)(2,1)S(1)} collective-permute-done((bf16[4,24,3200]{2,1,0:T(8,128)(2,1)S(1)}, bf16[4,24,3200]{2,1,0:T(8,128)(2,1)S(1)}, u32[]{:S(2)}, u32[]{:S(2)}) %collective-permute-start.9) | collective-permute-done | bytes 614432 | tf_op jit(solution)/shard_map/ppermute | solution.py:394
  58.4 6.4 constant_dynamic-slice_fusion.14
  68.0 3.5 collective-permute-start.3
  71.5 7.9 %collective-permute-done.4 = bf16[256,768]{1,0:T(8,128)(2,1)S(1)} collective-permute-done((bf16[256,768]{1,0:T(8,128)(2,1)S(1)}, bf16[256,768]{1,0:T(8,128)(2,1)S(1)}, u32[]{:S(2)}, u32[]{:S(2)}) %collective-permute-start.4) | collective-permute-done | bytes 393248 | tf_op jit(solution)/shard_map/ppermute | solution.py:481
  79.4 20.6 %collective-permute-done.2 = bf16[256,768]{1,0:T(8,128)(2,1)S(1)} collective-permute-done((bf16[256,768]{1,0:T(8,128)(2,1)S(1)}, bf16[256,768]{1,0:T(8,128)(2,1)S(1)}, u32[]{:S(2)}, u32[]{:S(2)}) %collective-permute-start.2) | collective-permute-done | bytes 393248 | tf_op jit(solution)/shard_map/ppermute | solution.py:481
  100.0 16.7 %collective-permute-done.3 = bf16[256,768]{1,0:T(8,128)(2,1)S(1)} collective-permute-done((bf16[256,768]{1,0:T(8,128)(2,1)S(1)}, bf16[256,768]{1,0:T(8,128)(2,1)S(1)}, u32[]{:S(2)}, u32[]{:S(2)}) %collective-permute-start.3) | collective-permute-done | bytes 393248 | tf_op jit(solution)/shard_map/ppermute | solution.py:481
  117.9 18.2 %collective-permute-start.11 = (bf16[24,3072]{1,0:T(8,128)(2,1)S(1)}, bf16[24,3072]{1,0:T(8,128)(2,1)S(1)}, u32[]{:S(2)}, u32[]{:S(2)}) collective-permute-start(bf16[24,3072]{1,0:T(8,128)(2,1)S(1)} %pad_maximum_fusion.13), channel_id=1, source_target_pairs={{0,6},{2,0},{4,2},{6,4},{1,7},{3,1},{5,3},{7,5},{8,14},{10,8},{12,... | collective-permute-start | bytes 442376 | tf_op jit(solution)/shard_map/ppermute | solution.py:394
  138.8 6.6 collective-permute-done.12
  172.1 15.0 %collective-permute-done.15 = bf16[4,24,3072]{2,1,0:T(8,128)(2,1)S(1)} collective-permute-done((bf16[4,24,3072]{2,1,0:T(8,128)(2,1)S(1)}, bf16[4,24,3072]{2,1,0:T(8,128)(2,1)S(1)}, u32[]{:S(2)}, u32[]{:S(2)}) %collective-permute-start.15) | collective-permute-done | bytes 589856 | tf_op jit(solution)/shard_map/ppermute | solution.py:394
  187.1 3.3 collective-permute-start.16
  191.3 5.5 attend_own.1
  197.6 28.7 %collective-permute-done.16 = bf16[2,4,24,3072]{3,2,1,0:T(8,128)(2,1)S(1)} collective-permute-done((bf16[2,4,24,3072]{3,2,1,0:T(8,128)(2,1)S(1)}, bf16[2,4,24,3072]{3,2,1,0:T(8,128)(2,1)S(1)}, u32[]{:S(2)}, u32[]{:S(2)}) %collective-permute-start.16) | collective-permute-done | bytes 1179680 | tf_op jit(solution)/shard_map/ppermute | solution.py:394
  226.7 4.5 collective-permute-done.17
  234.1 3.7 copy-done
  237.8 5.8 mlp_forward.2
  248.3 4.1 convolution_convert_fusion.refs_1_.refs_2_.refs_4_.refs_5_
  255.1 3.4 collective-permute-start.21
  262.0 31.5 %attend_far.1 = (bf16[1024,768]{1,0:T(8,128)(2,1)S(1)}, f32[6,2,1024]{2,1,0:T(2,128)S(1)}) custom-call(s32[1]{0:T(128)} %bitcast.13.start_ref.core_ref, bf16[1024,768]{1,0:T(8,128)(2,1)S(1)} %convolution_convert_fusion.5.refs_0_, bf16[1024,1536]{1,0:T(8,128)(2,1)} %convolution_convert_fusion.refs_1_.refs_2_.refs_4_.refs_5_, ...), custom_call_target="tpu_custom_call" | custom-call | flops 19327352832 | bytes 9437184 | tf_op jit(solution)/shard_map/attend_far/pallas_call | solution.py:93
  304.0 18.2 %mlp_forward.3 = (bf16[1024,3072]{1,0:T(8,128)(2,1)S(1)}, bf16[1024,3072]{1,0:T(8,128)(2,1)}, f32[1024,768]{1,0:T(8,128)S(1)}) custom-call(bf16[1024,768]{1,0:T(8,128)(2,1)S(1)} %copy-done.13, bf16[768,6144]{1,0:T(8,128)(2,1)} %all-gather.5.cloned.1.call-done.up_ref.down_ref, bf16[768,6144]{1,0:T(8,128)(2,1)} %all-gather.5.cloned.1.call-done.up_ref.down_ref), custom_call_target="tpu_custom_call" | custom-call | flops 9663676416 | bytes 26738688 | tf_op jit(solution)/shard_map/mlp_forward/pallas_call | solution.py:262
  324.9 26.7 %mlp_backward.2 = (bf16[768,3072]{1,0:T(8,128)(2,1)}, bf16[768,3072]{1,0:T(8,128)(2,1)}, f32[1024,768]{1,0:T(8,128)}) custom-call(bf16[1024,768]{1,0:T(8,128)(2,1)S(1)} %copy-done.12, bf16[1024,768]{1,0:T(8,128)(2,1)S(1)} %copy-done.14, bf16[1024,3072]{1,0:T(8,128)(2,1)} %copy-done.31, bf16[1024,3072]{1,0:T(8,128)(2,1)} %get-tuple-element.95.slope_ref, ...), custom_call_target="tpu_custom_call" | custom-call | flops 19327352832 | bytes 37748736 | tf_op jit(solution)/shard_map/mlp_backward/pallas_call | solution.py:307
  354.6 3.9 collective-permute-start.25
  366.5 3.1 collective-permute-start.28
  377.0 3.8 collective-permute-start.27
  383.1 36.1 %attend_back_far.2 = (bf16[1024,512]{1,0:T(8,128)(2,1)S(1)}, f32[2,1024,512]{2,1,0:T(8,128)}, bf16[2,1024,512]{2,1,0:T(8,128)(2,1)}) custom-call(s32[1]{0:T(128)} %bitcast.13.start_ref.core_ref, bf16[1024,768]{1,0:T(8,128)(2,1)S(1)} %copy-done.30, bf16[1024,768]{1,0:T(8,128)(2,1)S(1)} %convolution_convert_fusion.4.refs_1_, bf16[1024,768]{1,0:T(8,128)(2,1)S(1)} %copy-done.16, ...), custom_call_target="tpu_custom_call" | custom-call | flops 26843545600 | bytes 18874368 | tf_op jit(solution)/shard_map/attend_back_far/pallas_call | solution.py:185
  425.7 24.0 %collective-permute-done.26 = bf16[4,2,24,3072]{3,2,0,1:T(8,128)(2,1)S(1)} collective-permute-done((bf16[4,2,24,3072]{3,2,0,1:T(8,128)(2,1)S(1)}, bf16[4,2,24,3072]{3,2,0,1:T(8,128)(2,1)S(1)}, u32[]{:S(2)}, u32[]{:S(2)}) %collective-permute-start.26) | collective-permute-done | bytes 1179680 | tf_op jit(solution)/shard_map/ppermute | solution.py:394
  451.0 18.5 %attend_back_far.3 = (bf16[1024,256]{1,0:T(8,128)(2,1)S(1)}, f32[2,1024,256]{2,1,0:T(8,128)S(1)}, bf16[2,1024,256]{2,1,0:T(8,128)(2,1)S(1)}) custom-call(s32[1]{0:T(128)} %bitcast.13.start_ref.core_ref, bf16[1024,768]{1,0:T(8,128)(2,1)S(1)} %copy-done.30, bf16[1024,768]{1,0:T(8,128)(2,1)S(1)} %copy-done.28, bf16[1024,768]{1,0:T(8,128)(2,1)S(1)} %copy-done.16, ...), custom_call_target="tpu_custom_call" | custom-call | flops 13421772800 | bytes 18874368 | tf_op jit(solution)/shard_map/attend_back_far/pallas_call | solution.py:185
  486.0 3.7 convolution_convert_fusion.1
  498.8 3.3 pad_maximum_fusion.1
  506.2 10.4 %mlp_backward.3 = (bf16[768,3072]{1,0:T(8,128)(2,1)}, bf16[768,3072]{1,0:T(8,128)(2,1)}, f32[256,768]{1,0:T(8,128)S(1)}) custom-call(bf16[256,768]{1,0:T(8,128)(2,1)S(1)} %fusion.54.dm_ref, bf16[256,768]{1,0:T(8,128)(2,1)S(1)} %copy-done.9, bf16[256,3072]{1,0:T(8,128)(2,1)S(1)} %get-tuple-element.118.act_ref, bf16[256,3072]{1,0:T(8,128)(2,1)S(1)} %copy-done.11, ...), custom_call_target="tpu_custom_call" | custom-call | flops 4831838208 | bytes 23592960 | tf_op jit(solution)/shard_map/mlp_backward/pallas_call | solution.py:307
  520.0 5.4 attend_back_own.1
  554.6 4.1 stack_reshape.13
  558.8 6.4 collective-permute-done.38
  569.1 3.1 collective-permute-done.40
  572.2 4.9 collective-permute-start.37
  581.4 13.3 %collective-permute-done.36 = bf16[256,768]{1,0:T(8,128)(2,1)S(1)} collective-permute-done((bf16[256,768]{1,0:T(8,128)(2,1)S(1)}, bf16[256,768]{1,0:T(8,128)(2,1)S(1)}, u32[]{:S(2)}, u32[]{:S(2)}) %collective-permute-start.36) | collective-permute-done | bytes 393248 | tf_op jit(solution)/shard_map/ppermute | solution.py:491
  595.1 3.7 copy.349
  608.7 9.5 %collective-permute-done.48 = bf16[4,2,24,1536]{3,2,1,0:T(8,128)(2,1)S(1)} collective-permute-done((bf16[4,2,24,1536]{3,2,1,0:T(8,128)(2,1)S(1)}, bf16[4,2,24,1536]{3,2,1,0:T(8,128)(2,1)S(1)}, u32[]{:S(2)}, u32[]{:S(2)}) %collective-permute-start.48) | collective-permute-done | bytes 589856 | tf_op jit(solution)/shard_map/ppermute | solution.py:394
  621.7 9.1 %collective-permute-done.43 = bf16[4,2,24,1536]{3,2,1,0:T(8,128)(2,1)S(1)} collective-permute-done((bf16[4,2,24,1536]{3,2,1,0:T(8,128)(2,1)S(1)}, bf16[4,2,24,1536]{3,2,1,0:T(8,128)(2,1)S(1)}, u32[]{:S(2)}, u32[]{:S(2)}) %collective-permute-start.43) | collective-permute-done | bytes 589856 | tf_op jit(solution)/shard_map/ppermute | solution.py:394
  632.1 8.4 %collective-permute-done.52 = bf16[4,24,1536]{2,1,0:T(8,128)(2,1)S(1)} collective-permute-done((bf16[4,24,1536]{2,1,0:T(8,128)(2,1)S(1)}, bf16[4,24,1536]{2,1,0:T(8,128)(2,1)S(1)}, u32[]{:S(2)}, u32[]{:S(2)}) %collective-permute-start.52) | collective-permute-done | bytes 294944 | tf_op jit(solution)/shard_map/ppermute | solution.py:394
  641.9 3.8 collective-permute-done.44
  650.9 9.0 %collective-permute-done.47 = bf16[24,9344]{1,0:T(8,128)(2,1)S(1)} collective-permute-done((bf16[24,9344]{1,0:T(8,128)(2,1)S(1)}, bf16[24,9344]{1,0:T(8,128)(2,1)S(1)}, u32[]{:S(2)}, u32[]{:S(2)}) %collective-permute-start.47) | collective-permute-done | bytes 448544 | tf_op jit(solution)/shard_map/ppermute | solution.py:394
  660.0 24.9 %collective-permute-done.50 = bf16[24,9344]{1,0:T(8,128)(2,1)S(1)} collective-permute-done((bf16[24,9344]{1,0:T(8,128)(2,1)S(1)}, bf16[24,9344]{1,0:T(8,128)(2,1)S(1)}, u32[]{:S(2)}, u32[]{:S(2)}) %collective-permute-start.50) | collective-permute-done | bytes 448544 | tf_op jit(solution)/shard_map/ppermute | solution.py:394
  688.1 3.2 collective-permute-start.55
  700.7 4.1 collective-permute-done.55
  722.0 3.0 collective-permute-start.67
  (565 shorter events, 227.4 us)
Async XLA Ops:
  7.2 226.9 %all-gather.3.cloned.1.call-start = ((), (), s32[]{:S(2)}) async-start(), calls=%async_computation | async-start | bytes 9732096 | tf_op jit(solution)/shard_map/all_gather | solution.py:474
  13.4 289.3 %all-gather.5.cloned.1.call-start = ((), (), s32[]{:S(2)}) async-start(), calls=%async_computation.1 | async-start | bytes 9732096 | tf_op jit(solution)/shard_map/all_gather | solution.py:474
  18.8 17.7 %collective-permute-start.7 = (bf16[24,3200]{1,0:T(8,128)(2,1)S(1)}, bf16[24,3200]{1,0:T(8,128)(2,1)S(1)}, u32[]{:S(2)}, u32[]{:S(2)}) collective-permute-start(bf16[24,3200]{1,0:T(8,128)(2,1)S(1)} %get-tuple-element.363), channel_id=1, source_target_pairs={{0,4},{2,6},{4,0},{6,2},{1,5},{3,7},{5,1},{7,3},{8,12},{10,14},{12... | collective-permute-start | bytes 460808 | tf_op jit(solution)/shard_map/ppermute | solution.py:394
  18.8 17.7 %collective-permute-start.8 = (bf16[24,3200]{1,0:T(8,128)(2,1)S(1)}, bf16[24,3200]{1,0:T(8,128)(2,1)S(1)}, u32[]{:S(2)}, u32[]{:S(2)}) collective-permute-start(bf16[24,3200]{1,0:T(8,128)(2,1)S(1)} %get-tuple-element.363), channel_id=1, source_target_pairs={{0,2},{2,4},{4,6},{6,0},{1,3},{3,5},{5,7},{7,1},{8,10},{10,12},{12... | collective-permute-start | bytes 460808 | tf_op jit(solution)/shard_map/ppermute | solution.py:394
  36.5 20.1 %collective-permute-start.9 = (bf16[4,24,3200]{2,1,0:T(8,128)(2,1)S(1)}, bf16[4,24,3200]{2,1,0:T(8,128)(2,1)S(1)}, u32[]{:S(2)}, u32[]{:S(2)}) collective-permute-start(bf16[4,24,3200]{2,1,0:T(8,128)(2,1)S(1)} %bitcast.382), channel_id=1, source_target_pairs={{0,1},{1,0},{2,3},{3,2},{4,5},{5,4},{6,7},{7,6},{8,9},{9,8},{10,11... | collective-permute-start | bytes 1843208 | tf_op jit(solution)/shard_map/ppermute | solution.py:394
  56.8 90.2 %collective-permute-start.10 = (bf16[4,2,24,3200]{3,2,1,0:T(8,128)(2,1)S(1)}, bf16[4,2,24,3200]{3,2,1,0:T(8,128)(2,1)S(1)}, u32[]{:S(2)}, u32[]{:S(2)}) collective-permute-start(bf16[4,2,24,3200]{3,2,1,0:T(8,128)(2,1)S(1)} %bitcast.378), channel_id=1, source_target_pairs={{0,16},{16,0},{1,17},{17,1},{2,18},{18,2},{3,19},{19,3},{4,20},{20... | collective-permute-start | bytes 3686408 | tf_op jit(solution)/shard_map/ppermute | solution.py:394
  67.9 32.1 %collective-permute-start.2 = (bf16[256,768]{1,0:T(8,128)(2,1)S(1)}, bf16[256,768]{1,0:T(8,128)(2,1)S(1)}, u32[]{:S(2)}, u32[]{:S(2)}) collective-permute-start(bf16[256,768]{1,0:T(8,128)(2,1)S(1)} %bitcast.455), channel_id=1, source_target_pairs={{0,6},{1,14},{2,8},{3,0},{4,2},{5,10},{6,12},{7,4},{8,7},{9,15},{1... | collective-permute-start | bytes 1179656 | tf_op jit(solution)/shard_map/ppermute | solution.py:481
  68.0 48.7 %collective-permute-start.3 = (bf16[256,768]{1,0:T(8,128)(2,1)S(1)}, bf16[256,768]{1,0:T(8,128)(2,1)S(1)}, u32[]{:S(2)}, u32[]{:S(2)}) collective-permute-start(bf16[256,768]{1,0:T(8,128)(2,1)S(1)} %bitcast.456), channel_id=1, source_target_pairs={{0,4},{1,12},{2,14},{3,6},{4,0},{5,8},{6,10},{7,2},{8,5},{9,13},{1... | collective-permute-start | bytes 1179656 | tf_op jit(solution)/shard_map/ppermute | solution.py:481
  117.9 20.9 %collective-permute-start.11 = (bf16[24,3072]{1,0:T(8,128)(2,1)S(1)}, bf16[24,3072]{1,0:T(8,128)(2,1)S(1)}, u32[]{:S(2)}, u32[]{:S(2)}) collective-permute-start(bf16[24,3072]{1,0:T(8,128)(2,1)S(1)} %pad_maximum_fusion.13), channel_id=1, source_target_pairs={{0,6},{2,0},{4,2},{6,4},{1,7},{3,1},{5,3},{7,5},{8,14},{10,8},{12,... | collective-permute-start | bytes 442376 | tf_op jit(solution)/shard_map/ppermute | solution.py:394
  169.5 17.6 %collective-permute-start.15 = (bf16[4,24,3072]{2,1,0:T(8,128)(2,1)S(1)}, bf16[4,24,3072]{2,1,0:T(8,128)(2,1)S(1)}, u32[]{:S(2)}, u32[]{:S(2)}) collective-permute-start(bf16[4,24,3072]{2,1,0:T(8,128)(2,1)S(1)} %bitcast.384), channel_id=1, source_target_pairs={{0,16},{16,0},{1,17},{17,1},{2,18},{18,2},{3,19},{19,3},{4,20},{20... | collective-permute-start | bytes 1769480 | tf_op jit(solution)/shard_map/ppermute | solution.py:394
  187.1 39.1 %collective-permute-start.16 = (bf16[2,4,24,3072]{3,2,1,0:T(8,128)(2,1)S(1)}, bf16[2,4,24,3072]{3,2,1,0:T(8,128)(2,1)S(1)}, u32[]{:S(2)}, u32[]{:S(2)}) collective-permute-start(bf16[2,4,24,3072]{3,2,1,0:T(8,128)(2,1)S(1)} %bitcast.380), channel_id=1, source_target_pairs={{0,1},{1,0},{2,3},{3,2},{4,5},{5,4},{6,7},{7,6},{8,9},{9,8},{10,11... | collective-permute-start | bytes 3538952 | tf_op jit(solution)/shard_map/ppermute | solution.py:394
  254.0 39.5 %collective-permute-start.23 = (bf16[256,768]{1,0:T(8,128)(2,1)S(1)}, bf16[256,768]{1,0:T(8,128)(2,1)S(1)}, u32[]{:S(2)}, u32[]{:S(2)}) collective-permute-start(bf16[256,768]{1,0:T(8,128)(2,1)S(1)} %get-tuple-element.327), channel_id=1, source_target_pairs={{0,2},{1,10},{2,12},{3,4},{4,6},{5,14},{6,8},{7,0},{8,3},{9,11},{1... | collective-permute-start | bytes 1179656 | tf_op jit(solution)/shard_map/ppermute | solution.py:481
  254.1 39.5 %collective-permute-start.22 = (bf16[256,768]{1,0:T(8,128)(2,1)S(1)}, bf16[256,768]{1,0:T(8,128)(2,1)S(1)}, u32[]{:S(2)}, u32[]{:S(2)}) collective-permute-start(bf16[256,768]{1,0:T(8,128)(2,1)S(1)} %get-tuple-element.328), channel_id=1, source_target_pairs={{0,4},{1,12},{2,14},{3,6},{4,0},{5,8},{6,10},{7,2},{8,5},{9,13},{1... | collective-permute-start | bytes 1179656 | tf_op jit(solution)/shard_map/ppermute | solution.py:481
  255.1 38.5 %collective-permute-start.21 = (bf16[256,768]{1,0:T(8,128)(2,1)S(1)}, bf16[256,768]{1,0:T(8,128)(2,1)S(1)}, u32[]{:S(2)}, u32[]{:S(2)}) collective-permute-start(bf16[256,768]{1,0:T(8,128)(2,1)S(1)} %get-tuple-element.329), channel_id=1, source_target_pairs={{0,6},{1,14},{2,8},{3,0},{4,2},{5,10},{6,12},{7,4},{8,7},{9,15},{1... | collective-permute-start | bytes 1179656 | tf_op jit(solution)/shard_map/ppermute | solution.py:481
  258.5 35.1 %collective-permute-start.20 = (bf16[256,768]{1,0:T(8,128)(2,1)S(1)}, bf16[256,768]{1,0:T(8,128)(2,1)S(1)}, u32[]{:S(2)}, u32[]{:S(2)}) collective-permute-start(bf16[256,768]{1,0:T(8,128)(2,1)S(1)} %get-tuple-element.330), channel_id=1, source_target_pairs={{0,0},{1,8},{2,10},{3,2},{4,4},{5,12},{6,14},{7,6},{8,1},{9,9},{10... | collective-permute-start | bytes 1179656 | tf_op jit(solution)/shard_map/ppermute | solution.py:481
  354.6 19.1 %collective-permute-start.25 = (bf16[2,4,2,24,3072]{4,3,1,0,2:T(8,128)(2,1)S(1)}, bf16[2,4,2,24,3072]{4,3,1,0,2:T(8,128)(2,1)S(1)}, u32[]{:S(2)}, u32[]{:S(2)}) collective-permute-start(bf16[2,4,2,24,3072]{4,3,1,0,2:T(8,128)(2,1)S(1)} %bitcast.428), channel_id=1, source_target_pairs={{0,8},{8,0},{1,9},{9,1},{2,10},{10,2},{3,11},{11,3},{4,12},{12,4},... | collective-permute-start | bytes 7077896 | tf_op jit(solution)/shard_map/ppermute | solution.py:421
  359.2 17.8 %collective-permute-start.24 = (bf16[2,4,2,24,3072]{4,3,1,2,0:T(8,128)(2,1)S(1)}, bf16[2,4,2,24,3072]{4,3,1,2,0:T(8,128)(2,1)S(1)}, u32[]{:S(2)}, u32[]{:S(2)}) collective-permute-start(bf16[2,4,2,24,3072]{4,3,1,2,0:T(8,128)(2,1)S(1)} %bitcast.427), channel_id=1, source_target_pairs={{0,8},{8,0},{1,9},{9,1},{2,10},{10,2},{3,11},{11,3},{4,12},{12,4},... | collective-permute-start | bytes 7077896 | tf_op jit(solution)/shard_map/ppermute | solution.py:421
  364.8 54.5 %collective-permute-start.30 = (bf16[256,768]{1,0:T(8,128)(2,1)}, bf16[256,768]{1,0:T(8,128)(2,1)S(1)}, u32[]{:S(2)}, u32[]{:S(2)}) collective-permute-start(bf16[256,768]{1,0:T(8,128)(2,1)} %get-tuple-element.323), channel_id=1, source_target_pairs={{6,0},{14,1},{8,2},{0,3},{2,4},{10,5},{12,6},{4,7},{7,8},{15,9},{9... | collective-permute-start | bytes 1179656 | tf_op jit(solution)/shard_map/ppermute | solution.py:491
  365.7 53.5 %collective-permute-start.29 = (bf16[256,768]{1,0:T(8,128)(2,1)S(1)}, bf16[256,768]{1,0:T(8,128)(2,1)S(1)}, u32[]{:S(2)}, u32[]{:S(2)}) collective-permute-start(bf16[256,768]{1,0:T(8,128)(2,1)S(1)} %get-tuple-element.324), channel_id=1, source_target_pairs={{4,0},{12,1},{14,2},{6,3},{0,4},{8,5},{10,6},{2,7},{5,8},{13,9},{1... | collective-permute-start | bytes 1179656 | tf_op jit(solution)/shard_map/ppermute | solution.py:491
  366.5 52.7 %collective-permute-start.28 = (bf16[256,768]{1,0:T(8,128)(2,1)S(1)}, bf16[256,768]{1,0:T(8,128)(2,1)S(1)}, u32[]{:S(2)}, u32[]{:S(2)}) collective-permute-start(bf16[256,768]{1,0:T(8,128)(2,1)S(1)} %get-tuple-element.325), channel_id=1, source_target_pairs={{2,0},{10,1},{12,2},{4,3},{6,4},{14,5},{8,6},{0,7},{3,8},{11,9},{1... | collective-permute-start | bytes 1179656 | tf_op jit(solution)/shard_map/ppermute | solution.py:491
  373.7 47.1 %collective-permute-start.19 = (bf16[256,768]{1,0:T(8,128)(2,1)S(1)}, bf16[256,768]{1,0:T(8,128)(2,1)S(1)}, u32[]{:S(2)}, u32[]{:S(2)}) collective-permute-start(bf16[256,768]{1,0:T(8,128)(2,1)S(1)} %get-tuple-element.326), channel_id=1, source_target_pairs={{0,0},{8,1},{10,2},{2,3},{4,4},{12,5},{14,6},{6,7},{1,8},{9,9},{11... | collective-permute-start | bytes 1179656 | tf_op jit(solution)/shard_map/ppermute | solution.py:491
  377.0 44.0 %collective-permute-start.27 = (bf16[2,4,24,3072]{3,2,1,0:T(8,128)(2,1)}, bf16[2,4,24,3072]{3,2,1,0:T(8,128)(2,1)}, u32[]{:S(2)}, u32[]{:S(2)}) collective-permute-start(bf16[2,4,24,3072]{3,2,1,0:T(8,128)(2,1)} %dynamic-slice_bitcast_fusion.4), channel_id=1, source_target_pairs={{0,1},{1,0},{2,3},{3,2},{4,5},{5,4},{6,7},{7,6},{8,9},{9,8},{10,11... | collective-permute-start | bytes 3538952 | tf_op jit(solution)/shard_map/ppermute | solution.py:394
  420.8 29.0 %collective-permute-start.26 = (bf16[4,2,24,3072]{3,2,0,1:T(8,128)(2,1)S(1)}, bf16[4,2,24,3072]{3,2,0,1:T(8,128)(2,1)S(1)}, u32[]{:S(2)}, u32[]{:S(2)}) collective-permute-start(bf16[4,2,24,3072]{3,2,0,1:T(8,128)(2,1)S(1)} %dynamic-slice_bitcast_fusion.5), channel_id=1, source_target_pairs={{0,16},{16,0},{1,17},{17,1},{2,18},{18,2},{3,19},{19,3},{4,20},{20... | collective-permute-start | bytes 3538952 | tf_op jit(solution)/shard_map/ppermute | solution.py:394
  420.8 59.7 %collective-permute-start.31 = (bf16[2,1024,512]{2,1,0:T(8,128)(2,1)}, bf16[2,1024,512]{2,1,0:T(8,128)(2,1)}, u32[]{:S(2)}, u32[]{:S(2)}) collective-permute-start(bf16[2,1024,512]{2,1,0:T(8,128)(2,1)} %get-tuple-element.111), channel_id=1, source_target_pairs={{0,8},{8,0},{1,9},{9,1},{2,10},{10,2},{3,11},{11,3},{4,12},{12,4},... | collective-permute-start | bytes 6291464 | tf_op jit(solution)/shard_map/ppermute | solution.py:421
  423.9 49.7 %collective-permute-start.58 = (bf16[4,24,3072]{2,1,0:T(8,128)(2,1)}, bf16[4,24,3072]{2,1,0:T(8,128)(2,1)}, u32[]{:S(2)}, u32[]{:S(2)}) collective-permute-start(bf16[4,24,3072]{2,1,0:T(8,128)(2,1)} %dynamic-slice_bitcast_fusion.8), channel_id=1, source_target_pairs={{0,16},{16,0},{1,17},{17,1},{2,18},{18,2},{3,19},{19,3},{4,20},{20... | collective-permute-start | bytes 1769480 | tf_op jit(solution)/shard_map/ppermute | solution.py:394
  451.0 23.8 %collective-permute-start.57 = (bf16[4,24,3072]{2,1,0:T(8,128)(2,1)}, bf16[4,24,3072]{2,1,0:T(8,128)(2,1)}, u32[]{:S(2)}, u32[]{:S(2)}) collective-permute-start(bf16[4,24,3072]{2,1,0:T(8,128)(2,1)} %dynamic-slice_bitcast_fusion.9), channel_id=1, source_target_pairs={{0,1},{1,0},{2,3},{3,2},{4,5},{5,4},{6,7},{7,6},{8,9},{9,8},{10,11... | collective-permute-start | bytes 1769480 | tf_op jit(solution)/shard_map/ppermute | solution.py:394
  477.4 54.4 %collective-permute-start.59 = (bf16[24,6144]{1,0:T(8,128)(2,1)}, bf16[24,6144]{1,0:T(8,128)(2,1)}, u32[]{:S(2)}, u32[]{:S(2)}) collective-permute-start(bf16[24,6144]{1,0:T(8,128)(2,1)} %get-tuple-element.335), channel_id=1, source_target_pairs={{0,6},{2,0},{4,2},{6,4},{1,7},{3,1},{5,3},{7,5},{8,14},{10,8},{12,... | collective-permute-start | bytes 884744 | tf_op jit(solution)/shard_map/ppermute | solution.py:394
  478.0 53.8 %collective-permute-start.60 = (bf16[24,6144]{1,0:T(8,128)(2,1)}, bf16[24,6144]{1,0:T(8,128)(2,1)}, u32[]{:S(2)}, u32[]{:S(2)}) collective-permute-start(bf16[24,6144]{1,0:T(8,128)(2,1)} %get-tuple-element.337), channel_id=1, source_target_pairs={{0,4},{2,6},{4,0},{6,2},{1,5},{3,7},{5,1},{7,3},{8,12},{10,14},{12... | collective-permute-start | bytes 884744 | tf_op jit(solution)/shard_map/ppermute | solution.py:394
  478.7 54.0 %collective-permute-start.61 = (bf16[24,6144]{1,0:T(8,128)(2,1)}, bf16[24,6144]{1,0:T(8,128)(2,1)}, u32[]{:S(2)}, u32[]{:S(2)}) collective-permute-start(bf16[24,6144]{1,0:T(8,128)(2,1)} %get-tuple-element.336), channel_id=1, source_target_pairs={{0,2},{2,4},{4,6},{6,0},{1,3},{3,5},{5,7},{7,1},{8,10},{10,12},{12... | collective-permute-start | bytes 884744 | tf_op jit(solution)/shard_map/ppermute | solution.py:394
  502.1 102.3 %collective-permute-start.42 = (bf16[2,4,2,24,3200]{4,3,2,1,0:T(8,128)(2,1)}, bf16[2,4,2,24,3200]{4,3,2,1,0:T(8,128)(2,1)}, u32[]{:S(2)}, u32[]{:S(2)}) collective-permute-start(bf16[2,4,2,24,3200]{4,3,2,1,0:T(8,128)(2,1)} %pad_maximum_fusion.1), channel_id=1, source_target_pairs={{0,8},{8,0},{1,9},{9,1},{2,10},{10,2},{3,11},{11,3},{4,12},{12,4},... | collective-permute-start | bytes 7372808 | tf_op jit(solution)/shard_map/ppermute | solution.py:421
  536.9 28.3 %collective-permute-start.38 = (bf16[4,2,24,3072]{3,2,1,0:T(8,128)(2,1)}, bf16[4,2,24,3072]{3,2,1,0:T(8,128)(2,1)}, u32[]{:S(2)}, u32[]{:S(2)}) collective-permute-start(bf16[4,2,24,3072]{3,2,1,0:T(8,128)(2,1)} %dynamic-slice_bitcast_fusion.3), channel_id=1, source_target_pairs={{0,16},{16,0},{1,17},{17,1},{2,18},{18,2},{3,19},{19,3},{4,20},{20... | collective-permute-start | bytes 3538952 | tf_op jit(solution)/shard_map/ppermute | solution.py:394
  539.3 32.9 %collective-permute-start.40 = (bf16[2,4,24,3072]{3,2,1,0:T(8,128)(2,1)}, bf16[2,4,24,3072]{3,2,1,0:T(8,128)(2,1)}, u32[]{:S(2)}, u32[]{:S(2)}) collective-permute-start(bf16[2,4,24,3072]{3,2,1,0:T(8,128)(2,1)} %dynamic-slice_bitcast_fusion.2), channel_id=1, source_target_pairs={{0,1},{1,0},{2,3},{3,2},{4,5},{5,4},{6,7},{7,6},{8,9},{9,8},{10,11... | collective-permute-start | bytes 3538952 | tf_op jit(solution)/shard_map/ppermute | solution.py:394
  542.5 36.9 %collective-permute-start.34 = (bf16[256,768]{1,0:T(8,128)(2,1)}, bf16[256,768]{1,0:T(8,128)(2,1)S(1)}, u32[]{:S(2)}, u32[]{:S(2)}) collective-permute-start(bf16[256,768]{1,0:T(8,128)(2,1)} %get-tuple-element.322), channel_id=1, source_target_pairs={{0,0},{8,1},{10,2},{2,3},{4,4},{12,5},{14,6},{6,7},{1,8},{9,9},{11... | collective-permute-start | bytes 1179656 | tf_op jit(solution)/shard_map/ppermute | solution.py:491
  544.1 35.3 %collective-permute-start.35 = (bf16[256,768]{1,0:T(8,128)(2,1)}, bf16[256,768]{1,0:T(8,128)(2,1)S(1)}, u32[]{:S(2)}, u32[]{:S(2)}) collective-permute-start(bf16[256,768]{1,0:T(8,128)(2,1)} %get-tuple-element.321), channel_id=1, source_target_pairs={{2,0},{10,1},{12,2},{4,3},{6,4},{14,5},{8,6},{0,7},{3,8},{11,9},{1... | collective-permute-start | bytes 1179656 | tf_op jit(solution)/shard_map/ppermute | solution.py:491
  565.2 29.5 %collective-permute-start.36 = (bf16[256,768]{1,0:T(8,128)(2,1)S(1)}, bf16[256,768]{1,0:T(8,128)(2,1)S(1)}, u32[]{:S(2)}, u32[]{:S(2)}) collective-permute-start(bf16[256,768]{1,0:T(8,128)(2,1)S(1)} %copy-done.83), channel_id=1, source_target_pairs={{4,0},{12,1},{14,2},{6,3},{0,4},{8,5},{10,6},{2,7},{5,8},{13,9},{1... | collective-permute-start | bytes 1179656 | tf_op jit(solution)/shard_map/ppermute | solution.py:491
  572.2 22.5 %collective-permute-start.37 = (bf16[256,768]{1,0:T(8,128)(2,1)S(1)}, bf16[256,768]{1,0:T(8,128)(2,1)S(1)}, u32[]{:S(2)}, u32[]{:S(2)}) collective-permute-start(bf16[256,768]{1,0:T(8,128)(2,1)S(1)} %copy-done.82), channel_id=1, source_target_pairs={{6,0},{14,1},{8,2},{0,3},{2,4},{10,5},{12,6},{4,7},{7,8},{15,9},{9... | collective-permute-start | bytes 1179656 | tf_op jit(solution)/shard_map/ppermute | solution.py:491
  579.3 22.2 %collective-permute-start.39 = (bf16[4,24,3072]{2,1,0:T(8,128)(2,1)S(1)}, bf16[4,24,3072]{2,1,0:T(8,128)(2,1)S(1)}, u32[]{:S(2)}, u32[]{:S(2)}) collective-permute-start(bf16[4,24,3072]{2,1,0:T(8,128)(2,1)S(1)} %dynamic-slice_bitcast_fusion.21), channel_id=1, source_target_pairs={{0,1},{1,0},{2,3},{3,2},{4,5},{5,4},{6,7},{7,6},{8,9},{9,8},{10,11... | collective-permute-start | bytes 1769480 | tf_op jit(solution)/shard_map/ppermute | solution.py:394
  579.4 22.1 %collective-permute-start.41 = (bf16[4,24,3072]{2,1,0:T(8,128)(2,1)S(1)}, bf16[4,24,3072]{2,1,0:T(8,128)(2,1)S(1)}, u32[]{:S(2)}, u32[]{:S(2)}) collective-permute-start(bf16[4,24,3072]{2,1,0:T(8,128)(2,1)S(1)} %dynamic-slice_bitcast_fusion.20), channel_id=1, source_target_pairs={{0,16},{16,0},{1,17},{17,1},{2,18},{18,2},{3,19},{19,3},{4,20},{20... | collective-permute-start | bytes 1769480 | tf_op jit(solution)/shard_map/ppermute | solution.py:394
  602.0 16.2 %collective-permute-start.48 = (bf16[4,2,24,1536]{3,2,1,0:T(8,128)(2,1)S(1)}, bf16[4,2,24,1536]{3,2,1,0:T(8,128)(2,1)S(1)}, u32[]{:S(2)}, u32[]{:S(2)}) collective-permute-start(bf16[4,2,24,1536]{3,2,1,0:T(8,128)(2,1)S(1)} %dynamic-slice_bitcast_fusion.12), channel_id=1, source_target_pairs={{0,16},{16,0},{1,17},{17,1},{2,18},{18,2},{3,19},{19,3},{4,20},{20... | collective-permute-start | bytes 1769480 | tf_op jit(solution)/shard_map/ppermute | solution.py:394
  603.2 17.3 %collective-permute-start.49 = (bf16[2,4,24,1664]{3,2,1,0:T(8,128)(2,1)S(1)}, bf16[2,4,24,1664]{3,2,1,0:T(8,128)(2,1)S(1)}, u32[]{:S(2)}, u32[]{:S(2)}) collective-permute-start(bf16[2,4,24,1664]{3,2,1,0:T(8,128)(2,1)S(1)} %dynamic-slice_bitcast_fusion.6), channel_id=1, source_target_pairs={{0,1},{1,0},{2,3},{3,2},{4,5},{5,4},{6,7},{7,6},{8,9},{9,8},{10,11... | collective-permute-start | bytes 1916936 | tf_op jit(solution)/shard_map/ppermute | solution.py:394
  606.7 24.1 %collective-permute-start.43 = (bf16[4,2,24,1536]{3,2,1,0:T(8,128)(2,1)S(1)}, bf16[4,2,24,1536]{3,2,1,0:T(8,128)(2,1)S(1)}, u32[]{:S(2)}, u32[]{:S(2)}) collective-permute-start(bf16[4,2,24,1536]{3,2,1,0:T(8,128)(2,1)S(1)} %dynamic-slice_bitcast_fusion.15), channel_id=1, source_target_pairs={{0,16},{16,0},{1,17},{17,1},{2,18},{18,2},{3,19},{19,3},{4,20},{20... | collective-permute-start | bytes 1769480 | tf_op jit(solution)/shard_map/ppermute | solution.py:394
  607.6 33.0 %collective-permute-start.45 = (bf16[2,4,24,1664]{3,2,1,0:T(8,128)(2,1)S(1)}, bf16[2,4,24,1664]{3,2,1,0:T(8,128)(2,1)S(1)}, u32[]{:S(2)}, u32[]{:S(2)}) collective-permute-start(bf16[2,4,24,1664]{3,2,1,0:T(8,128)(2,1)S(1)} %dynamic-slice_bitcast_fusion.7), channel_id=1, source_target_pairs={{0,1},{1,0},{2,3},{3,2},{4,5},{5,4},{6,7},{7,6},{8,9},{9,8},{10,11... | collective-permute-start | bytes 1916936 | tf_op jit(solution)/shard_map/ppermute | solution.py:394
  618.4 22.1 %collective-permute-start.52 = (bf16[4,24,1536]{2,1,0:T(8,128)(2,1)S(1)}, bf16[4,24,1536]{2,1,0:T(8,128)(2,1)S(1)}, u32[]{:S(2)}, u32[]{:S(2)}) collective-permute-start(bf16[4,24,1536]{2,1,0:T(8,128)(2,1)S(1)} %dynamic-slice_bitcast_fusion.34), channel_id=1, source_target_pairs={{0,1},{1,0},{2,3},{3,2},{4,5},{5,4},{6,7},{7,6},{8,9},{9,8},{10,11... | collective-permute-start | bytes 884744 | tf_op jit(solution)/shard_map/ppermute | solution.py:394
  620.8 21.1 %collective-permute-start.53 = (bf16[4,24,1664]{2,1,0:T(8,128)(2,1)S(1)}, bf16[4,24,1664]{2,1,0:T(8,128)(2,1)S(1)}, u32[]{:S(2)}, u32[]{:S(2)}) collective-permute-start(bf16[4,24,1664]{2,1,0:T(8,128)(2,1)S(1)} %dynamic-slice_bitcast_fusion.29), channel_id=1, source_target_pairs={{0,16},{16,0},{1,17},{17,1},{2,18},{18,2},{3,19},{19,3},{4,20},{20... | collective-permute-start | bytes 958472 | tf_op jit(solution)/shard_map/ppermute | solution.py:394
  631.0 14.7 %collective-permute-start.44 = (bf16[4,24,1536]{2,1,0:T(8,128)(2,1)S(1)}, bf16[4,24,1536]{2,1,0:T(8,128)(2,1)S(1)}, u32[]{:S(2)}, u32[]{:S(2)}) collective-permute-start(bf16[4,24,1536]{2,1,0:T(8,128)(2,1)S(1)} %dynamic-slice_bitcast_fusion.35), channel_id=1, source_target_pairs={{0,1},{1,0},{2,3},{3,2},{4,5},{5,4},{6,7},{7,6},{8,9},{9,8},{10,11... | collective-permute-start | bytes 884744 | tf_op jit(solution)/shard_map/ppermute | solution.py:394
  649.2 35.6 %collective-permute-start.50 = (bf16[24,9344]{1,0:T(8,128)(2,1)S(1)}, bf16[24,9344]{1,0:T(8,128)(2,1)S(1)}, u32[]{:S(2)}, u32[]{:S(2)}) collective-permute-start(bf16[24,9344]{1,0:T(8,128)(2,1)S(1)} %get-tuple-element.318), channel_id=1, source_target_pairs={{0,4},{2,6},{4,0},{6,2},{1,5},{3,7},{5,1},{7,3},{8,12},{10,14},{12... | collective-permute-start | bytes 1345544 | tf_op jit(solution)/shard_map/ppermute | solution.py:394
  649.2 35.6 %collective-permute-start.51 = (bf16[24,9344]{1,0:T(8,128)(2,1)S(1)}, bf16[24,9344]{1,0:T(8,128)(2,1)S(1)}, u32[]{:S(2)}, u32[]{:S(2)}) collective-permute-start(bf16[24,9344]{1,0:T(8,128)(2,1)S(1)} %get-tuple-element.317), channel_id=1, source_target_pairs={{0,2},{2,4},{4,6},{6,0},{1,3},{3,5},{5,7},{7,1},{8,10},{10,12},{12... | collective-permute-start | bytes 1345544 | tf_op jit(solution)/shard_map/ppermute | solution.py:394
  688.1 16.7 %collective-permute-start.55 = (bf16[24,3200]{1,0:T(8,128)(2,1)}, bf16[24,3200]{1,0:T(8,128)(2,1)}, u32[]{:S(2)}, u32[]{:S(2)}) collective-permute-start(bf16[24,3200]{1,0:T(8,128)(2,1)} %get-tuple-element.352), channel_id=1, source_target_pairs={{0,4},{2,6},{4,0},{6,2},{1,5},{3,7},{5,1},{7,3},{8,12},{10,14},{12... | collective-permute-start | bytes 460808 | tf_op jit(solution)/shard_map/ppermute | solution.py:394
  (145 other events, 1576.2 us)
Sparse Core Ops, SparseCore 0:
  13.5 112.1 all-gather.2
  164.1 95.2 all-gather.4

commit v3 on v2

--- a/solution.py
+++ b/solution.py
@@ -262,21 +262,21 @@
     return pl.pallas_call(
         mlp_kernel,
         grid=(FF // wide,),
-        in_specs=[whole, up_spec(wide), down_spec(wide, FF // D)],
+        in_specs=[whole, up_spec(wide), down_spec(wide, w_mlp[2])],
         out_specs=[across, across, whole],
         out_shape=[
             jax.ShapeDtypeStruct((rows, FF), BF),
             jax.ShapeDtypeStruct((rows, FF), BF),
             jax.ShapeDtypeStruct((rows, D), F32),
         ],
-        compiler_params=pltpu.CompilerParams(vmem_limit_bytes=40 * 2**20),
+        compiler_params=pltpu.CompilerParams(vmem_limit_bytes=56 * 2**20),
         cost_estimate=pl.CostEstimate(
             flops=4 * rows * D * FF,
             bytes_accessed=4 * rows * FF + 4 * D * FF + 6 * rows * D,
             transcendentals=rows * FF,
         ),
         name="mlp_forward",
-    )(n2, w_mlp, w_mlp)
+    )(n2, w_mlp[0], w_mlp[1])
 
 
 def mlp_back_kernel(
@@ -307,7 +307,7 @@
     return pl.pallas_call(
         mlp_back_kernel,
         grid=(FF // wide,),
-        in_specs=[whole, whole, across, across, up_spec(wide), down_spec(wide, FF // D)],
+        in_specs=[whole, whole, across, across, up_spec(wide), down_spec(wide, w_mlp[2])],
         out_specs=[up_spec(wide), down_spec(wide), whole],
         out_shape=[
             jax.ShapeDtypeStruct((D, FF), BF),
@@ -319,14 +319,14 @@
             pltpu.VMEM((D, rows), BF),
             pltpu.VMEM((rows, wide), BF),
         ],
-        compiler_params=pltpu.CompilerParams(vmem_limit_bytes=48 * 2**20),
+        compiler_params=pltpu.CompilerParams(vmem_limit_bytes=56 * 2**20),
         cost_estimate=pl.CostEstimate(
             flops=8 * rows * D * FF,
             bytes_accessed=4 * rows * FF + 8 * D * FF + 8 * rows * D,
             transcendentals=0,
         ),
         name="mlp_backward",
-    )(d_mlp, n2, act, slope, w_mlp, w_mlp)
+    )(d_mlp, n2, act, slope, w_mlp[0], w_mlp[1])
 
 
 def norm_parts(rows):
@@ -343,10 +343,11 @@
 
 def gelu_parts(pre):
     c = math.sqrt(2.0 / math.pi)
+    k = 0.044715 * c
     sq = pre * pre
-    t = jnp.tanh(c * pre * (1.0 + 0.044715 * sq))
-    act = 0.5 * pre * (1.0 + t)
-    slope = 0.5 * (1.0 + t) + 0.5 * pre * (1.0 - t * t) * (c * (1.0 + 3 * 0.044715 * sq))
+    h = 0.5 * jnp.tanh(pre * (c + k * sq)) + 0.5
+    act = pre * h
+    slope = h + (act * (1.0 - h)) * (2.0 * c + (6.0 * k) * sq)
     return act.astype(BF), slope.astype(BF)
 
 
@@ -401,9 +402,11 @@
     z_n = seq // x_n
     half = seq // 2
     ways = dp * seq
-    inner = Mesh(mesh.devices.reshape(y_n, 2, z_n, x_n), ("y", "core", "z", "x"))
-    every = ("y", "core", "z", "x")
-    home_axes = ("core", "z", "x")
+    inner = Mesh(
+        mesh.devices.reshape(y_n, 2, z_n, x_n // 2, 2), ("y", "core", "z", "xh", "xl")
+    )
+    both_x = ("xh", "xl")
+    every = ("y", "core", "z", "xh", "xl")
     lb = LEN // seq
 
     def route(t):
@@ -411,17 +414,34 @@
         for c in range(2):
             for s in range(seq):
                 block = s // 2
-                core = (s ^ block) & 1
-                pairs.append((c * seq + s, core * seq + 2 * ((block + t) % half) + c))
+                pairs.append((c * seq + s, ((s ^ block) & 1) * seq + 2 * ((block + t) % half) + c))
         return pairs
 
     routes = [route(t) for t in range(half)]
+
+    def turn(odd):
+        return [(c * 2 + e, (e ^ odd) * 2 + c) for c in range(2) for e in range(2)]
 
     def swap_core(value):
         return lax.ppermute(value, "core", [(0, 1), (1, 0)])
 
     def all_sum(value):
-        for axis, size in (("core", 2), ("x", x_n), ("y", y_n), ("z", z_n)):
+        pair = [
+            lax.ppermute(
+                value,
+                ("core", *both_x),
+                [
+                    (c * x_n + i, ((c + dc) % 2) * x_n + (i + dx) % x_n)
+                    for c in range(2)
+                    for i in range(x_n)
+                ],
+            )
+            for dc in range(2)
+            for dx in range(x_n)
+            if dc or dx
+        ]
+        value = sum(pair, start=value)
+        for axis, size in (("y", y_n), ("z", z_n)):
             value = sum(
                 (ahead(value, axis, size, s) for s in range(1, size)), start=value
             )
@@ -433,7 +453,7 @@
         qkv_mom, out_mom, up_mom, down_mom, vec_mom,
         qkv_avg, out_avg, up_avg, down_avg, vec_avg,
     ):
-        y, core, z, x = (lax.axis_index(a) for a in every)
+        y, core, z, x = (lax.axis_index(a) for a in ("y", "core", "z", both_x))
         chip = z * x_n + x
         seq_id = chip // 2
         group = chip % 2
@@ -451,7 +471,7 @@
             return grown(shard, "z", z_n, z, 0)
 
         def spread_x(value, x_first):
-            return grown(value, "x", x_n, x, 1 if x_first else 2)
+            return grown(value, both_x, x_n, x, 1 if x_first else 2)
 
         def spread_y(value):
             return grown(value, "y", y_n, y, 0)
@@ -473,37 +493,50 @@
         def gather_mlp(shard):
             return lax.all_gather(shard, every, axis=0, tiled=True)
 
-        def come(source):
+        def along_seqs(blocks):
+            return lax.all_to_all(blocks, ("z", "xh"), split_axis=0, concat_axis=0, tiled=True)
+
+        def parts_of(source):
             by_seq = source.transpose(1, 0, 2)
-            got = []
-            for t in range(half):
-                sent = lax.dynamic_index_in_dim(by_seq, (chip // 2 + t) % half, 0, keepdims=False)
-                got.append(lax.ppermute(sent, home_axes, routes[t]))
-            return got
+            return [
+                lax.dynamic_index_in_dim(by_seq, (chip // 2 + t) % half, 0, keepdims=False)
+                for t in range(half)
+            ]
+
+        def come(parts):
+            return [lax.ppermute(p, every[1:], route) for p, route in zip(parts, routes)]
 
         def own_rows(got):
             return placed(got[:1] + got[:0:-1], seq_id, 0).reshape(half * lb, D)
 
         def leave(rows):
+            blocks = rows.reshape(half // 2, 2, lb, D)
+            got = [
+                lax.ppermute(blocks[:, odd], ("core", "xl"), [(b, a) for a, b in turn(odd)])
+                for odd in range(2)
+            ]
+            return along_seqs(jnp.stack(got, axis=1).reshape(half, lb, D))
+
+        def arrived(got):
+            return got.transpose(1, 0, 2)
+
+        def leave_at_once(rows):
             got = []
             for t in range(half):
                 sent = lax.dynamic_slice(rows, (((seq_id - t) % half) * lb, 0), (lb, D))
-                got.append(lax.ppermute(sent, home_axes, [(b, a) for a, b in routes[t]]))
+                got.append(lax.ppermute(sent, every[1:], [(b, a) for a, b in routes[t]]))
             return got
 
-        def arrived(got):
-            return placed(got, chip // 2, 0).transpose(1, 0, 2)
-
         gains_row = jnp.pad(vectors.T, ((0, 0), (0, 128 - 5))).astype(BF)
-        mlp0 = gather_mlp(shard_mlp(0))
-        chips_a = spread_z(jnp.concatenate([shard_a(0), gains_row], axis=1))
+        x_parts = parts_of(tokens)
+        chips_a = jnp.concatenate([shard_a(0), gains_row], axis=1)
+        chips_a = spread_z(after(chips_a, *x_parts))
+        mlp0 = gather_mlp(after(shard_mlp(0), chips_a))
         chips_a = spread_x(chips_a, True)
-        own_x = own_rows(come(tokens))
-        next_a = after(shard_a(1), own_x)
-        chips_b = spread_z(next_a)
-        chips_a = after(spread_y(chips_a), own_x, chips_b)
-        full_a = spread_core(chips_a)
-        gains = full_a[:, 4 * D : 4 * D + 5].T.astype(F32)
+        own_x = own_rows(come(x_parts))
+        next_mlp = shard_mlp(1)
+        chips_b = spread_z(after(shard_a(1), own_x))
+        chips_a = after(spread_y(after(chips_a, own_x, next_mlp)), chips_b)
         meta = jnp.concatenate([picked_ids, lengths[:, None]], axis=1)
         meta = lax.dynamic_index_in_dim(
             jnp.where(group == core, meta, swap_core(meta)), seq_id, 0, keepdims=False
@@ -522,24 +555,27 @@
         def to_rows(values):
             return dotf(chosen, values, TN)
 
-        mlp1 = gather_mlp(after(shard_mlp(1), full_a))
         x_low = at_picks(own_x)
+        full_a = spread_core(after(chips_a, x_low))
+        gains = full_a[:, 4 * D : 4 * D + 5].T.astype(F32)
+        chips_b = spread_y(chips_b)
+        mlp1 = gather_mlp(after(next_mlp, full_a))
         x_rows = x_low.astype(F32)
         gate = jax.nn.sigmoid(jnp.sum(x_rows * gains[2], axis=-1, keepdims=True))
         n1_0, kv0 = forward_first(x_rows, gains[0], full_a)
         q0 = dotf(n1_0, full_a[:, :D], NN).astype(BF)
-        chips_b = spread_y(after(chips_b, x_low))
+        chips_b = spread_x(after(chips_b, q0), False)
         own0 = ((q0, 0), (kv0, 0), (kv0, 6))
         o0, lse0 = attend(*own0, (), core_arr, lb)
         branch0, mid0, n2_0 = forward_second(x_rows, gains[1], full_a, o0)
-        chips_b = spread_x(after(chips_b, q0), False)
+        mlp0 = (mlp0, mlp0, FF // D)
         act0, slope0, out0 = mlp_forward(n2_0, mlp0)
         both0 = branch0 + out0
         delta = (gate * both0).astype(BF)
         mixed = own_x.astype(F32) + to_rows(delta)
 
         full_b = spread_core(after(chips_b, n2_0))
-        cot_sent = come(after(cotangent, full_b))
+        cot_sent = come(parts_of(after(cotangent, full_b)))
         n1_1, kv1 = forward_first(mixed, gains[3], full_b)
         far = swap_core(kv1)
         far1 = ((far, 0), (far, 6))
@@ -547,9 +583,11 @@
         own1 = ((q1, 0), (kv1, 0), (kv1, 6))
         o1, lse1 = attend(*own1, far1, core_arr, lb)
         branch1, mid1, n2_1 = forward_second(mixed, gains[4], full_b, o1)
+        mlp1 = (mlp1, mlp1, FF // D)
         act1, slope1, out1 = mlp_forward(n2_1, mlp1)
-        act_sent = leave((live * (mid1 + out1)).astype(BF))
-        d_top = live * own_rows([after(c, o1) for c in cot_sent]).astype(F32)
+        act_rows = (live * (mid1 + out1)).astype(BF)
+        act_sent = leave(act_rows)
+        d_top = live * own_rows([after(c, n2_1) for c in cot_sent]).astype(F32)
 
         def by_shard(grad):
             return grad.reshape(y_n, 2, z_n, x_n, grad.shape[0] // ways, grad.shape[1])
@@ -567,45 +605,60 @@
         def of_core(*grads):
             return at([by_shard(g) for g in grads], core, 1)
 
-        def over(value, axis, size, place, dim, kind=BF, late=()):
-            total = at([value], place, dim).astype(F32)
-            for s in range(1, size):
-                sent = at([value], (place + size - s) % size, dim)
-                total = total + after(ahead(sent, axis, size, s), *late).astype(F32)
-            return total.astype(kind)
+        class Sum:
+            def __init__(self, value, axis, dim):
+                size, place = (y_n, y) if axis == "y" else (x_n, x)
+                self.own = at([value], place, dim)
+                self.cut = [at([value], (place + size - s) % size, dim) for s in range(1, size)]
+                self.got = [ahead(c, axis, size, s + 1) for s, c in enumerate(self.cut)]
+
+            def done(self, *late):
+                total = self.own.astype(F32)
+                for got in self.got:
+                    total = total + after(got, *late).astype(F32)
+                return total.astype(BF)
+
+        class LastSum:
+            def __init__(self, *values):
+                whole = jnp.concatenate(values, axis=-1)
+                self.own = at([whole], z, 0)
+                self.cut = [at([whole], (z + z_n - s) % z_n, 0) for s in range(1, z_n)]
+                self.got = [ahead(c, "z", z_n, s + 1) for s, c in enumerate(self.cut)]
+
+            def done(self, *late):
+                total = self.own.astype(F32)
+                for got in self.got:
+                    total = total + after(got, *late).astype(F32)
+                return total
 
         def first_way(value, x_first):
-            return over(value, "x", x_n, x, 2) if x_first else over(value, "y", y_n, y, 0)
+            return Sum(value, both_x, 2) if x_first else Sum(value, "y", 0)
 
         def second_way(value, x_first):
-            return over(value, "y", y_n, y, 0) if x_first else over(value, "x", x_n, x, 1)
-
-        def last_way(value, *late):
-            return over(value, "z", z_n, z, 0, F32, late)
-
-        def along(value, x_first):
-            return last_way(second_way(first_way(value, x_first), x_first))
+            return Sum(value, "y", 0) if x_first else Sum(value, both_x, 1)
 
         def columns(*vectors):
             return jnp.pad(jnp.stack(vectors, 1), ((0, 0), (0, 128 - len(vectors)))).astype(BF)
 
         d_mid1, do1, g_out1, g_up1, g_down1, g_b1 = back_mlp(
-            mid1, (full_b, mlp1), gains[4], (o1, n2_1, act1, slope1), d_top.astype(BF), d_top, None
+            mid1, (full_b, mlp1), gains[4], (o1, n2_1, act1, slope1),
+            after(d_top.astype(BF), act_rows), d_top, None
         )
         up1, down1 = over_core(g_up1), over_core(g_down1)
-        do1 = after(do1, up1, down1)
         up1, down1 = first_way(up1, False), first_way(down1, True)
+        do1 = after(do1, *up1.cut, *down1.cut)
         parts = []
         for first, count in ((0, 4), (4, 2)):
             dq, d_own, d_far = attend_back(
                 own1[0], (do1, 0), (o1, 0), lse1, own1[1], own1[2], far1, core_arr, lb, first, count
             )
             parts.append((dq, d_own, swap_core(d_far)))
-            up1, down1 = after(up1, dq), after(down1, dq)
+            up1, down1 = up1.done(dq), down1.done(dq)
             if first == 0:
-                act_sent = [after(a, dq) for a in act_sent]
-                do1 = after(do1, up1, down1, dq, *act_sent)
                 up1, down1 = second_way(up1, False), second_way(down1, True)
+                act_sent = after(act_sent, dq)
+                do1 = after(do1, dq, act_sent, *up1.cut, *down1.cut)
+        pair1 = LastSum(up1, down1)
         d_q1 = jnp.concatenate([parts[0][0], dq], axis=1)
         sums = [(d_own + back.astype(F32)).astype(BF) for _, d_own, back in parts]
         d_kv1 = jnp.concatenate([s[0] for s in sums] + [s[1] for s in sums], axis=1)
@@ -615,38 +668,46 @@
         d_delta = at_picks(d_mixed.astype(BF)).astype(F32)
         gated = gate * d_delta
         d_logit = gate * (1.0 - gate) * jnp.sum(d_delta * both0, axis=-1, keepdims=True)
-        activations = arrived([after(a, d_mixed) for a in act_sent])
-        pair1 = jnp.concatenate([up1, down1], axis=-1)
         head1a = first_way(head1[..., : 2 * D], False)
         head1b = first_way(head1[..., 2 * D :], True)
+        gated_low = after(gated.astype(BF), *head1a.cut, *head1b.cut)
         d_mid0, do0, g_out0, g_up0, g_down0, g_b0 = back_mlp(
-            mid0, (full_a, mlp0), gains[1], (o0, n2_0, act0, slope0), gated.astype(BF), None, gated
+            mid0, (full_a, mlp0), gains[1], (o0, n2_0, act0, slope0), gated_low, None, gated
         )
         up0, down0 = first_way(of_core(g_up0), False), first_way(of_core(g_down0), True)
+        head1a = second_way(head1a.done(d_mid0), False)
+        head1b = second_way(head1b.done(d_mid0), True)
+        do0 = after(do0, *up0.cut, *down0.cut, *head1a.cut, *head1b.cut, *pair1.got)
         dq, d_kv = attend_back(
             own0[0], (do0, 0), (o0, 0), lse0, own0[1], own0[2], (), core_arr, lb, 0, PAIRS
         )
-        head1a, head1b = second_way(after(head1a, dq), False), second_way(after(head1b, dq), True)
         d_kv0 = jnp.concatenate([d_kv[0], d_kv[1]], axis=1)
         d_rows0, g_q0, g_kv0, g_a0 = back_qkv(x_rows, full_a, gains[0], n1_0, dq, d_kv0, d_mid0)
         g_r = jnp.sum(d_logit * x_rows, axis=0)
         d_chosen = (d_rows0 + d_logit * gains[2]).astype(BF)
         grad_rows = (d_mixed + to_rows(d_chosen)).astype(BF)
-        pair1 = last_way(pair1, grad_rows)
-        grad_sent = leave(grad_rows)
+        grad_sent = leave_at_once(grad_rows)
+        head1a, head1b = head1a.done(grad_rows), head1b.done(grad_rows)
+        up0, down0 = up0.done(grad_rows), down0.done(grad_rows)
         up0, down0 = second_way(up0, False), second_way(down0, True)
-        head0a = after(of_core(g_q0, g_kv0[:, :D]), grad_rows, up0, down0)
+        head0a = after(of_core(g_q0, g_kv0[:, :D]), *up0.cut, *down0.cut)
         head0b = of_core(g_kv0[:, D:], g_out0, columns(g_a0, g_b0, g_r))
-        head0b = after(head0b, grad_rows, up0, down0)
-        early = jnp.concatenate([up0, down0, head1a, head1b], axis=-1)
+        head0b = after(head0b, *up0.cut, *down0.cut)
         head0a, head0b = first_way(head0a, False), first_way(head0b, True)
-        early = last_way(after(early, *grad_sent), head0a, head0b)
+        up0, down0 = up0.done(*head0a.cut, *head0b.cut), down0.done(*head0a.cut, *head0b.cut)
+        early = LastSum(up0, down0, head1a, head1b)
+        grad_sent = [after(g, *early.cut) for g in grad_sent]
+        input_grad = arrived(placed(grad_sent, chip // 2, 0)).astype(F32)
+        activations = arrived(after(act_sent, *early.cut))
+        head0a, head0b = head0a.done(*early.cut), head0b.done(*early.cut)
+        pair1 = pair1.done(*early.cut)
         head0a, head0b = second_way(head0a, False), second_way(head0b, True)
-        head0 = last_way(after(jnp.concatenate([head0a, head0b], axis=-1), early))
+        head0 = LastSum(head0a.done(), head0b.done())
+        early = early.done(*head0.cut)
+        head0 = head0.done(early)
         squares = sum(jnp.sum(v * v) for v in (early, head0, pair1))
         up0, down0, head1 = early[:, :FF], early[:, FF : 2 * FF], early[:, 2 * FF :]
         up1, down1 = pair1[:, :FF], pair1[:, FF:]
-        input_grad = arrived(grad_sent).astype(F32)
 
         def unmixed(up):
             return up.reshape(piece, 4, ways, piece).swapaxes(1, 2).reshape(piece, FF)
@@ -679,7 +740,7 @@
         return (activations, input_grad, grad_norm, *new_w, *new_m, *new_z)
 
     group_spec = ("y", "core")
-    pos_spec = ("z", "x")
+    pos_spec = ("z", "xh", "xl")
     rows_spec = P(pos_spec, group_spec, None)
     param_specs = (
         P(None, None, every, None),

time: 751 us -> 679 us (0.904)
  waiting for transfers between devices: 263 us -> 154 us
  other arithmetic: 47.6 us -> 67.7 us
  local copies, waits for them, and re-layouts: 103 us -> 111 us
    ppermute x43 -> x41, waiting for transfers between devices: 203 us -> 116 us  [ahead(): lax.ppermute(value, axis, [(i, (i - step) % size) for i in range(size)])]
    ppermute x16 -> x17, waiting for transfers between devices: 58.5 us -> 37 us  [the longest x8 37 us: come(): lax.ppermute(p, every[1:], route)]
    convert_element_type x18 -> x19, other arithmetic: 11.6 us -> 20.3 us  [the longest x16 16.6 us: done(): return total.astype(BF)]
    ppermute x43 -> x41, starting transfers between devices: 73.8 us -> 65.6 us  [ahead(): lax.ppermute(value, axis, [(i, (i - step) % size) for i in range(size)])]
    unnamed x260 -> x300, local copies, waits for them, and re-layouts: 39.4 us -> 41.3 us
    ppermute x16 -> x17, starting transfers between devices: 27.9 us -> 29.6 us  [the longest x8 12.1 us: come(): lax.ppermute(p, every[1:], route)]
    squeeze x28 -> x24, local copies, waits for them, and re-layouts: 19.3 us -> 17.8 us  [at(): lax.dynamic_index_in_dim(g, which, dim, keepdims=False)]
  transfers between devices with their start and end apart: 70 -> 70, of which waited for: 31 -> 19; matrix products, arithmetic and copies ran while one was open for 18% -> 23% of each run, Pallas kernels for 16% -> 22%
where the time goes in v3:
time: 679 us; the launch traced here: 670 us
  Pallas kernels  167 us (25%)
  waiting for transfers between devices  154 us (23%)
  local copies, waits for them, and re-layouts  111 us (16%)
  starting transfers between devices  103 us (15%)
  other arithmetic  67.7 us (10%)
  matrix products  43.2 us (6%)
  between operations  24.6 us (4%)
    ppermute x41, waiting for transfers between devices, ahead(): lax.ppermute(value, axis, [(i, (i - step) % size) for i in range(size)])  116 us
    ppermute x41, starting transfers between devices, ahead(): lax.ppermute(value, axis, [(i, (i - step) % size) for i in range(size)])  65.6 us
    pallas_call x3, Pallas kernels, attend_back(): pl.pallas_call(functools.partial(attend_back_kernel, lb if far else 0, kc...  59.8 us
    dot_general x22, matrix products, dotf(): return lax.dot_general(left, right, dims, preferred_element_type=F32)  43.2 us
    unnamed x300, local copies, waits for them, and re-layouts  41.3 us
    pallas_call x2, Pallas kernels, mlp_backward(): pl.pallas_call(mlp_back_kernel, grid=(FF // wide,), in_specs=[whole, whol...  39.5 us
    pallas_call x2, Pallas kernels, attend(): pl.pallas_call(functools.partial(attend_kernel, lb if far else 0), grid=(...  37.4 us
    ppermute x8, waiting for transfers between devices, come(): lax.ppermute(p, every[1:], route)  37 us
  transfers between devices with their start and end apart: 70, of which 19 were waited for; matrix products, arithmetic and copies ran while one was open for 23% of the time, Pallas kernels for 22%

profile of v3, /device:TPU:0, one launch (start us, length us, event | category | flops | bytes accessed | tf_op | source)
XLA Modules:
  0.0 670.0 jit_solution(14300397170230947358)
XLA Ops:
  10.1 3.3 constant_dynamic-slice_fusion.10
  16.7 5.1 collective-permute-start.6
  27.1 7.7 %collective-permute-done.7 = bf16[24,3200]{1,0:T(8,128)(2,1)S(1)} collective-permute-done((bf16[24,3200]{1,0:T(8,128)(2,1)S(1)}, bf16[24,3200]{1,0:T(8,128)(2,1)S(1)}, u32[]{:S(2)}, u32[]{:S(2)}) %collective-permute-start.7) | collective-permute-done | bytes 153632 | tf_op jit(solution)/shard_map/ppermute | solution.py:395
  49.2 3.3 collective-permute-done.2
  53.2 26.7 %collective-permute-done.3 = bf16[256,768]{1,0:T(8,128)(2,1)S(1)} collective-permute-done((bf16[256,768]{1,0:T(8,128)(2,1)}, bf16[256,768]{1,0:T(8,128)(2,1)S(1)}, u32[]{:S(2)}, u32[]{:S(2)}) %collective-permute-start.3) | collective-permute-done | bytes 393248 | tf_op jit(solution)/shard_map/ppermute | solution.py:507
  96.1 4.3 collective-permute-done.11
  101.0 10.3 %collective-permute-done.12 = bf16[24,3072]{1,0:T(8,128)(2,1)S(1)} collective-permute-done((bf16[24,3072]{1,0:T(8,128)(2,1)S(1)}, bf16[24,3072]{1,0:T(8,128)(2,1)S(1)}, u32[]{:S(2)}, u32[]{:S(2)}) %collective-permute-start.12) | collective-permute-done | bytes 147488 | tf_op jit(solution)/shard_map/ppermute | solution.py:395
  117.4 3.2 collective-permute-done.10
  123.4 4.3 collective-permute-done.14
  133.3 13.9 %collective-permute-done.15 = bf16[4,24,3072]{2,1,0:T(8,128)(2,1)S(1)} collective-permute-done((bf16[4,24,3072]{2,1,0:T(8,128)(2,1)S(1)}, bf16[4,24,3072]{2,1,0:T(8,128)(2,1)S(1)}, u32[]{:S(2)}, u32[]{:S(2)}) %collective-permute-start.15) | collective-permute-done | bytes 589856 | tf_op jit(solution)/shard_map/ppermute | solution.py:395
  155.5 5.5 attend_own.1
  164.0 20.1 %collective-permute-done.16 = bf16[2,4,24,3072]{3,2,1,0:T(8,128)(2,1)S(1)} collective-permute-done((bf16[2,4,24,3072]{3,2,1,0:T(8,128)(2,1)S(1)}, bf16[2,4,24,3072]{3,2,1,0:T(8,128)(2,1)S(1)}, u32[]{:S(2)}, u32[]{:S(2)}) %collective-permute-start.16) | collective-permute-done | bytes 1179680 | tf_op jit(solution)/shard_map/ppermute | solution.py:395
  184.6 4.5 collective-permute-done.17
  191.9 7.8 %mlp_forward.2 = (bf16[256,3072]{1,0:T(8,128)(2,1)}, bf16[256,3072]{1,0:T(8,128)(2,1)}, f32[256,768]{1,0:T(8,128)}) custom-call(bf16[256,768]{1,0:T(8,128)(2,1)} %multiply_convert_fusion.4.n2_ref, bf16[768,6144]{1,0:T(8,128)(2,1)} %all-gather.3.cloned.1.call-done.up_ref.down_ref, bf16[768,6144]{1,0:T(8,128)(2,1)} %all-gather.3.cloned.1.call-done.up_ref.down_ref), custom_call_target="tpu_custom_call" | custom-call | flops 2415919104 | bytes 13762560 | tf_op jit(solution)/shard_map/mlp_forward/pallas_call | solution.py:262
  203.9 2.8 convolution_convert_fusion.refs_1_.refs_2_.refs_4_.refs_5_
  211.2 5.2 collective-permute-start.24
  219.1 31.9 %attend_far.1 = (bf16[1024,768]{1,0:T(8,128)(2,1)S(1)}, f32[6,2,1024]{2,1,0:T(2,128)S(1)}) custom-call(s32[1]{0:T(128)} %bitcast.13.start_ref.core_ref, bf16[1024,768]{1,0:T(8,128)(2,1)S(1)} %convolution_convert_fusion.5.refs_0_, bf16[1024,1536]{1,0:T(8,128)(2,1)S(1)} %copy-done.19, bf16[1024,1536]{1,0:T(8,128)(2,1)S(1)} %copy-done.19, ...), custom_call_target="tpu_custom_call" | custom-call | flops 19327352832 | bytes 9437184 | tf_op jit(solution)/shard_map/attend_far/pallas_call | solution.py:93
  256.1 7.0 %collective-permute-done.23 = bf16[256,768]{1,0:T(8,128)(2,1)S(1)} collective-permute-done((bf16[256,768]{1,0:T(8,128)(2,1)S(1)}, bf16[256,768]{1,0:T(8,128)(2,1)S(1)}, u32[]{:S(2)}, u32[]{:S(2)}) %collective-permute-start.23) | collective-permute-done | bytes 393248 | tf_op jit(solution)/shard_map/ppermute | solution.py:507
  263.2 18.3 %mlp_forward.3 = (bf16[1024,3072]{1,0:T(8,128)(2,1)}, bf16[1024,3072]{1,0:T(8,128)(2,1)}, f32[1024,768]{1,0:T(8,128)}) custom-call(bf16[1024,768]{1,0:T(8,128)(2,1)} %multiply_convert_fusion.1.n2_ref, bf16[768,6144]{1,0:T(8,128)(2,1)} %all-gather.5.cloned.1.call-done.up_ref.down_ref, bf16[768,6144]{1,0:T(8,128)(2,1)} %all-gather.5.cloned.1.call-done.up_ref.down_ref), custom_call_target="tpu_custom_call" | custom-call | flops 9663676416 | bytes 26738688 | tf_op jit(solution)/shard_map/mlp_forward/pallas_call | solution.py:262
  281.5 3.7 fusion.3
  290.1 28.0 %mlp_backward.2 = (bf16[768,3072]{1,0:T(8,128)(2,1)}, bf16[768,3072]{1,0:T(8,128)(2,1)}, f32[1024,768]{1,0:T(8,128)}) custom-call(bf16[1024,768]{1,0:T(8,128)(2,1)} %get-tuple-element.110.dm_ref, bf16[1024,768]{1,0:T(8,128)(2,1)} %multiply_convert_fusion.1.n2_ref, bf16[1024,3072]{1,0:T(8,128)(2,1)} %get-tuple-element.111.act_ref, ...), custom_call_target="tpu_custom_call" | custom-call | flops 19327352832 | bytes 37748736 | tf_op jit(solution)/shard_map/mlp_backward/pallas_call | solution.py:307
  318.2 4.3 constant_dynamic-slice_fusion.9
  337.7 4.8 all-to-all-start
  342.5 3.3 fusion.1
  354.9 36.1 %attend_back_far.2 = (bf16[1024,512]{1,0:T(8,128)(2,1)S(1)}, f32[2,1024,512]{2,1,0:T(8,128)}, bf16[2,1024,512]{2,1,0:T(8,128)(2,1)}) custom-call(s32[1]{0:T(128)} %bitcast.13.start_ref.core_ref, bf16[1024,768]{1,0:T(8,128)(2,1)S(1)} %copy-done.27, bf16[1024,768]{1,0:T(8,128)(2,1)S(1)} %convolution_convert_fusion.4.refs_1_, ...), custom_call_target="tpu_custom_call" | custom-call | flops 26843545600 | bytes 18874368 | tf_op jit(solution)/shard_map/attend_back_far/pallas_call | solution.py:185
  398.4 18.6 %attend_back_far.3 = (bf16[1024,256]{1,0:T(8,128)(2,1)S(1)}, f32[2,1024,256]{2,1,0:T(8,128)S(1)}, bf16[2,1024,256]{2,1,0:T(8,128)(2,1)S(1)}) custom-call(s32[1]{0:T(128)} %bitcast.13.start_ref.core_ref, bf16[1024,768]{1,0:T(8,128)(2,1)S(1)} %copy-done.28, bf16[1024,768]{1,0:T(8,128)(2,1)S(1)} %convolution_convert_fusion.4.refs_1_, ...), custom_call_target="tpu_custom_call" | custom-call | flops 13421772800 | bytes 18874368 | tf_op jit(solution)/shard_map/attend_back_far/pallas_call | solution.py:185
  427.9 4.6 convolution_convert_fusion.1
  432.5 3.4 multiply_reduce_fusion.2
  444.6 3.6 collective-permute-start.38
  456.0 11.4 %mlp_backward.3 = (bf16[768,3072]{1,0:T(8,128)(2,1)}, bf16[768,3072]{1,0:T(8,128)(2,1)}, f32[256,768]{1,0:T(8,128)}) custom-call(bf16[256,768]{1,0:T(8,128)(2,1)} %fusion.54.dm_ref, bf16[256,768]{1,0:T(8,128)(2,1)} %multiply_convert_fusion.4.n2_ref, bf16[256,3072]{1,0:T(8,128)(2,1)} %get-tuple-element.129.act_ref, ...), custom_call_target="tpu_custom_call" | custom-call | flops 4831838208 | bytes 23592960 | tf_op jit(solution)/shard_map/mlp_backward/pallas_call | solution.py:307
  487.5 5.0 attend_back_own.1
  508.7 4.4 collective-permute-done.44
  513.1 3.2 collective-permute-start.47
  517.4 3.9 collective-permute-start.48
  528.3 11.8 %collective-permute-done.43 = bf16[4,24,3072]{2,1,0:T(8,128)(2,1)S(1)} collective-permute-done((bf16[4,24,3072]{2,1,0:T(8,128)(2,1)S(1)}, bf16[4,24,3072]{2,1,0:T(8,128)(2,1)S(1)}, u32[]{:S(2)}, u32[]{:S(2)}) %collective-permute-start.43) | collective-permute-done | bytes 589856 | tf_op jit(solution)/shard_map/ppermute | solution.py:395
  540.3 18.6 %collective-permute-done.41 = bf16[4,24,3072]{2,1,0:T(8,128)(2,1)S(1)} collective-permute-done((bf16[4,24,3072]{2,1,0:T(8,128)(2,1)S(1)}, bf16[4,24,3072]{2,1,0:T(8,128)(2,1)S(1)}, u32[]{:S(2)}, u32[]{:S(2)}) %collective-permute-start.41) | collective-permute-done | bytes 589856 | tf_op jit(solution)/shard_map/ppermute | solution.py:395
  560.8 3.8 copy.345
  566.8 3.8 collective-permute-start.50
  571.0 3.7 copy.346
  584.0 4.1 stack_reshape.13
  593.3 5.6 collective-permute-done.54
  601.2 3.1 collective-permute-start.57
  615.2 3.6 collective-permute-done.58
  625.2 3.1 collective-permute-start.62
  630.5 2.9 collective-permute-start.63
  634.7 9.4 %collective-permute-start.64 = (f32[1,1]{1,0:T(1,128)}, f32[1,1]{1,0:T(1,128)}, u32[]{:S(2)}, u32[]{:S(2)}) collective-permute-start(f32[1,1]{1,0:T(1,128)} %add.701), channel_id=1, source_target_pairs={{0,6},{2,0},{4,2},{6,4},{1,7},{3,1},{5,3},{7,5},{8,14},{10,8},{12,... | collective-permute-start | bytes 20 | tf_op jit(solution)/shard_map/ppermute | solution.py:395
  644.1 2.9 collective-permute-start.65
  649.5 2.8 collective-permute-done.66
  (604 shorter events, 242.6 us)
Async XLA Ops:
  7.2 184.7 %all-gather.3.cloned.1.call-start = ((), (), s32[]{:S(2)}) async-start(), calls=%async_computation.1 | async-start | bytes 9732096 | tf_op jit(solution)/shard_map/all_gather | solution.py:494
  34.9 228.3 %all-gather.5.cloned.1.call-start = ((), (), s32[]{:S(2)}) async-start(), calls=%async_computation.2 | async-start | bytes 9732096 | tf_op jit(solution)/shard_map/all_gather | solution.py:494
  36.6 15.9 %collective-permute-start.2 = (bf16[256,768]{1,0:T(8,128)(2,1)}, bf16[256,768]{1,0:T(8,128)(2,1)S(1)}, u32[]{:S(2)}, u32[]{:S(2)}) collective-permute-start(bf16[256,768]{1,0:T(8,128)(2,1)} %bitcast.460), channel_id=1, source_target_pairs={{0,6},{1,14},{2,8},{3,0},{4,2},{5,10},{6,12},{7,4},{8,7},{9,15},{1... | collective-permute-start | bytes 1179656 | tf_op jit(solution)/shard_map/ppermute | solution.py:507
  38.2 41.7 %collective-permute-start.3 = (bf16[256,768]{1,0:T(8,128)(2,1)}, bf16[256,768]{1,0:T(8,128)(2,1)S(1)}, u32[]{:S(2)}, u32[]{:S(2)}) collective-permute-start(bf16[256,768]{1,0:T(8,128)(2,1)} %bitcast.459), channel_id=1, source_target_pairs={{0,4},{1,12},{2,14},{3,6},{4,0},{5,8},{6,10},{7,2},{8,5},{9,13},{1... | collective-permute-start | bytes 1179656 | tf_op jit(solution)/shard_map/ppermute | solution.py:507
  39.4 41.2 %collective-permute-start.4 = (bf16[256,768]{1,0:T(8,128)(2,1)}, bf16[256,768]{1,0:T(8,128)(2,1)S(1)}, u32[]{:S(2)}, u32[]{:S(2)}) collective-permute-start(bf16[256,768]{1,0:T(8,128)(2,1)} %bitcast.458), channel_id=1, source_target_pairs={{0,2},{1,10},{2,12},{3,4},{4,6},{5,14},{6,8},{7,0},{8,3},{9,11},{1... | collective-permute-start | bytes 1179656 | tf_op jit(solution)/shard_map/ppermute | solution.py:507
  45.4 39.1 %collective-permute-start.9 = (bf16[4,24,3200]{2,1,0:T(8,128)(2,1)S(1)}, bf16[4,24,3200]{2,1,0:T(8,128)(2,1)S(1)}, u32[]{:S(2)}, u32[]{:S(2)}) collective-permute-start(bf16[4,24,3200]{2,1,0:T(8,128)(2,1)S(1)} %bitcast.389), channel_id=1, source_target_pairs={{0,1},{1,0},{2,3},{3,2},{4,5},{5,4},{6,7},{7,6},{8,9},{9,8},{10,11... | collective-permute-start | bytes 1843208 | tf_op jit(solution)/shard_map/ppermute | solution.py:395
  86.6 34.0 %collective-permute-start.10 = (bf16[4,2,24,3200]{3,2,1,0:T(8,128)(2,1)S(1)}, bf16[4,2,24,3200]{3,2,1,0:T(8,128)(2,1)}, u32[]{:S(2)}, u32[]{:S(2)}) collective-permute-start(bf16[4,2,24,3200]{3,2,1,0:T(8,128)(2,1)S(1)} %bitcast.384), channel_id=1, source_target_pairs={{0,16},{16,0},{1,17},{17,1},{2,18},{18,2},{3,19},{19,3},{4,20},{20... | collective-permute-start | bytes 3686408 | tf_op jit(solution)/shard_map/ppermute | solution.py:395
  91.7 23.7 %collective-permute-start.5 = (bf16[256,768]{1,0:T(8,128)(2,1)}, bf16[256,768]{1,0:T(8,128)(2,1)}, u32[]{:S(2)}, u32[]{:S(2)}) collective-permute-start(bf16[256,768]{1,0:T(8,128)(2,1)} %fusion.26), channel_id=1, source_target_pairs={{0,8},{8,0},{1,9},{9,1},{2,10},{10,2},{3,11},{11,3},{4,12},{12,4},... | collective-permute-start | bytes 1179656 | tf_op jit(solution)/shard_map/ppermute | solution.py:426
  92.1 19.2 %collective-permute-start.12 = (bf16[24,3072]{1,0:T(8,128)(2,1)S(1)}, bf16[24,3072]{1,0:T(8,128)(2,1)S(1)}, u32[]{:S(2)}, u32[]{:S(2)}) collective-permute-start(bf16[24,3072]{1,0:T(8,128)(2,1)S(1)} %pad_maximum_fusion.12), channel_id=1, source_target_pairs={{0,4},{2,6},{4,0},{6,2},{1,5},{3,7},{5,1},{7,3},{8,12},{10,14},{12... | collective-permute-start | bytes 442376 | tf_op jit(solution)/shard_map/ppermute | solution.py:395
  93.6 18.4 %collective-permute-start.13 = (bf16[24,3072]{1,0:T(8,128)(2,1)S(1)}, bf16[24,3072]{1,0:T(8,128)(2,1)S(1)}, u32[]{:S(2)}, u32[]{:S(2)}) collective-permute-start(bf16[24,3072]{1,0:T(8,128)(2,1)S(1)} %pad_maximum_fusion.12), channel_id=1, source_target_pairs={{0,2},{2,4},{4,6},{6,0},{1,3},{3,5},{5,7},{7,1},{8,10},{10,12},{12... | collective-permute-start | bytes 442376 | tf_op jit(solution)/shard_map/ppermute | solution.py:395
  130.6 16.5 %collective-permute-start.15 = (bf16[4,24,3072]{2,1,0:T(8,128)(2,1)S(1)}, bf16[4,24,3072]{2,1,0:T(8,128)(2,1)S(1)}, u32[]{:S(2)}, u32[]{:S(2)}) collective-permute-start(bf16[4,24,3072]{2,1,0:T(8,128)(2,1)S(1)} %bitcast.391), channel_id=1, source_target_pairs={{0,16},{16,0},{1,17},{17,1},{2,18},{18,2},{3,19},{19,3},{4,20},{20... | collective-permute-start | bytes 1769480 | tf_op jit(solution)/shard_map/ppermute | solution.py:395
  151.7 32.5 %collective-permute-start.16 = (bf16[2,4,24,3072]{3,2,1,0:T(8,128)(2,1)S(1)}, bf16[2,4,24,3072]{3,2,1,0:T(8,128)(2,1)S(1)}, u32[]{:S(2)}, u32[]{:S(2)}) collective-permute-start(bf16[2,4,24,3072]{3,2,1,0:T(8,128)(2,1)S(1)} %bitcast.386), channel_id=1, source_target_pairs={{0,1},{1,0},{2,3},{3,2},{4,5},{5,4},{6,7},{7,6},{8,9},{9,8},{10,11... | collective-permute-start | bytes 3538952 | tf_op jit(solution)/shard_map/ppermute | solution.py:395
  210.2 45.9 %collective-permute-start.21 = (bf16[256,768]{1,0:T(8,128)(2,1)S(1)}, bf16[256,768]{1,0:T(8,128)(2,1)S(1)}, u32[]{:S(2)}, u32[]{:S(2)}) collective-permute-start(bf16[256,768]{1,0:T(8,128)(2,1)S(1)} %get-tuple-element.351), channel_id=1, source_target_pairs={{0,0},{1,8},{2,10},{3,2},{4,4},{5,12},{6,14},{7,6},{8,1},{9,9},{10... | collective-permute-start | bytes 1179656 | tf_op jit(solution)/shard_map/ppermute | solution.py:507
  211.0 45.0 %collective-permute-start.22 = (bf16[256,768]{1,0:T(8,128)(2,1)S(1)}, bf16[256,768]{1,0:T(8,128)(2,1)S(1)}, u32[]{:S(2)}, u32[]{:S(2)}) collective-permute-start(bf16[256,768]{1,0:T(8,128)(2,1)S(1)} %get-tuple-element.350), channel_id=1, source_target_pairs={{0,6},{1,14},{2,8},{3,0},{4,2},{5,10},{6,12},{7,4},{8,7},{9,15},{1... | collective-permute-start | bytes 1179656 | tf_op jit(solution)/shard_map/ppermute | solution.py:507
  211.1 52.0 %collective-permute-start.23 = (bf16[256,768]{1,0:T(8,128)(2,1)S(1)}, bf16[256,768]{1,0:T(8,128)(2,1)S(1)}, u32[]{:S(2)}, u32[]{:S(2)}) collective-permute-start(bf16[256,768]{1,0:T(8,128)(2,1)S(1)} %get-tuple-element.349), channel_id=1, source_target_pairs={{0,4},{1,12},{2,14},{3,6},{4,0},{5,8},{6,10},{7,2},{8,5},{9,13},{1... | collective-permute-start | bytes 1179656 | tf_op jit(solution)/shard_map/ppermute | solution.py:507
  211.2 51.9 %collective-permute-start.24 = (bf16[256,768]{1,0:T(8,128)(2,1)S(1)}, bf16[256,768]{1,0:T(8,128)(2,1)S(1)}, u32[]{:S(2)}, u32[]{:S(2)}) collective-permute-start(bf16[256,768]{1,0:T(8,128)(2,1)S(1)} %get-tuple-element.348), channel_id=1, source_target_pairs={{0,2},{1,10},{2,12},{3,4},{4,6},{5,14},{6,8},{7,0},{8,3},{9,11},{1... | collective-permute-start | bytes 1179656 | tf_op jit(solution)/shard_map/ppermute | solution.py:507
  286.5 49.8 %collective-permute-start.20 = (bf16[2,256,768]{2,1,0:T(8,128)(2,1)}, bf16[2,256,768]{2,1,0:T(8,128)(2,1)S(1)}, u32[]{:S(2)}, u32[]{:S(2)}) collective-permute-start(bf16[2,256,768]{2,1,0:T(8,128)(2,1)} %get-tuple-element.353), channel_id=1, source_target_pairs={{8,0},{0,1},{9,8},{1,9},{10,2},{2,3},{11,10},{3,11},{12,4},{4,5},{... | collective-permute-start | bytes 2359304 | tf_op jit(solution)/shard_map/ppermute | solution.py:515
  288.2 48.2 %collective-permute-start.19 = (bf16[2,256,768]{2,1,0:T(8,128)(2,1)}, bf16[2,256,768]{2,1,0:T(8,128)(2,1)S(1)}, u32[]{:S(2)}, u32[]{:S(2)}) collective-permute-start(bf16[2,256,768]{2,1,0:T(8,128)(2,1)} %get-tuple-element.352), channel_id=1, source_target_pairs={{0,0},{8,1},{1,8},{9,9},{2,2},{10,3},{3,10},{11,11},{4,4},{12,5},{... | collective-permute-start | bytes 2359304 | tf_op jit(solution)/shard_map/ppermute | solution.py:515
  324.1 18.4 %collective-permute-start.25 = (bf16[2,4,2,24,3072]{4,3,1,2,0:T(8,128)(2,1)}, bf16[2,4,2,24,3072]{4,3,1,2,0:T(8,128)(2,1)}, u32[]{:S(2)}, u32[]{:S(2)}) collective-permute-start(bf16[2,4,2,24,3072]{4,3,1,2,0:T(8,128)(2,1)} %bitcast.349), channel_id=1, source_target_pairs={{0,8},{8,0},{1,9},{9,1},{2,10},{10,2},{3,11},{11,3},{4,12},{12,4},... | collective-permute-start | bytes 7077896 | tf_op jit(solution)/shard_map/ppermute | solution.py:426
  327.7 19.3 %collective-permute-start.26 = (bf16[2,4,2,24,3072]{4,3,1,0,2:T(8,128)(2,1)}, bf16[2,4,2,24,3072]{4,3,1,0,2:T(8,128)(2,1)}, u32[]{:S(2)}, u32[]{:S(2)}) collective-permute-start(bf16[2,4,2,24,3072]{4,3,1,0,2:T(8,128)(2,1)} %bitcast.348), channel_id=1, source_target_pairs={{0,8},{8,0},{1,9},{9,1},{2,10},{10,2},{3,11},{11,3},{4,12},{12,4},... | collective-permute-start | bytes 7077896 | tf_op jit(solution)/shard_map/ppermute | solution.py:426
  337.7 54.4 %all-to-all-start = ((bf16[4,256,768]{2,1,0:T(8,128)(2,1)}), bf16[4,256,768]{2,1,0:T(8,128)(2,1)}, u32[]{:S(2)}, u32[]{:S(2)}) async-start(bf16[4,256,768]{2,1,0:T(8,128)(2,1)} %bitcast.417), calls=%async_computation | async-start | bytes 3145728 | tf_op jit(solution)/shard_map/all_to_all | solution.py:497
  352.6 39.5 %collective-permute-start.27 = (bf16[4,2,24,3072]{3,2,0,1:T(8,128)(2,1)}, bf16[4,2,24,3072]{3,2,0,1:T(8,128)(2,1)}, u32[]{:S(2)}, u32[]{:S(2)}) collective-permute-start(bf16[4,2,24,3072]{3,2,0,1:T(8,128)(2,1)} %dynamic-slice_bitcast_fusion.5), channel_id=1, source_target_pairs={{0,16},{16,0},{1,17},{17,1},{2,18},{18,2},{3,19},{19,3},{4,20},{20... | collective-permute-start | bytes 3538952 | tf_op jit(solution)/shard_map/ppermute | solution.py:395
  354.1 40.4 %collective-permute-start.28 = (bf16[2,4,24,3072]{3,2,1,0:T(8,128)(2,1)}, bf16[2,4,24,3072]{3,2,1,0:T(8,128)(2,1)}, u32[]{:S(2)}, u32[]{:S(2)}) collective-permute-start(bf16[2,4,24,3072]{3,2,1,0:T(8,128)(2,1)} %dynamic-slice_bitcast_fusion.4), channel_id=1, source_target_pairs={{0,1},{1,0},{2,3},{3,2},{4,5},{5,4},{6,7},{7,6},{8,9},{9,8},{10,11... | collective-permute-start | bytes 3538952 | tf_op jit(solution)/shard_map/ppermute | solution.py:395
  391.0 29.7 %collective-permute-start.29 = (bf16[2,1024,512]{2,1,0:T(8,128)(2,1)}, bf16[2,1024,512]{2,1,0:T(8,128)(2,1)}, u32[]{:S(2)}, u32[]{:S(2)}) collective-permute-start(bf16[2,1024,512]{2,1,0:T(8,128)(2,1)} %get-tuple-element.125), channel_id=1, source_target_pairs={{0,8},{8,0},{1,9},{9,1},{2,10},{10,2},{3,11},{11,3},{4,12},{12,4},... | collective-permute-start | bytes 6291464 | tf_op jit(solution)/shard_map/ppermute | solution.py:426
  396.4 23.3 %collective-permute-start.36 = (bf16[4,24,3072]{2,1,0:T(8,128)(2,1)S(1)}, bf16[4,24,3072]{2,1,0:T(8,128)(2,1)S(1)}, u32[]{:S(2)}, u32[]{:S(2)}) collective-permute-start(bf16[4,24,3072]{2,1,0:T(8,128)(2,1)S(1)} %dynamic-slice_bitcast_fusion.21), channel_id=1, source_target_pairs={{0,1},{1,0},{2,3},{3,2},{4,5},{5,4},{6,7},{7,6},{8,9},{9,8},{10,11... | collective-permute-start | bytes 1769480 | tf_op jit(solution)/shard_map/ppermute | solution.py:395
  397.7 23.0 %collective-permute-start.37 = (bf16[4,24,3072]{2,1,0:T(8,128)(2,1)S(1)}, bf16[4,24,3072]{2,1,0:T(8,128)(2,1)S(1)}, u32[]{:S(2)}, u32[]{:S(2)}) collective-permute-start(bf16[4,24,3072]{2,1,0:T(8,128)(2,1)S(1)} %dynamic-slice_bitcast_fusion.20), channel_id=1, source_target_pairs={{0,16},{16,0},{1,17},{17,1},{2,18},{18,2},{3,19},{19,3},{4,20},{20... | collective-permute-start | bytes 1769480 | tf_op jit(solution)/shard_map/ppermute | solution.py:395
  444.6 40.3 %collective-permute-start.38 = (bf16[24,6144]{1,0:T(8,128)(2,1)}, bf16[24,6144]{1,0:T(8,128)(2,1)}, u32[]{:S(2)}, u32[]{:S(2)}) collective-permute-start(bf16[24,6144]{1,0:T(8,128)(2,1)} %get-tuple-element.359), channel_id=1, source_target_pairs={{0,6},{2,0},{4,2},{6,4},{1,7},{3,1},{5,3},{7,5},{8,14},{10,8},{12,... | collective-permute-start | bytes 884744 | tf_op jit(solution)/shard_map/ppermute | solution.py:395
  448.2 37.7 %collective-permute-start.39 = (bf16[24,6144]{1,0:T(8,128)(2,1)}, bf16[24,6144]{1,0:T(8,128)(2,1)}, u32[]{:S(2)}, u32[]{:S(2)}) collective-permute-start(bf16[24,6144]{1,0:T(8,128)(2,1)} %get-tuple-element.360), channel_id=1, source_target_pairs={{0,4},{2,6},{4,0},{6,2},{1,5},{3,7},{5,1},{7,3},{8,12},{10,14},{12... | collective-permute-start | bytes 884744 | tf_op jit(solution)/shard_map/ppermute | solution.py:395
  448.2 39.2 %collective-permute-start.40 = (bf16[24,6144]{1,0:T(8,128)(2,1)}, bf16[24,6144]{1,0:T(8,128)(2,1)}, u32[]{:S(2)}, u32[]{:S(2)}) collective-permute-start(bf16[24,6144]{1,0:T(8,128)(2,1)} %get-tuple-element.358), channel_id=1, source_target_pairs={{0,2},{2,4},{4,6},{6,0},{1,3},{3,5},{5,7},{7,1},{8,10},{10,12},{12... | collective-permute-start | bytes 884744 | tf_op jit(solution)/shard_map/ppermute | solution.py:395
  452.6 29.6 %collective-permute-start.35 = (bf16[2,4,24,1664]{3,2,1,0:T(8,128)(2,1)}, bf16[2,4,24,1664]{3,2,1,0:T(8,128)(2,1)}, u32[]{:S(2)}, u32[]{:S(2)}) collective-permute-start(bf16[2,4,24,1664]{3,2,1,0:T(8,128)(2,1)} %dynamic-slice_bitcast_fusion.7), channel_id=1, source_target_pairs={{0,1},{1,0},{2,3},{3,2},{4,5},{5,4},{6,7},{7,6},{8,9},{9,8},{10,11... | collective-permute-start | bytes 1916936 | tf_op jit(solution)/shard_map/ppermute | solution.py:395
  454.5 24.6 %collective-permute-start.34 = (bf16[4,2,24,1536]{3,2,1,0:T(8,128)(2,1)}, bf16[4,2,24,1536]{3,2,1,0:T(8,128)(2,1)}, u32[]{:S(2)}, u32[]{:S(2)}) collective-permute-start(bf16[4,2,24,1536]{3,2,1,0:T(8,128)(2,1)} %dynamic-slice_bitcast_fusion.15), channel_id=1, source_target_pairs={{0,16},{16,0},{1,17},{17,1},{2,18},{18,2},{3,19},{19,3},{4,20},{20... | collective-permute-start | bytes 1769480 | tf_op jit(solution)/shard_map/ppermute | solution.py:395
  479.1 43.2 %collective-permute-start.42 = (bf16[2,4,24,3072]{3,2,1,0:T(8,128)(2,1)}, bf16[2,4,24,3072]{3,2,1,0:T(8,128)(2,1)}, u32[]{:S(2)}, u32[]{:S(2)}) collective-permute-start(bf16[2,4,24,3072]{3,2,1,0:T(8,128)(2,1)} %dynamic-slice_bitcast_fusion), channel_id=1, source_target_pairs={{0,1},{1,0},{2,3},{3,2},{4,5},{5,4},{6,7},{7,6},{8,9},{9,8},{10,11... | collective-permute-start | bytes 3538952 | tf_op jit(solution)/shard_map/ppermute | solution.py:395
  482.3 42.4 %collective-permute-start.33 = (bf16[4,2,24,3072]{3,2,1,0:T(8,128)(2,1)}, bf16[4,2,24,3072]{3,2,1,0:T(8,128)(2,1)}, u32[]{:S(2)}, u32[]{:S(2)}) collective-permute-start(bf16[4,2,24,3072]{3,2,1,0:T(8,128)(2,1)} %dynamic-slice_bitcast_fusion.1), channel_id=1, source_target_pairs={{0,16},{16,0},{1,17},{17,1},{2,18},{18,2},{3,19},{19,3},{4,20},{20... | collective-permute-start | bytes 3538952 | tf_op jit(solution)/shard_map/ppermute | solution.py:395
  484.9 28.2 %collective-permute-start.44 = (bf16[4,24,1536]{2,1,0:T(8,128)(2,1)}, bf16[4,24,1536]{2,1,0:T(8,128)(2,1)}, u32[]{:S(2)}, u32[]{:S(2)}) collective-permute-start(bf16[4,24,1536]{2,1,0:T(8,128)(2,1)} %dynamic-slice_bitcast_fusion.32), channel_id=1, source_target_pairs={{0,1},{1,0},{2,3},{3,2},{4,5},{5,4},{6,7},{7,6},{8,9},{9,8},{10,11... | collective-permute-start | bytes 884744 | tf_op jit(solution)/shard_map/ppermute | solution.py:395
  486.0 31.4 %collective-permute-start.45 = (bf16[4,24,1664]{2,1,0:T(8,128)(2,1)}, bf16[4,24,1664]{2,1,0:T(8,128)(2,1)}, u32[]{:S(2)}, u32[]{:S(2)}) collective-permute-start(bf16[4,24,1664]{2,1,0:T(8,128)(2,1)} %dynamic-slice_bitcast_fusion.30), channel_id=1, source_target_pairs={{0,16},{16,0},{1,17},{17,1},{2,18},{18,2},{3,19},{19,3},{4,20},{20... | collective-permute-start | bytes 958472 | tf_op jit(solution)/shard_map/ppermute | solution.py:395
  505.4 59.2 %collective-permute-start.46 = (bf16[256,768]{1,0:T(8,128)(2,1)S(1)}, bf16[256,768]{1,0:T(8,128)(2,1)S(1)}, u32[]{:S(2)}, u32[]{:S(2)}) collective-permute-start(bf16[256,768]{1,0:T(8,128)(2,1)S(1)} %get-tuple-element.347), channel_id=1, source_target_pairs={{0,0},{8,1},{10,2},{2,3},{4,4},{12,5},{14,6},{6,7},{1,8},{9,9},{11... | collective-permute-start | bytes 1179656 | tf_op jit(solution)/shard_map/ppermute | solution.py:527
  513.1 53.6 %collective-permute-start.47 = (bf16[256,768]{1,0:T(8,128)(2,1)S(1)}, bf16[256,768]{1,0:T(8,128)(2,1)S(1)}, u32[]{:S(2)}, u32[]{:S(2)}) collective-permute-start(bf16[256,768]{1,0:T(8,128)(2,1)S(1)} %get-tuple-element.346), channel_id=1, source_target_pairs={{2,0},{10,1},{12,2},{4,3},{6,4},{14,5},{8,6},{0,7},{3,8},{11,9},{1... | collective-permute-start | bytes 1179656 | tf_op jit(solution)/shard_map/ppermute | solution.py:527
  517.4 49.3 %collective-permute-start.48 = (bf16[256,768]{1,0:T(8,128)(2,1)S(1)}, bf16[256,768]{1,0:T(8,128)(2,1)S(1)}, u32[]{:S(2)}, u32[]{:S(2)}) collective-permute-start(bf16[256,768]{1,0:T(8,128)(2,1)S(1)} %get-tuple-element.345), channel_id=1, source_target_pairs={{4,0},{12,1},{14,2},{6,3},{0,4},{8,5},{10,6},{2,7},{5,8},{13,9},{1... | collective-permute-start | bytes 1179656 | tf_op jit(solution)/shard_map/ppermute | solution.py:527
  522.3 44.5 %collective-permute-start.49 = (bf16[256,768]{1,0:T(8,128)(2,1)S(1)}, bf16[256,768]{1,0:T(8,128)(2,1)S(1)}, u32[]{:S(2)}, u32[]{:S(2)}) collective-permute-start(bf16[256,768]{1,0:T(8,128)(2,1)S(1)} %get-tuple-element.344), channel_id=1, source_target_pairs={{6,0},{14,1},{8,2},{0,3},{2,4},{10,5},{12,6},{4,7},{7,8},{15,9},{9... | collective-permute-start | bytes 1179656 | tf_op jit(solution)/shard_map/ppermute | solution.py:527
  540.1 18.8 %collective-permute-start.41 = (bf16[4,24,3072]{2,1,0:T(8,128)(2,1)S(1)}, bf16[4,24,3072]{2,1,0:T(8,128)(2,1)S(1)}, u32[]{:S(2)}, u32[]{:S(2)}) collective-permute-start(bf16[4,24,3072]{2,1,0:T(8,128)(2,1)S(1)} %dynamic-slice_bitcast_fusion.14), channel_id=1, source_target_pairs={{0,1},{1,0},{2,3},{3,2},{4,5},{5,4},{6,7},{7,6},{8,9},{9,8},{10,11... | collective-permute-start | bytes 1769480 | tf_op jit(solution)/shard_map/ppermute | solution.py:395
  558.9 15.8 %collective-permute-start.51 = (bf16[4,2,24,1536]{3,2,1,0:T(8,128)(2,1)S(1)}, bf16[4,2,24,1536]{3,2,1,0:T(8,128)(2,1)S(1)}, u32[]{:S(2)}, u32[]{:S(2)}) collective-permute-start(bf16[4,2,24,1536]{3,2,1,0:T(8,128)(2,1)S(1)} %dynamic-slice_bitcast_fusion.10), channel_id=1, source_target_pairs={{0,16},{16,0},{1,17},{17,1},{2,18},{18,2},{3,19},{19,3},{4,20},{20... | collective-permute-start | bytes 1769480 | tf_op jit(solution)/shard_map/ppermute | solution.py:395
  564.6 25.2 %collective-permute-start.53 = (bf16[2,4,24,1664]{3,2,1,0:T(8,128)(2,1)}, bf16[2,4,24,1664]{3,2,1,0:T(8,128)(2,1)}, u32[]{:S(2)}, u32[]{:S(2)}) collective-permute-start(bf16[2,4,24,1664]{3,2,1,0:T(8,128)(2,1)} %dynamic-slice_bitcast_fusion.6), channel_id=1, source_target_pairs={{0,1},{1,0},{2,3},{3,2},{4,5},{5,4},{6,7},{7,6},{8,9},{9,8},{10,11... | collective-permute-start | bytes 1916936 | tf_op jit(solution)/shard_map/ppermute | solution.py:395
  566.7 34.5 %collective-permute-start.56 = (bf16[24,9344]{1,0:T(8,128)(2,1)}, bf16[24,9344]{1,0:T(8,128)(2,1)}, u32[]{:S(2)}, u32[]{:S(2)}) collective-permute-start(bf16[24,9344]{1,0:T(8,128)(2,1)} %get-tuple-element.341), channel_id=1, source_target_pairs={{0,2},{2,4},{4,6},{6,0},{1,3},{3,5},{5,7},{7,1},{8,10},{10,12},{12... | collective-permute-start | bytes 1345544 | tf_op jit(solution)/shard_map/ppermute | solution.py:395
  566.7 37.6 %collective-permute-start.55 = (bf16[24,9344]{1,0:T(8,128)(2,1)}, bf16[24,9344]{1,0:T(8,128)(2,1)}, u32[]{:S(2)}, u32[]{:S(2)}) collective-permute-start(bf16[24,9344]{1,0:T(8,128)(2,1)} %get-tuple-element.342), channel_id=1, source_target_pairs={{0,4},{2,6},{4,0},{6,2},{1,5},{3,7},{5,1},{7,3},{8,12},{10,14},{12... | collective-permute-start | bytes 1345544 | tf_op jit(solution)/shard_map/ppermute | solution.py:395
  566.8 37.5 %collective-permute-start.50 = (bf16[24,9344]{1,0:T(8,128)(2,1)}, bf16[24,9344]{1,0:T(8,128)(2,1)}, u32[]{:S(2)}, u32[]{:S(2)}) collective-permute-start(bf16[24,9344]{1,0:T(8,128)(2,1)} %get-tuple-element.343), channel_id=1, source_target_pairs={{0,6},{2,0},{4,2},{6,4},{1,7},{3,1},{5,3},{7,5},{8,14},{10,8},{12,... | collective-permute-start | bytes 1345544 | tf_op jit(solution)/shard_map/ppermute | solution.py:395
  575.6 16.7 %collective-permute-start.52 = (bf16[4,24,1536]{2,1,0:T(8,128)(2,1)}, bf16[4,24,1536]{2,1,0:T(8,128)(2,1)}, u32[]{:S(2)}, u32[]{:S(2)}) collective-permute-start(bf16[4,24,1536]{2,1,0:T(8,128)(2,1)} %dynamic-slice_bitcast_fusion.31), channel_id=1, source_target_pairs={{0,1},{1,0},{2,3},{3,2},{4,5},{5,4},{6,7},{7,6},{8,9},{9,8},{10,11... | collective-permute-start | bytes 884744 | tf_op jit(solution)/shard_map/ppermute | solution.py:395
  599.9 18.9 %collective-permute-start.58 = (bf16[24,3200]{1,0:T(8,128)(2,1)}, bf16[24,3200]{1,0:T(8,128)(2,1)}, u32[]{:S(2)}, u32[]{:S(2)}) collective-permute-start(bf16[24,3200]{1,0:T(8,128)(2,1)} %get-tuple-element.374), channel_id=1, source_target_pairs={{0,4},{2,6},{4,0},{6,2},{1,5},{3,7},{5,1},{7,3},{8,12},{10,14},{12... | collective-permute-start | bytes 460808 | tf_op jit(solution)/shard_map/ppermute | solution.py:395
  601.2 17.6 %collective-permute-start.57 = (bf16[24,3200]{1,0:T(8,128)(2,1)}, bf16[24,3200]{1,0:T(8,128)(2,1)}, u32[]{:S(2)}, u32[]{:S(2)}) collective-permute-start(bf16[24,3200]{1,0:T(8,128)(2,1)} %get-tuple-element.373), channel_id=1, source_target_pairs={{0,6},{2,0},{4,2},{6,4},{1,7},{3,1},{5,3},{7,5},{8,14},{10,8},{12,... | collective-permute-start | bytes 460808 | tf_op jit(solution)/shard_map/ppermute | solution.py:395
  (165 other events, 1542.0 us)
Sparse Core Ops, SparseCore 0:
  35.0 110.6 all-gather.2
  149.2 112.9 all-gather.4

commit v4 on v3

--- a/solution.py
+++ b/solution.py
@@ -165,7 +165,7 @@
         d_far[1] = afv[...].astype(BF)
 
 
-def attend_back(q, do, o, lse, k_own, v_own, far, core, lb, first, count, kc=512):
+def attend_back(q, do, o, lse, k_own, v_own, far, core, lb, first, count, kc=1024):
     rows = do[0].shape[0]
 
     def spec(off):

time: 679 us -> 678 us (level)
  no operation moved by 1% of the time
where the time goes in v4:
time: 678 us; the launch traced here: 669 us
  Pallas kernels  165 us (24%)
  waiting for transfers between devices  154 us (23%)
  local copies, waits for them, and re-layouts  111 us (16%)
  starting transfers between devices  104 us (15%)
  other arithmetic  67.7 us (10%)
  matrix products  43.2 us (6%)
  between operations  24.6 us (4%)
    ppermute x41, waiting for transfers between devices, ahead(): lax.ppermute(value, axis, [(i, (i - step) % size) for i in range(size)])  116 us
    ppermute x41, starting transfers between devices, ahead(): lax.ppermute(value, axis, [(i, (i - step) % size) for i in range(size)])  65.7 us
    pallas_call x3, Pallas kernels, attend_back(): pl.pallas_call(functools.partial(attend_back_kernel, lb if far else 0, kc...  58.3 us
    dot_general x22, matrix products, dotf(): return lax.dot_general(left, right, dims, preferred_element_type=F32)  43.2 us
    unnamed x300, local copies, waits for them, and re-layouts  41.3 us
    pallas_call x2, Pallas kernels, mlp_backward(): pl.pallas_call(mlp_back_kernel, grid=(FF // wide,), in_specs=[whole, whol...  39.5 us
    pallas_call x2, Pallas kernels, attend(): pl.pallas_call(functools.partial(attend_kernel, lb if far else 0), grid=(...  37.4 us
    ppermute x8, waiting for transfers between devices, come(): lax.ppermute(p, every[1:], route)  37 us
  transfers between devices with their start and end apart: 70, of which 19 were waited for; matrix products, arithmetic and copies ran while one was open for 23% of the time, Pallas kernels for 22%

profile of v4, /device:TPU:0, one launch (start us, length us, event | category | flops | bytes accessed | tf_op | source)
XLA Modules:
  0.0 668.6 jit_solution(463956423651438694)
XLA Ops:
  10.1 3.3 constant_dynamic-slice_fusion.10
  16.7 5.1 collective-permute-start.6
  27.1 7.7 %collective-permute-done.7 = bf16[24,3200]{1,0:T(8,128)(2,1)S(1)} collective-permute-done((bf16[24,3200]{1,0:T(8,128)(2,1)S(1)}, bf16[24,3200]{1,0:T(8,128)(2,1)S(1)}, u32[]{:S(2)}, u32[]{:S(2)}) %collective-permute-start.7) | collective-permute-done | bytes 153632 | tf_op jit(solution)/shard_map/ppermute | solution.py:395
  49.2 3.3 collective-permute-done.2
  53.2 26.7 %collective-permute-done.3 = bf16[256,768]{1,0:T(8,128)(2,1)S(1)} collective-permute-done((bf16[256,768]{1,0:T(8,128)(2,1)}, bf16[256,768]{1,0:T(8,128)(2,1)S(1)}, u32[]{:S(2)}, u32[]{:S(2)}) %collective-permute-start.3) | collective-permute-done | bytes 393248 | tf_op jit(solution)/shard_map/ppermute | solution.py:507
  96.1 4.3 collective-permute-done.11
  101.0 10.3 %collective-permute-done.12 = bf16[24,3072]{1,0:T(8,128)(2,1)S(1)} collective-permute-done((bf16[24,3072]{1,0:T(8,128)(2,1)S(1)}, bf16[24,3072]{1,0:T(8,128)(2,1)S(1)}, u32[]{:S(2)}, u32[]{:S(2)}) %collective-permute-start.12) | collective-permute-done | bytes 147488 | tf_op jit(solution)/shard_map/ppermute | solution.py:395
  117.4 3.2 collective-permute-done.10
  123.4 4.3 collective-permute-done.14
  133.3 13.9 %collective-permute-done.15 = bf16[4,24,3072]{2,1,0:T(8,128)(2,1)S(1)} collective-permute-done((bf16[4,24,3072]{2,1,0:T(8,128)(2,1)S(1)}, bf16[4,24,3072]{2,1,0:T(8,128)(2,1)S(1)}, u32[]{:S(2)}, u32[]{:S(2)}) %collective-permute-start.15) | collective-permute-done | bytes 589856 | tf_op jit(solution)/shard_map/ppermute | solution.py:395
  155.5 5.5 attend_own.1
  164.0 20.1 %collective-permute-done.16 = bf16[2,4,24,3072]{3,2,1,0:T(8,128)(2,1)S(1)} collective-permute-done((bf16[2,4,24,3072]{3,2,1,0:T(8,128)(2,1)S(1)}, bf16[2,4,24,3072]{3,2,1,0:T(8,128)(2,1)S(1)}, u32[]{:S(2)}, u32[]{:S(2)}) %collective-permute-start.16) | collective-permute-done | bytes 1179680 | tf_op jit(solution)/shard_map/ppermute | solution.py:395
  184.6 4.5 collective-permute-done.17
  191.9 7.8 %mlp_forward.2 = (bf16[256,3072]{1,0:T(8,128)(2,1)}, bf16[256,3072]{1,0:T(8,128)(2,1)}, f32[256,768]{1,0:T(8,128)}) custom-call(bf16[256,768]{1,0:T(8,128)(2,1)} %multiply_convert_fusion.4.n2_ref, bf16[768,6144]{1,0:T(8,128)(2,1)} %all-gather.3.cloned.1.call-done.up_ref.down_ref, bf16[768,6144]{1,0:T(8,128)(2,1)} %all-gather.3.cloned.1.call-done.up_ref.down_ref), custom_call_target="tpu_custom_call" | custom-call | flops 2415919104 | bytes 13762560 | tf_op jit(solution)/shard_map/mlp_forward/pallas_call | solution.py:262
  203.9 2.8 convolution_convert_fusion.refs_1_.refs_2_.refs_4_.refs_5_
  211.2 5.2 collective-permute-start.24
  219.1 31.9 %attend_far.1 = (bf16[1024,768]{1,0:T(8,128)(2,1)S(1)}, f32[6,2,1024]{2,1,0:T(2,128)S(1)}) custom-call(s32[1]{0:T(128)} %bitcast.13.start_ref.core_ref, bf16[1024,768]{1,0:T(8,128)(2,1)S(1)} %convolution_convert_fusion.5.refs_0_, bf16[1024,1536]{1,0:T(8,128)(2,1)S(1)} %copy-done.19, bf16[1024,1536]{1,0:T(8,128)(2,1)S(1)} %copy-done.19, ...), custom_call_target="tpu_custom_call" | custom-call | flops 19327352832 | bytes 9437184 | tf_op jit(solution)/shard_map/attend_far/pallas_call | solution.py:93
  256.1 7.0 %collective-permute-done.23 = bf16[256,768]{1,0:T(8,128)(2,1)S(1)} collective-permute-done((bf16[256,768]{1,0:T(8,128)(2,1)S(1)}, bf16[256,768]{1,0:T(8,128)(2,1)S(1)}, u32[]{:S(2)}, u32[]{:S(2)}) %collective-permute-start.23) | collective-permute-done | bytes 393248 | tf_op jit(solution)/shard_map/ppermute | solution.py:507
  263.2 18.3 %mlp_forward.3 = (bf16[1024,3072]{1,0:T(8,128)(2,1)}, bf16[1024,3072]{1,0:T(8,128)(2,1)}, f32[1024,768]{1,0:T(8,128)}) custom-call(bf16[1024,768]{1,0:T(8,128)(2,1)} %multiply_convert_fusion.1.n2_ref, bf16[768,6144]{1,0:T(8,128)(2,1)} %all-gather.5.cloned.1.call-done.up_ref.down_ref, bf16[768,6144]{1,0:T(8,128)(2,1)} %all-gather.5.cloned.1.call-done.up_ref.down_ref), custom_call_target="tpu_custom_call" | custom-call | flops 9663676416 | bytes 26738688 | tf_op jit(solution)/shard_map/mlp_forward/pallas_call | solution.py:262
  281.5 3.7 fusion.3
  290.1 28.0 %mlp_backward.2 = (bf16[768,3072]{1,0:T(8,128)(2,1)}, bf16[768,3072]{1,0:T(8,128)(2,1)}, f32[1024,768]{1,0:T(8,128)}) custom-call(bf16[1024,768]{1,0:T(8,128)(2,1)} %get-tuple-element.110.dm_ref, bf16[1024,768]{1,0:T(8,128)(2,1)} %multiply_convert_fusion.1.n2_ref, bf16[1024,3072]{1,0:T(8,128)(2,1)} %get-tuple-element.111.act_ref, ...), custom_call_target="tpu_custom_call" | custom-call | flops 19327352832 | bytes 37748736 | tf_op jit(solution)/shard_map/mlp_backward/pallas_call | solution.py:307
  318.2 4.3 constant_dynamic-slice_fusion.9
  337.7 4.8 all-to-all-start
  342.5 3.3 fusion.1
  354.9 35.2 %attend_back_far.2 = (bf16[1024,512]{1,0:T(8,128)(2,1)S(1)}, f32[2,1024,512]{2,1,0:T(8,128)}, bf16[2,1024,512]{2,1,0:T(8,128)(2,1)}) custom-call(s32[1]{0:T(128)} %bitcast.13.start_ref.core_ref, bf16[1024,768]{1,0:T(8,128)(2,1)S(1)} %copy-done.27, bf16[1024,768]{1,0:T(8,128)(2,1)S(1)} %convolution_convert_fusion.4.refs_1_, ...), custom_call_target="tpu_custom_call" | custom-call | flops 26843545600 | bytes 18874368 | tf_op jit(solution)/shard_map/attend_back_far/pallas_call | solution.py:185
  397.5 18.1 %attend_back_far.3 = (bf16[1024,256]{1,0:T(8,128)(2,1)S(1)}, f32[2,1024,256]{2,1,0:T(8,128)S(1)}, bf16[2,1024,256]{2,1,0:T(8,128)(2,1)S(1)}) custom-call(s32[1]{0:T(128)} %bitcast.13.start_ref.core_ref, bf16[1024,768]{1,0:T(8,128)(2,1)S(1)} %copy-done.28, bf16[1024,768]{1,0:T(8,128)(2,1)S(1)} %convolution_convert_fusion.4.refs_1_, ...), custom_call_target="tpu_custom_call" | custom-call | flops 13421772800 | bytes 18874368 | tf_op jit(solution)/shard_map/attend_back_far/pallas_call | solution.py:185
  426.5 4.6 convolution_convert_fusion.1
  431.0 3.4 multiply_reduce_fusion.2
  443.2 3.7 collective-permute-start.38
  454.6 11.4 %mlp_backward.3 = (bf16[768,3072]{1,0:T(8,128)(2,1)}, bf16[768,3072]{1,0:T(8,128)(2,1)}, f32[256,768]{1,0:T(8,128)}) custom-call(bf16[256,768]{1,0:T(8,128)(2,1)} %fusion.54.dm_ref, bf16[256,768]{1,0:T(8,128)(2,1)} %multiply_convert_fusion.4.n2_ref, bf16[256,3072]{1,0:T(8,128)(2,1)} %get-tuple-element.129.act_ref, ...), custom_call_target="tpu_custom_call" | custom-call | flops 4831838208 | bytes 23592960 | tf_op jit(solution)/shard_map/mlp_backward/pallas_call | solution.py:307
  486.1 5.0 attend_back_own.1
  507.3 4.4 collective-permute-done.44
  511.7 3.2 collective-permute-start.47
  516.0 3.8 collective-permute-start.48
  526.9 11.8 %collective-permute-done.43 = bf16[4,24,3072]{2,1,0:T(8,128)(2,1)S(1)} collective-permute-done((bf16[4,24,3072]{2,1,0:T(8,128)(2,1)S(1)}, bf16[4,24,3072]{2,1,0:T(8,128)(2,1)S(1)}, u32[]{:S(2)}, u32[]{:S(2)}) %collective-permute-start.43) | collective-permute-done | bytes 589856 | tf_op jit(solution)/shard_map/ppermute | solution.py:395
  538.8 18.6 %collective-permute-done.41 = bf16[4,24,3072]{2,1,0:T(8,128)(2,1)S(1)} collective-permute-done((bf16[4,24,3072]{2,1,0:T(8,128)(2,1)S(1)}, bf16[4,24,3072]{2,1,0:T(8,128)(2,1)S(1)}, u32[]{:S(2)}, u32[]{:S(2)}) %collective-permute-start.41) | collective-permute-done | bytes 589856 | tf_op jit(solution)/shard_map/ppermute | solution.py:395
  559.4 3.8 copy.345
  565.4 3.8 collective-permute-start.50
  569.6 3.7 copy.346
  582.5 4.1 stack_reshape.13
  591.9 5.6 collective-permute-done.54
  599.8 3.1 collective-permute-start.57
  613.8 3.6 collective-permute-done.58
  623.8 3.1 collective-permute-start.62
  629.1 2.8 collective-permute-start.63
  633.3 9.4 %collective-permute-start.64 = (f32[1,1]{1,0:T(1,128)}, f32[1,1]{1,0:T(1,128)}, u32[]{:S(2)}, u32[]{:S(2)}) collective-permute-start(f32[1,1]{1,0:T(1,128)} %add.701), channel_id=1, source_target_pairs={{0,6},{2,0},{4,2},{6,4},{1,7},{3,1},{5,3},{7,5},{8,14},{10,8},{12,... | collective-permute-start | bytes 20 | tf_op jit(solution)/shard_map/ppermute | solution.py:395
  642.7 2.9 collective-permute-start.65
  648.1 2.8 collective-permute-done.66
  (604 shorter events, 242.7 us)
Async XLA Ops:
  7.2 184.7 %all-gather.3.cloned.1.call-start = ((), (), s32[]{:S(2)}) async-start(), calls=%async_computation.1 | async-start | bytes 9732096 | tf_op jit(solution)/shard_map/all_gather | solution.py:494
  34.9 228.3 %all-gather.5.cloned.1.call-start = ((), (), s32[]{:S(2)}) async-start(), calls=%async_computation.2 | async-start | bytes 9732096 | tf_op jit(solution)/shard_map/all_gather | solution.py:494
  36.6 15.9 %collective-permute-start.2 = (bf16[256,768]{1,0:T(8,128)(2,1)}, bf16[256,768]{1,0:T(8,128)(2,1)S(1)}, u32[]{:S(2)}, u32[]{:S(2)}) collective-permute-start(bf16[256,768]{1,0:T(8,128)(2,1)} %bitcast.460), channel_id=1, source_target_pairs={{0,6},{1,14},{2,8},{3,0},{4,2},{5,10},{6,12},{7,4},{8,7},{9,15},{1... | collective-permute-start | bytes 1179656 | tf_op jit(solution)/shard_map/ppermute | solution.py:507
  38.2 41.7 %collective-permute-start.3 = (bf16[256,768]{1,0:T(8,128)(2,1)}, bf16[256,768]{1,0:T(8,128)(2,1)S(1)}, u32[]{:S(2)}, u32[]{:S(2)}) collective-permute-start(bf16[256,768]{1,0:T(8,128)(2,1)} %bitcast.459), channel_id=1, source_target_pairs={{0,4},{1,12},{2,14},{3,6},{4,0},{5,8},{6,10},{7,2},{8,5},{9,13},{1... | collective-permute-start | bytes 1179656 | tf_op jit(solution)/shard_map/ppermute | solution.py:507
  39.4 41.2 %collective-permute-start.4 = (bf16[256,768]{1,0:T(8,128)(2,1)}, bf16[256,768]{1,0:T(8,128)(2,1)S(1)}, u32[]{:S(2)}, u32[]{:S(2)}) collective-permute-start(bf16[256,768]{1,0:T(8,128)(2,1)} %bitcast.458), channel_id=1, source_target_pairs={{0,2},{1,10},{2,12},{3,4},{4,6},{5,14},{6,8},{7,0},{8,3},{9,11},{1... | collective-permute-start | bytes 1179656 | tf_op jit(solution)/shard_map/ppermute | solution.py:507
  45.4 39.1 %collective-permute-start.9 = (bf16[4,24,3200]{2,1,0:T(8,128)(2,1)S(1)}, bf16[4,24,3200]{2,1,0:T(8,128)(2,1)S(1)}, u32[]{:S(2)}, u32[]{:S(2)}) collective-permute-start(bf16[4,24,3200]{2,1,0:T(8,128)(2,1)S(1)} %bitcast.389), channel_id=1, source_target_pairs={{0,1},{1,0},{2,3},{3,2},{4,5},{5,4},{6,7},{7,6},{8,9},{9,8},{10,11... | collective-permute-start | bytes 1843208 | tf_op jit(solution)/shard_map/ppermute | solution.py:395
  86.6 34.0 %collective-permute-start.10 = (bf16[4,2,24,3200]{3,2,1,0:T(8,128)(2,1)S(1)}, bf16[4,2,24,3200]{3,2,1,0:T(8,128)(2,1)}, u32[]{:S(2)}, u32[]{:S(2)}) collective-permute-start(bf16[4,2,24,3200]{3,2,1,0:T(8,128)(2,1)S(1)} %bitcast.384), channel_id=1, source_target_pairs={{0,16},{16,0},{1,17},{17,1},{2,18},{18,2},{3,19},{19,3},{4,20},{20... | collective-permute-start | bytes 3686408 | tf_op jit(solution)/shard_map/ppermute | solution.py:395
  91.7 23.7 %collective-permute-start.5 = (bf16[256,768]{1,0:T(8,128)(2,1)}, bf16[256,768]{1,0:T(8,128)(2,1)}, u32[]{:S(2)}, u32[]{:S(2)}) collective-permute-start(bf16[256,768]{1,0:T(8,128)(2,1)} %fusion.26), channel_id=1, source_target_pairs={{0,8},{8,0},{1,9},{9,1},{2,10},{10,2},{3,11},{11,3},{4,12},{12,4},... | collective-permute-start | bytes 1179656 | tf_op jit(solution)/shard_map/ppermute | solution.py:426
  92.1 19.2 %collective-permute-start.12 = (bf16[24,3072]{1,0:T(8,128)(2,1)S(1)}, bf16[24,3072]{1,0:T(8,128)(2,1)S(1)}, u32[]{:S(2)}, u32[]{:S(2)}) collective-permute-start(bf16[24,3072]{1,0:T(8,128)(2,1)S(1)} %pad_maximum_fusion.12), channel_id=1, source_target_pairs={{0,4},{2,6},{4,0},{6,2},{1,5},{3,7},{5,1},{7,3},{8,12},{10,14},{12... | collective-permute-start | bytes 442376 | tf_op jit(solution)/shard_map/ppermute | solution.py:395
  93.6 18.4 %collective-permute-start.13 = (bf16[24,3072]{1,0:T(8,128)(2,1)S(1)}, bf16[24,3072]{1,0:T(8,128)(2,1)S(1)}, u32[]{:S(2)}, u32[]{:S(2)}) collective-permute-start(bf16[24,3072]{1,0:T(8,128)(2,1)S(1)} %pad_maximum_fusion.12), channel_id=1, source_target_pairs={{0,2},{2,4},{4,6},{6,0},{1,3},{3,5},{5,7},{7,1},{8,10},{10,12},{12... | collective-permute-start | bytes 442376 | tf_op jit(solution)/shard_map/ppermute | solution.py:395
  130.6 16.5 %collective-permute-start.15 = (bf16[4,24,3072]{2,1,0:T(8,128)(2,1)S(1)}, bf16[4,24,3072]{2,1,0:T(8,128)(2,1)S(1)}, u32[]{:S(2)}, u32[]{:S(2)}) collective-permute-start(bf16[4,24,3072]{2,1,0:T(8,128)(2,1)S(1)} %bitcast.391), channel_id=1, source_target_pairs={{0,16},{16,0},{1,17},{17,1},{2,18},{18,2},{3,19},{19,3},{4,20},{20... | collective-permute-start | bytes 1769480 | tf_op jit(solution)/shard_map/ppermute | solution.py:395
  151.7 32.5 %collective-permute-start.16 = (bf16[2,4,24,3072]{3,2,1,0:T(8,128)(2,1)S(1)}, bf16[2,4,24,3072]{3,2,1,0:T(8,128)(2,1)S(1)}, u32[]{:S(2)}, u32[]{:S(2)}) collective-permute-start(bf16[2,4,24,3072]{3,2,1,0:T(8,128)(2,1)S(1)} %bitcast.386), channel_id=1, source_target_pairs={{0,1},{1,0},{2,3},{3,2},{4,5},{5,4},{6,7},{7,6},{8,9},{9,8},{10,11... | collective-permute-start | bytes 3538952 | tf_op jit(solution)/shard_map/ppermute | solution.py:395
  210.2 45.9 %collective-permute-start.21 = (bf16[256,768]{1,0:T(8,128)(2,1)S(1)}, bf16[256,768]{1,0:T(8,128)(2,1)S(1)}, u32[]{:S(2)}, u32[]{:S(2)}) collective-permute-start(bf16[256,768]{1,0:T(8,128)(2,1)S(1)} %get-tuple-element.351), channel_id=1, source_target_pairs={{0,0},{1,8},{2,10},{3,2},{4,4},{5,12},{6,14},{7,6},{8,1},{9,9},{10... | collective-permute-start | bytes 1179656 | tf_op jit(solution)/shard_map/ppermute | solution.py:507
  211.0 45.0 %collective-permute-start.22 = (bf16[256,768]{1,0:T(8,128)(2,1)S(1)}, bf16[256,768]{1,0:T(8,128)(2,1)S(1)}, u32[]{:S(2)}, u32[]{:S(2)}) collective-permute-start(bf16[256,768]{1,0:T(8,128)(2,1)S(1)} %get-tuple-element.350), channel_id=1, source_target_pairs={{0,6},{1,14},{2,8},{3,0},{4,2},{5,10},{6,12},{7,4},{8,7},{9,15},{1... | collective-permute-start | bytes 1179656 | tf_op jit(solution)/shard_map/ppermute | solution.py:507
  211.1 52.0 %collective-permute-start.23 = (bf16[256,768]{1,0:T(8,128)(2,1)S(1)}, bf16[256,768]{1,0:T(8,128)(2,1)S(1)}, u32[]{:S(2)}, u32[]{:S(2)}) collective-permute-start(bf16[256,768]{1,0:T(8,128)(2,1)S(1)} %get-tuple-element.349), channel_id=1, source_target_pairs={{0,4},{1,12},{2,14},{3,6},{4,0},{5,8},{6,10},{7,2},{8,5},{9,13},{1... | collective-permute-start | bytes 1179656 | tf_op jit(solution)/shard_map/ppermute | solution.py:507
  211.2 51.9 %collective-permute-start.24 = (bf16[256,768]{1,0:T(8,128)(2,1)S(1)}, bf16[256,768]{1,0:T(8,128)(2,1)S(1)}, u32[]{:S(2)}, u32[]{:S(2)}) collective-permute-start(bf16[256,768]{1,0:T(8,128)(2,1)S(1)} %get-tuple-element.348), channel_id=1, source_target_pairs={{0,2},{1,10},{2,12},{3,4},{4,6},{5,14},{6,8},{7,0},{8,3},{9,11},{1... | collective-permute-start | bytes 1179656 | tf_op jit(solution)/shard_map/ppermute | solution.py:507
  286.5 49.8 %collective-permute-start.20 = (bf16[2,256,768]{2,1,0:T(8,128)(2,1)}, bf16[2,256,768]{2,1,0:T(8,128)(2,1)S(1)}, u32[]{:S(2)}, u32[]{:S(2)}) collective-permute-start(bf16[2,256,768]{2,1,0:T(8,128)(2,1)} %get-tuple-element.353), channel_id=1, source_target_pairs={{8,0},{0,1},{9,8},{1,9},{10,2},{2,3},{11,10},{3,11},{12,4},{4,5},{... | collective-permute-start | bytes 2359304 | tf_op jit(solution)/shard_map/ppermute | solution.py:515
  288.2 48.2 %collective-permute-start.19 = (bf16[2,256,768]{2,1,0:T(8,128)(2,1)}, bf16[2,256,768]{2,1,0:T(8,128)(2,1)S(1)}, u32[]{:S(2)}, u32[]{:S(2)}) collective-permute-start(bf16[2,256,768]{2,1,0:T(8,128)(2,1)} %get-tuple-element.352), channel_id=1, source_target_pairs={{0,0},{8,1},{1,8},{9,9},{2,2},{10,3},{3,10},{11,11},{4,4},{12,5},{... | collective-permute-start | bytes 2359304 | tf_op jit(solution)/shard_map/ppermute | solution.py:515
  324.1 18.4 %collective-permute-start.25 = (bf16[2,4,2,24,3072]{4,3,1,2,0:T(8,128)(2,1)}, bf16[2,4,2,24,3072]{4,3,1,2,0:T(8,128)(2,1)}, u32[]{:S(2)}, u32[]{:S(2)}) collective-permute-start(bf16[2,4,2,24,3072]{4,3,1,2,0:T(8,128)(2,1)} %bitcast.349), channel_id=1, source_target_pairs={{0,8},{8,0},{1,9},{9,1},{2,10},{10,2},{3,11},{11,3},{4,12},{12,4},... | collective-permute-start | bytes 7077896 | tf_op jit(solution)/shard_map/ppermute | solution.py:426
  327.7 19.3 %collective-permute-start.26 = (bf16[2,4,2,24,3072]{4,3,1,0,2:T(8,128)(2,1)}, bf16[2,4,2,24,3072]{4,3,1,0,2:T(8,128)(2,1)}, u32[]{:S(2)}, u32[]{:S(2)}) collective-permute-start(bf16[2,4,2,24,3072]{4,3,1,0,2:T(8,128)(2,1)} %bitcast.348), channel_id=1, source_target_pairs={{0,8},{8,0},{1,9},{9,1},{2,10},{10,2},{3,11},{11,3},{4,12},{12,4},... | collective-permute-start | bytes 7077896 | tf_op jit(solution)/shard_map/ppermute | solution.py:426
  337.7 53.5 %all-to-all-start = ((bf16[4,256,768]{2,1,0:T(8,128)(2,1)}), bf16[4,256,768]{2,1,0:T(8,128)(2,1)}, u32[]{:S(2)}, u32[]{:S(2)}) async-start(bf16[4,256,768]{2,1,0:T(8,128)(2,1)} %bitcast.417), calls=%async_computation | async-start | bytes 3145728 | tf_op jit(solution)/shard_map/all_to_all | solution.py:497
  352.6 38.6 %collective-permute-start.27 = (bf16[4,2,24,3072]{3,2,0,1:T(8,128)(2,1)}, bf16[4,2,24,3072]{3,2,0,1:T(8,128)(2,1)}, u32[]{:S(2)}, u32[]{:S(2)}) collective-permute-start(bf16[4,2,24,3072]{3,2,0,1:T(8,128)(2,1)} %dynamic-slice_bitcast_fusion.5), channel_id=1, source_target_pairs={{0,16},{16,0},{1,17},{17,1},{2,18},{18,2},{3,19},{19,3},{4,20},{20... | collective-permute-start | bytes 3538952 | tf_op jit(solution)/shard_map/ppermute | solution.py:395
  354.1 39.4 %collective-permute-start.28 = (bf16[2,4,24,3072]{3,2,1,0:T(8,128)(2,1)}, bf16[2,4,24,3072]{3,2,1,0:T(8,128)(2,1)}, u32[]{:S(2)}, u32[]{:S(2)}) collective-permute-start(bf16[2,4,24,3072]{3,2,1,0:T(8,128)(2,1)} %dynamic-slice_bitcast_fusion.4), channel_id=1, source_target_pairs={{0,1},{1,0},{2,3},{3,2},{4,5},{5,4},{6,7},{7,6},{8,9},{9,8},{10,11... | collective-permute-start | bytes 3538952 | tf_op jit(solution)/shard_map/ppermute | solution.py:395
  390.1 29.2 %collective-permute-start.29 = (bf16[2,1024,512]{2,1,0:T(8,128)(2,1)}, bf16[2,1024,512]{2,1,0:T(8,128)(2,1)}, u32[]{:S(2)}, u32[]{:S(2)}) collective-permute-start(bf16[2,1024,512]{2,1,0:T(8,128)(2,1)} %get-tuple-element.125), channel_id=1, source_target_pairs={{0,8},{8,0},{1,9},{9,1},{2,10},{10,2},{3,11},{11,3},{4,12},{12,4},... | collective-permute-start | bytes 6291464 | tf_op jit(solution)/shard_map/ppermute | solution.py:426
  395.5 22.8 %collective-permute-start.36 = (bf16[4,24,3072]{2,1,0:T(8,128)(2,1)S(1)}, bf16[4,24,3072]{2,1,0:T(8,128)(2,1)S(1)}, u32[]{:S(2)}, u32[]{:S(2)}) collective-permute-start(bf16[4,24,3072]{2,1,0:T(8,128)(2,1)S(1)} %dynamic-slice_bitcast_fusion.21), channel_id=1, source_target_pairs={{0,1},{1,0},{2,3},{3,2},{4,5},{5,4},{6,7},{7,6},{8,9},{9,8},{10,11... | collective-permute-start | bytes 1769480 | tf_op jit(solution)/shard_map/ppermute | solution.py:395
  396.8 22.5 %collective-permute-start.37 = (bf16[4,24,3072]{2,1,0:T(8,128)(2,1)S(1)}, bf16[4,24,3072]{2,1,0:T(8,128)(2,1)S(1)}, u32[]{:S(2)}, u32[]{:S(2)}) collective-permute-start(bf16[4,24,3072]{2,1,0:T(8,128)(2,1)S(1)} %dynamic-slice_bitcast_fusion.20), channel_id=1, source_target_pairs={{0,16},{16,0},{1,17},{17,1},{2,18},{18,2},{3,19},{19,3},{4,20},{20... | collective-permute-start | bytes 1769480 | tf_op jit(solution)/shard_map/ppermute | solution.py:395
  443.2 40.3 %collective-permute-start.38 = (bf16[24,6144]{1,0:T(8,128)(2,1)}, bf16[24,6144]{1,0:T(8,128)(2,1)}, u32[]{:S(2)}, u32[]{:S(2)}) collective-permute-start(bf16[24,6144]{1,0:T(8,128)(2,1)} %get-tuple-element.359), channel_id=1, source_target_pairs={{0,6},{2,0},{4,2},{6,4},{1,7},{3,1},{5,3},{7,5},{8,14},{10,8},{12,... | collective-permute-start | bytes 884744 | tf_op jit(solution)/shard_map/ppermute | solution.py:395
  446.8 37.7 %collective-permute-start.39 = (bf16[24,6144]{1,0:T(8,128)(2,1)}, bf16[24,6144]{1,0:T(8,128)(2,1)}, u32[]{:S(2)}, u32[]{:S(2)}) collective-permute-start(bf16[24,6144]{1,0:T(8,128)(2,1)} %get-tuple-element.360), channel_id=1, source_target_pairs={{0,4},{2,6},{4,0},{6,2},{1,5},{3,7},{5,1},{7,3},{8,12},{10,14},{12... | collective-permute-start | bytes 884744 | tf_op jit(solution)/shard_map/ppermute | solution.py:395
  446.8 39.2 %collective-permute-start.40 = (bf16[24,6144]{1,0:T(8,128)(2,1)}, bf16[24,6144]{1,0:T(8,128)(2,1)}, u32[]{:S(2)}, u32[]{:S(2)}) collective-permute-start(bf16[24,6144]{1,0:T(8,128)(2,1)} %get-tuple-element.358), channel_id=1, source_target_pairs={{0,2},{2,4},{4,6},{6,0},{1,3},{3,5},{5,7},{7,1},{8,10},{10,12},{12... | collective-permute-start | bytes 884744 | tf_op jit(solution)/shard_map/ppermute | solution.py:395
  451.1 29.6 %collective-permute-start.35 = (bf16[2,4,24,1664]{3,2,1,0:T(8,128)(2,1)}, bf16[2,4,24,1664]{3,2,1,0:T(8,128)(2,1)}, u32[]{:S(2)}, u32[]{:S(2)}) collective-permute-start(bf16[2,4,24,1664]{3,2,1,0:T(8,128)(2,1)} %dynamic-slice_bitcast_fusion.7), channel_id=1, source_target_pairs={{0,1},{1,0},{2,3},{3,2},{4,5},{5,4},{6,7},{7,6},{8,9},{9,8},{10,11... | collective-permute-start | bytes 1916936 | tf_op jit(solution)/shard_map/ppermute | solution.py:395
  453.1 24.6 %collective-permute-start.34 = (bf16[4,2,24,1536]{3,2,1,0:T(8,128)(2,1)}, bf16[4,2,24,1536]{3,2,1,0:T(8,128)(2,1)}, u32[]{:S(2)}, u32[]{:S(2)}) collective-permute-start(bf16[4,2,24,1536]{3,2,1,0:T(8,128)(2,1)} %dynamic-slice_bitcast_fusion.15), channel_id=1, source_target_pairs={{0,16},{16,0},{1,17},{17,1},{2,18},{18,2},{3,19},{19,3},{4,20},{20... | collective-permute-start | bytes 1769480 | tf_op jit(solution)/shard_map/ppermute | solution.py:395
  477.7 43.2 %collective-permute-start.42 = (bf16[2,4,24,3072]{3,2,1,0:T(8,128)(2,1)}, bf16[2,4,24,3072]{3,2,1,0:T(8,128)(2,1)}, u32[]{:S(2)}, u32[]{:S(2)}) collective-permute-start(bf16[2,4,24,3072]{3,2,1,0:T(8,128)(2,1)} %dynamic-slice_bitcast_fusion), channel_id=1, source_target_pairs={{0,1},{1,0},{2,3},{3,2},{4,5},{5,4},{6,7},{7,6},{8,9},{9,8},{10,11... | collective-permute-start | bytes 3538952 | tf_op jit(solution)/shard_map/ppermute | solution.py:395
  480.8 42.4 %collective-permute-start.33 = (bf16[4,2,24,3072]{3,2,1,0:T(8,128)(2,1)}, bf16[4,2,24,3072]{3,2,1,0:T(8,128)(2,1)}, u32[]{:S(2)}, u32[]{:S(2)}) collective-permute-start(bf16[4,2,24,3072]{3,2,1,0:T(8,128)(2,1)} %dynamic-slice_bitcast_fusion.1), channel_id=1, source_target_pairs={{0,16},{16,0},{1,17},{17,1},{2,18},{18,2},{3,19},{19,3},{4,20},{20... | collective-permute-start | bytes 3538952 | tf_op jit(solution)/shard_map/ppermute | solution.py:395
  483.5 28.2 %collective-permute-start.44 = (bf16[4,24,1536]{2,1,0:T(8,128)(2,1)}, bf16[4,24,1536]{2,1,0:T(8,128)(2,1)}, u32[]{:S(2)}, u32[]{:S(2)}) collective-permute-start(bf16[4,24,1536]{2,1,0:T(8,128)(2,1)} %dynamic-slice_bitcast_fusion.32), channel_id=1, source_target_pairs={{0,1},{1,0},{2,3},{3,2},{4,5},{5,4},{6,7},{7,6},{8,9},{9,8},{10,11... | collective-permute-start | bytes 884744 | tf_op jit(solution)/shard_map/ppermute | solution.py:395
  484.6 31.4 %collective-permute-start.45 = (bf16[4,24,1664]{2,1,0:T(8,128)(2,1)}, bf16[4,24,1664]{2,1,0:T(8,128)(2,1)}, u32[]{:S(2)}, u32[]{:S(2)}) collective-permute-start(bf16[4,24,1664]{2,1,0:T(8,128)(2,1)} %dynamic-slice_bitcast_fusion.30), channel_id=1, source_target_pairs={{0,16},{16,0},{1,17},{17,1},{2,18},{18,2},{3,19},{19,3},{4,20},{20... | collective-permute-start | bytes 958472 | tf_op jit(solution)/shard_map/ppermute | solution.py:395
  503.9 59.3 %collective-permute-start.46 = (bf16[256,768]{1,0:T(8,128)(2,1)S(1)}, bf16[256,768]{1,0:T(8,128)(2,1)S(1)}, u32[]{:S(2)}, u32[]{:S(2)}) collective-permute-start(bf16[256,768]{1,0:T(8,128)(2,1)S(1)} %get-tuple-element.347), channel_id=1, source_target_pairs={{0,0},{8,1},{10,2},{2,3},{4,4},{12,5},{14,6},{6,7},{1,8},{9,9},{11... | collective-permute-start | bytes 1179656 | tf_op jit(solution)/shard_map/ppermute | solution.py:527
  511.7 53.6 %collective-permute-start.47 = (bf16[256,768]{1,0:T(8,128)(2,1)S(1)}, bf16[256,768]{1,0:T(8,128)(2,1)S(1)}, u32[]{:S(2)}, u32[]{:S(2)}) collective-permute-start(bf16[256,768]{1,0:T(8,128)(2,1)S(1)} %get-tuple-element.346), channel_id=1, source_target_pairs={{2,0},{10,1},{12,2},{4,3},{6,4},{14,5},{8,6},{0,7},{3,8},{11,9},{1... | collective-permute-start | bytes 1179656 | tf_op jit(solution)/shard_map/ppermute | solution.py:527
  516.0 49.4 %collective-permute-start.48 = (bf16[256,768]{1,0:T(8,128)(2,1)S(1)}, bf16[256,768]{1,0:T(8,128)(2,1)S(1)}, u32[]{:S(2)}, u32[]{:S(2)}) collective-permute-start(bf16[256,768]{1,0:T(8,128)(2,1)S(1)} %get-tuple-element.345), channel_id=1, source_target_pairs={{4,0},{12,1},{14,2},{6,3},{0,4},{8,5},{10,6},{2,7},{5,8},{13,9},{1... | collective-permute-start | bytes 1179656 | tf_op jit(solution)/shard_map/ppermute | solution.py:527
  520.9 44.5 %collective-permute-start.49 = (bf16[256,768]{1,0:T(8,128)(2,1)S(1)}, bf16[256,768]{1,0:T(8,128)(2,1)S(1)}, u32[]{:S(2)}, u32[]{:S(2)}) collective-permute-start(bf16[256,768]{1,0:T(8,128)(2,1)S(1)} %get-tuple-element.344), channel_id=1, source_target_pairs={{6,0},{14,1},{8,2},{0,3},{2,4},{10,5},{12,6},{4,7},{7,8},{15,9},{9... | collective-permute-start | bytes 1179656 | tf_op jit(solution)/shard_map/ppermute | solution.py:527
  538.7 18.8 %collective-permute-start.41 = (bf16[4,24,3072]{2,1,0:T(8,128)(2,1)S(1)}, bf16[4,24,3072]{2,1,0:T(8,128)(2,1)S(1)}, u32[]{:S(2)}, u32[]{:S(2)}) collective-permute-start(bf16[4,24,3072]{2,1,0:T(8,128)(2,1)S(1)} %dynamic-slice_bitcast_fusion.14), channel_id=1, source_target_pairs={{0,1},{1,0},{2,3},{3,2},{4,5},{5,4},{6,7},{7,6},{8,9},{9,8},{10,11... | collective-permute-start | bytes 1769480 | tf_op jit(solution)/shard_map/ppermute | solution.py:395
  557.5 15.8 %collective-permute-start.51 = (bf16[4,2,24,1536]{3,2,1,0:T(8,128)(2,1)S(1)}, bf16[4,2,24,1536]{3,2,1,0:T(8,128)(2,1)S(1)}, u32[]{:S(2)}, u32[]{:S(2)}) collective-permute-start(bf16[4,2,24,1536]{3,2,1,0:T(8,128)(2,1)S(1)} %dynamic-slice_bitcast_fusion.10), channel_id=1, source_target_pairs={{0,16},{16,0},{1,17},{17,1},{2,18},{18,2},{3,19},{19,3},{4,20},{20... | collective-permute-start | bytes 1769480 | tf_op jit(solution)/shard_map/ppermute | solution.py:395
  563.2 25.1 %collective-permute-start.53 = (bf16[2,4,24,1664]{3,2,1,0:T(8,128)(2,1)}, bf16[2,4,24,1664]{3,2,1,0:T(8,128)(2,1)}, u32[]{:S(2)}, u32[]{:S(2)}) collective-permute-start(bf16[2,4,24,1664]{3,2,1,0:T(8,128)(2,1)} %dynamic-slice_bitcast_fusion.6), channel_id=1, source_target_pairs={{0,1},{1,0},{2,3},{3,2},{4,5},{5,4},{6,7},{7,6},{8,9},{9,8},{10,11... | collective-permute-start | bytes 1916936 | tf_op jit(solution)/shard_map/ppermute | solution.py:395
  565.3 34.5 %collective-permute-start.56 = (bf16[24,9344]{1,0:T(8,128)(2,1)}, bf16[24,9344]{1,0:T(8,128)(2,1)}, u32[]{:S(2)}, u32[]{:S(2)}) collective-permute-start(bf16[24,9344]{1,0:T(8,128)(2,1)} %get-tuple-element.341), channel_id=1, source_target_pairs={{0,2},{2,4},{4,6},{6,0},{1,3},{3,5},{5,7},{7,1},{8,10},{10,12},{12... | collective-permute-start | bytes 1345544 | tf_op jit(solution)/shard_map/ppermute | solution.py:395
  565.3 37.6 %collective-permute-start.55 = (bf16[24,9344]{1,0:T(8,128)(2,1)}, bf16[24,9344]{1,0:T(8,128)(2,1)}, u32[]{:S(2)}, u32[]{:S(2)}) collective-permute-start(bf16[24,9344]{1,0:T(8,128)(2,1)} %get-tuple-element.342), channel_id=1, source_target_pairs={{0,4},{2,6},{4,0},{6,2},{1,5},{3,7},{5,1},{7,3},{8,12},{10,14},{12... | collective-permute-start | bytes 1345544 | tf_op jit(solution)/shard_map/ppermute | solution.py:395
  565.4 37.5 %collective-permute-start.50 = (bf16[24,9344]{1,0:T(8,128)(2,1)}, bf16[24,9344]{1,0:T(8,128)(2,1)}, u32[]{:S(2)}, u32[]{:S(2)}) collective-permute-start(bf16[24,9344]{1,0:T(8,128)(2,1)} %get-tuple-element.343), channel_id=1, source_target_pairs={{0,6},{2,0},{4,2},{6,4},{1,7},{3,1},{5,3},{7,5},{8,14},{10,8},{12,... | collective-permute-start | bytes 1345544 | tf_op jit(solution)/shard_map/ppermute | solution.py:395
  574.2 16.6 %collective-permute-start.52 = (bf16[4,24,1536]{2,1,0:T(8,128)(2,1)}, bf16[4,24,1536]{2,1,0:T(8,128)(2,1)}, u32[]{:S(2)}, u32[]{:S(2)}) collective-permute-start(bf16[4,24,1536]{2,1,0:T(8,128)(2,1)} %dynamic-slice_bitcast_fusion.31), channel_id=1, source_target_pairs={{0,1},{1,0},{2,3},{3,2},{4,5},{5,4},{6,7},{7,6},{8,9},{9,8},{10,11... | collective-permute-start | bytes 884744 | tf_op jit(solution)/shard_map/ppermute | solution.py:395
  598.4 18.9 %collective-permute-start.58 = (bf16[24,3200]{1,0:T(8,128)(2,1)}, bf16[24,3200]{1,0:T(8,128)(2,1)}, u32[]{:S(2)}, u32[]{:S(2)}) collective-permute-start(bf16[24,3200]{1,0:T(8,128)(2,1)} %get-tuple-element.374), channel_id=1, source_target_pairs={{0,4},{2,6},{4,0},{6,2},{1,5},{3,7},{5,1},{7,3},{8,12},{10,14},{12... | collective-permute-start | bytes 460808 | tf_op jit(solution)/shard_map/ppermute | solution.py:395
  599.8 17.6 %collective-permute-start.57 = (bf16[24,3200]{1,0:T(8,128)(2,1)}, bf16[24,3200]{1,0:T(8,128)(2,1)}, u32[]{:S(2)}, u32[]{:S(2)}) collective-permute-start(bf16[24,3200]{1,0:T(8,128)(2,1)} %get-tuple-element.373), channel_id=1, source_target_pairs={{0,6},{2,0},{4,2},{6,4},{1,7},{3,1},{5,3},{7,5},{8,14},{10,8},{12,... | collective-permute-start | bytes 460808 | tf_op jit(solution)/shard_map/ppermute | solution.py:395
  (165 other events, 1541.0 us)
Sparse Core Ops, SparseCore 0:
  35.0 110.6 all-gather.2
  149.2 112.9 all-gather.4
